TPU v7x, 32 devices: a whole 2x2x4 slice. The times are simulated.
32 devices in a mesh: roll: 16 (over z, y, x), tp: 2 (over core).
Axes of the slice: x: 2, y: 2, z: 4, core: 2. Of those that a mesh axis runs over, the one named last changes fastest.
Arguments:
- hidden_rows: bfloat16 [12288, 7168], P('roll', 'tp'), may hold values from -100 to 100
- target_latents: bfloat16 [12288, 576], P('roll'), may hold values from -6 to 6
- group_lengths: int32 [16, 8], P('roll'), may hold values from 1 to 288, 768 in all within a row
- dest_ids: int32 [12288, 1], P('roll'), may hold values from 0 to 15; in each aligned block of 768 rows (0 to 767, 768 to 1535, ...) at most 72 rows name the same one
- input_gain: float32 [7168], P('tp'), may hold values from 0.1 to 1.9
- latent_gain: float32 [512], replicated, may hold values from 0.1 to 1.9
- kv_weight: bfloat16 [7168, 576], P('tp'), may hold values from -0.0625 to 0.0625
Outputs:
- trainer_loss: float32 [16], P('roll')
- weight_codes: bfloat16 [7168, 576], P('tp')
Inputs may be any that keep to these rules, and one draw needn't show every extreme that they name: `dest_ids`: at most 72 of the rows of one index of roll name the same trainer, and exactly 72 in some index. `group_lengths`: each index's 8 lengths sum to 768; the longest is exactly 288.
All inputs are finite; a program needn't handle non-finite values. Where the computation divides by a largest or mean magnitude, that divisor is 1e-20 or more.
Results may differ from a plain program's by a relative error of at most 0.0085.
Values may be sent and summed in bfloat16 or wider, within the bound.
No kernel may reach another device: no remote copies, remote signals or barrier semaphores. Data moves between devices by JAX's collectives and lax.ppermute only.
A program may use at most 128 MiB of HBM per device.

v0:
```python
import jax
import jax.numpy as jnp
from jax import lax
from jax.sharding import PartitionSpec as P

EPS = 1e-06
RATE = 0.5


def row_weights(lengths, row_count):
    bounds = jnp.cumsum(lengths)
    position = lax.iota(jnp.int32, row_count)
    group_index = jnp.sum((position[:, None] >= bounds[None, :]).astype(jnp.int32), axis=1)
    member = group_index[:, None] == lax.iota(jnp.int32, lengths.shape[0])[None, :]
    length = jnp.sum(jnp.where(member, lengths[None, :], 0), axis=1)
    return (1.0 / length.astype(jnp.float32)).astype(jnp.bfloat16)


def head_terms(latent, targets, weights, gain_vec, groups):
    latent_width = gain_vec.shape[0]
    compressed = latent[:, :latent_width]
    rotary = latent[:, latent_width:]
    factor = lax.rsqrt(jnp.mean(compressed * compressed, axis=1) + EPS)
    predicted = compressed * factor[:, None] * gain_vec
    weight_f = weights.astype(jnp.float32)
    residue = jnp.concatenate([predicted, rotary], axis=1) - targets.astype(jnp.float32)
    row_terms = weight_f * (0.5 * jnp.mean(residue * residue, axis=1)) / groups
    d_pred = weight_f[:, None] * residue
    d_scaled = d_pred[:, :latent_width] * gain_vec
    inner_sum = jnp.mean(d_scaled * compressed, axis=1)
    d_compressed = (
        factor[:, None] * d_scaled - compressed * (factor * factor * factor * inner_sum)[:, None]
    )
    return (row_terms, jnp.concatenate([d_compressed, d_pred[:, latent_width:]], axis=1))


def forward_backward(
    rows_x, rows_t, rows_w, input_gain, latent_gain, kv_weight, model_width, groups
):
    wide = rows_x.astype(jnp.float32)
    squares = jnp.sum(wide * wide, axis=1)
    total_sq = lax.psum(squares, "tp")
    scale = lax.rsqrt(total_sq / model_width + EPS)
    normed = (wide * scale[:, None] * input_gain).astype(jnp.bfloat16)
    partial_latent = jnp.dot(normed, kv_weight, preferred_element_type=jnp.float32)
    latent = lax.psum(partial_latent, "tp")
    row_terms, d_latent = head_terms(latent, rows_t, rows_w, latent_gain, groups)
    d_rounded = d_latent.astype(jnp.bfloat16)
    grad_part = lax.dot_general(
        normed, d_rounded, (((0,), (0,)), ((), ())), preferred_element_type=jnp.float32
    )
    return (row_terms, grad_part)


def shards(
    hidden_rows, target_latents, group_lengths, dest_ids, input_gain, latent_gain, kv_weight
):
    source_rows = hidden_rows.shape[0]
    feature_cols = hidden_rows.shape[1]
    roll_count = lax.axis_size("roll")
    tp_count = lax.axis_size("tp")
    model_width = feature_cols * tp_count
    groups = group_lengths.shape[1]
    weights_row = row_weights(group_lengths[0], source_rows)
    capacity = 3 * source_rows // (2 * roll_count)
    slot_total = roll_count * capacity
    destination = dest_ids[:, 0]
    member = destination[:, None] == lax.iota(jnp.int32, roll_count)[None, :]
    running = jnp.cumsum(member.astype(jnp.int32), axis=0)
    slot_index = jnp.sum(jnp.where(member, running, 0), axis=1) - 1
    position = destination * capacity + slot_index
    row_terms, grad_part = forward_backward(
        hidden_rows,
        target_latents,
        weights_row,
        input_gain,
        latent_gain,
        kv_weight,
        model_width,
        groups,
    )
    sent_terms = jnp.zeros((slot_total,), jnp.float32).at[position].set(row_terms)
    got_terms = lax.all_to_all(
        sent_terms.reshape(roll_count, capacity), "roll", split_axis=0, concat_axis=0, tiled=True
    )
    loss_local = jnp.sum(got_terms)
    entry_count = model_width * kv_weight.shape[1]
    grad = lax.psum(grad_part, "roll")
    power = lax.psum(jnp.sum(grad * grad), "tp")
    updated = kv_weight.astype(jnp.float32) - RATE * grad * lax.rsqrt(power / entry_count + EPS)
    peak = lax.pmax(jnp.max(jnp.abs(updated), axis=0), "tp") + EPS
    weight_codes = (updated / peak[None, :]).astype(jnp.bfloat16)
    return (loss_local.reshape(1), weight_codes)


def solution(mesh):
    in_specs = (
        P("roll", "tp"),
        P("roll", None),
        P("roll", None),
        P("roll", None),
        P("tp"),
        P(),
        P("tp", None),
    )
    out_specs = (P("roll"), P("tp", None))
    return jax.shard_map(shards, mesh=mesh, in_specs=in_specs, out_specs=out_specs, check_vma=False)
```

profile of v0, /device:TPU:0, one launch (start us, length us, event | category | flops | bytes accessed | tf_op | source)
XLA Modules:
  0.0 344.2 jit_solution(3830620076535215943)
XLA Ops:
  7.2 0.0 copy-start.5
  7.2 0.0 all-reduce.3.cloned.1.call-start
  7.2 3.7 %fusion = f32[768]{0:T(1024)S(1)} fusion(bf16[768,3584]{1,0:T(8,128)(2,1)} %param.7), kind=kLoop, calls=%fused_computation.3 | loop fusion | flops 8256768 | bytes 5508096 | tf_op jit(solution)/shard_map/reduce_sum | solution.py:41
  10.9 2.6 psum.28
  13.5 0.0 copy-done.5
  13.5 0.0 copy-start.4
  13.5 0.0 copy-start.2
  13.5 8.5 %fusion.5 = f32[768,576]{0,1:T(8,128)} fusion(bf16[3584,576]{0,1:T(8,128)(2,1)} %param.13, bf16[768,3584]{1,0:T(8,128)(2,1)} %param.7, f32[3584]{0:T(1024)S(1)} %copy-done.5, f32[768]{0:T(1024)S(1)} %add_rsqrt_fusion.1), kind=kOutput, calls=%fused_computation.13 | convolution fusion | flops 3181903872 | bytes 11420672 | tf_op jit(solution)/shard_map/dot_general | solution.py:45
  22.1 0.0 copy-start.1
  22.1 0.0 all-reduce.3.cloned.1.call-update
  22.1 0.0 all-reduce.5.cloned.1.call-start
  22.1 0.0 copy-done.4
  22.1 0.2 reduce-window.20
  22.3 0.1 convert_reduce_fusion
  22.4 0.1 select_reduce_fusion
  22.5 23.0 %all-reduce.3.cloned.1.call-done = f32[768,576]{0,1:T(8,128)} async-done(((f32[768,576]{0,1:T(8,128)}), f32[768,576]{0,1:T(8,128)}) %all-reduce.3.cloned.1.call-update) | async-done | bytes 1769488 | tf_op jit(solution)/shard_map/psum | solution.py:46
  45.5 0.0 slice-start
  45.5 1.6 multiply_reduce_fusion.3
  47.1 0.0 copy-start
  47.1 0.0 copy-done.2
  47.1 0.0 slice-start.1
  47.1 1.7 multiply_multiply_fusion
  48.9 0.0 copy-done.1
  48.9 0.0 slice-done
  48.9 0.0 slice-start.2
  48.9 0.4 fusion.7
  49.3 0.0 copy-done
  49.3 0.2 multiply_reduce_fusion.2
  49.6 0.3 subtract_convert_fusion
  49.9 0.4 slice-done.1
  50.3 0.6 slice-done.2
  50.9 6.0 %fusion.3 = f32[3584,576]{0,1:T(8,128)} fusion(bf16[768,3584]{1,0:T(8,128)(2,1)S(1)} %bitcast.25, f32[3584]{0:T(1024)S(1)} %copy-done.5, f32[768]{0:T(1024)S(1)} %add_rsqrt_fusion.1, bf16[768,64]{0,1:T(8,128)(2,1)S(1)} %slice.41, bf16[768,512]{0,1:T(8,128)(2,1)S(1)} %subtract_convert_fusion), kind=kOutput, calls=%fused_computation.12 | convolution fusion | flops 3183673344 | bytes 14664704 | tf_op jit(solution)/shard_map/dot_general | solution.py:49
  56.9 0.0 copy-start.3
  56.9 0.0 all-reduce.5.cloned.1.call-update
  56.9 0.7 copy-done.3
  57.6 1.7 reduce-window.18
  59.3 0.3 slice_reduce_fusion
  59.6 0.1 fusion.12
  59.7 3.4 scatter_custom_fusion
  63.1 0.7 all_to_all.6
  63.8 6.8 %all-to-all-start = ((f32[16,1,72]{2,1,0:T(1,128)}), f32[16,1,72]{2,1,0:T(1,128)S(1)}, u32[]{:S(2)}, u32[]{:S(2)}) async-start(f32[16,1,72]{2,1,0:T(1,128)} %all_to_all.6), calls=%async_computation | async-start | bytes 16384 | tf_op jit(solution)/shard_map/all_to_all | solution.py:83
  70.6 241.2 %all-reduce.5.cloned.1.call-done = f32[3584,576]{0,1:T(8,128)} async-done(((f32[3584,576]{0,1:T(8,128)}), f32[3584,576]{0,1:T(8,128)}) %all-reduce.5.cloned.1.call-update) | async-done | bytes 8257552 | tf_op jit(solution)/shard_map/psum | solution.py:88
  311.8 6.1 %multiply_reduce_fusion = f32[]{:T(128)} fusion(f32[3584,576]{0,1:T(8,128)} %all-reduce.5.cloned.1.call-done), kind=kLoop, calls=%fused_computation.9 | loop fusion | flops 4128767 | bytes 8257540 | tf_op jit(solution)/shard_map/reduce_sum | solution.py:89
  317.9 0.0 all-to-all-done
  317.9 0.6 reduce_sum.87
  318.5 3.1 psum.31
  322.3 5.9 %abs_reduce_fusion = f32[576]{0:T(1024)S(1)} fusion(f32[3584,576]{0,1:T(8,128)} %all-reduce.5.cloned.1.call-done, bf16[3584,576]{0,1:T(8,128)(2,1)} %param.13, f32[]{:T(128)S(6)} %mul.149), kind=kLoop, calls=%fused_computation.7 | loop fusion | flops 10321344 | bytes 12388612 | tf_op jit(solution)/shard_map/reduce_max | solution.py:91
  328.2 2.5 pmax.7
  330.7 6.7 %divide_convert_fusion = bf16[3584,576]{0,1:T(8,128)(2,1)} fusion(f32[3584,576]{0,1:T(8,128)} %all-reduce.5.cloned.1.call-done, bf16[3584,576]{0,1:T(8,128)(2,1)} %param.13, f32[576]{0:T(1024)S(1)} %broadcast_add_fusion, f32[]{:T(128)S(6)} %mul.149), kind=kLoop, calls=%fused_computation.6 | loop fusion | flops 10321920 | bytes 16517380 | tf_op jit(solution)/shard_map/convert_element_type | solution.py:92
  (13 shorter events, 0.1 us)
Async XLA Ops:
  7.2 6.4 %copy-start.5 = (f32[3584]{0:T(1024)S(1)}, f32[3584]{0:T(1024)}, u32[]{:S(2)}) copy-start(f32[3584]{0:T(1024)} %param.11) | copy-start | bytes 43012
  7.2 38.3 %all-reduce.3.cloned.1.call-start = ((), (), s32[]{:S(2)}) async-start(), calls=%async_computation.1 | async-start | bytes 3538944 | tf_op jit(solution)/shard_map/psum | solution.py:46
  13.5 8.6 %copy-start.4 = (s32[1,8]{1,0:T(1,128)S(1)}, s32[1,8]{1,0:T(1,128)}, u32[]{:S(2)}) copy-start(s32[1,8]{1,0:T(1,128)} %param.9) | copy-start | bytes 100
  13.5 33.6 %copy-start.2 = (f32[512]{0:T(512)S(1)}, f32[512]{0:T(512)}, u32[]{:S(2)}) copy-start(f32[512]{0:T(512)} %param.12) | copy-start | bytes 6148
  22.1 26.8 %copy-start.1 = (bf16[768,576]{0,1:T(8,128)(2,1)S(1)}, bf16[768,576]{0,1:T(8,128)(2,1)}, u32[]{:S(2)}) copy-start(bf16[768,576]{0,1:T(8,128)(2,1)} %param.8) | copy-start | bytes 2654212
  22.1 289.8 %all-reduce.5.cloned.1.call-start = ((), (), s32[]{:S(2)}) async-start(), calls=%async_computation.2 | async-start | bytes 16515072 | tf_op jit(solution)/shard_map/psum | solution.py:88
  45.5 3.4 slice-start
  47.1 2.2 copy-start
  47.1 3.2 slice-start.1
  48.9 2.0 slice-start.2
  56.9 0.7 copy-start.3
  63.8 254.1 %all-to-all-start = ((f32[16,1,72]{2,1,0:T(1,128)}), f32[16,1,72]{2,1,0:T(1,128)S(1)}, u32[]{:S(2)}, u32[]{:S(2)}) async-start(f32[16,1,72]{2,1,0:T(1,128)} %all_to_all.6), calls=%async_computation | async-start | bytes 16384 | tf_op jit(solution)/shard_map/all_to_all | solution.py:83
Sparse Core Ops, SparseCore 0:
  22.2 23.2 all-reduce.2
  57.0 254.7 all-reduce.4
where the time goes:
time: 345 us; the launch traced here: 344 us
  waiting for transfers between devices  264 us (77%)
  other arithmetic  29.5 us (9%)
  between operations  14.9 us (4%)
  matrix products  14.5 us (4%)
  blocking collectives  8.14 us (2%)
  starting transfers between devices  6.87 us (2%)
  local copies, waits for them, and re-layouts  6.04 us (2%)
    psum x1, waiting for transfers between devices, shards(): grad = lax.psum(grad_part, 'roll')  241 us
    psum x1, waiting for transfers between devices, forward_backward(): latent = lax.psum(partial_latent, 'tp')  23 us
    dot_general x1, matrix products, forward_backward(): jnp.dot(normed, kv_weight, preferred_element_type=jnp.float32)  8.51 us
  transfers between devices with their start and end apart: 3, of which 2 were waited for; matrix products, arithmetic and copies ran while one was open for 3% of the time, Pallas kernels for 0%

commit v1 on v0

v1 whole, which is shorter than its diff:
```python
import jax
import jax.numpy as jnp
from jax import lax
from jax.experimental import pallas as pl
from jax.experimental.pallas import tpu as pltpu
from jax.sharding import PartitionSpec as P

EPS = 1e-06
RATE = 0.5
F32 = jnp.float32
BF16 = jnp.bfloat16

STEPS = {"xy": (1, 2), "yx": (2, 1), "z_lo": (4, 4), "z_hi": (8, 8)}
ROW_ORDER = ("xy", "yx", "z_lo", "z_hi")
COL_ORDER = ("z_lo", "xy", "yx", "z_hi")


def row_weights(lengths, row_count):
    bounds = jnp.cumsum(lengths)
    position = lax.iota(jnp.int32, row_count)
    group_index = jnp.sum((position[None, :] >= bounds[:, None]).astype(jnp.int32), axis=0)
    member = group_index[None, :] == lax.iota(jnp.int32, lengths.shape[0])[:, None]
    length = jnp.sum(jnp.where(member, lengths[:, None], 0), axis=0)
    return (1.0 / length.astype(F32)).astype(BF16)


def exchange(value, step):
    pairs = []
    for roll in range(16):
        for core in range(2):
            pairs.append((2 * roll + core, 2 * (roll ^ STEPS[step][core]) + core))
    return lax.ppermute(value, ("roll", "tp"), pairs)


def swap_cores(value):
    return lax.ppermute(value, "tp", [(0, 1), (1, 0)])


def add(a, b):
    return (a.astype(F32) + b.astype(F32)).astype(a.dtype)


def scatter_step(value, step):
    half = value.shape[0] // 2
    got = exchange(value[half:], step)
    return add(value[:half], got)


def gather_step(value, step):
    return jnp.concatenate([value, exchange(value, step)], axis=0)


def head(latent, targets, weights, gain_vec, groups):
    width = gain_vec.shape[0]
    compressed = latent[:width]
    factor = lax.rsqrt(jnp.mean(compressed * compressed, axis=0) + EPS)
    gain_col = gain_vec[:, None]
    weight_f = weights.astype(F32)
    targets = targets.astype(F32)
    res_c = compressed * factor[None, :] * gain_col - targets[:width]
    res_r = latent[width:] - targets[width:]
    total = jnp.sum(res_c * res_c, axis=0) + jnp.sum(res_r * res_r, axis=0)
    row_terms = weight_f * (0.5 * total / latent.shape[0]) / groups
    scaled = weight_f[None, :] * res_c * gain_col
    inner = jnp.mean(scaled * compressed, axis=0)
    d_c = factor[None, :] * scaled - compressed * (factor * factor * factor * inner)[None, :]
    return row_terms, jnp.concatenate([d_c, weight_f[None, :] * res_r], axis=0)


def update_of(w, g, gain, coef):
    return w.astype(F32) - coef * gain * g.astype(F32)


def peak_kernel(where_ref, coef_ref, g_ref, w_ref, gain_ref, out_ref):
    rows, cols = w_ref.shape[-2:]
    upd = jnp.abs(update_of(w_ref[...].reshape(rows, cols), g_ref[...].reshape(rows, cols), gain_ref[...], coef_ref[0]))
    top = jnp.max(upd, axis=1, keepdims=True)
    out_ref[...] = jnp.broadcast_to(top, (rows, 128)).reshape(out_ref.shape)


def code_kernel(where_ref, coef_ref, g_ref, w_ref, gain_ref, peak_ref, *rest):
    out_ref = rest[-1]
    rows, cols = w_ref.shape[-2:]
    upd = update_of(w_ref[...].reshape(rows, cols), g_ref[...].reshape(rows, cols), gain_ref[...], coef_ref[0])
    inv = 1.0 / peak_ref[...].reshape(rows, 128)[:, :1]
    out_ref[...] = (upd * inv).astype(BF16).reshape(out_ref.shape)


def finish(g_rows, g_cols, w3, gain_row, coef, where):
    blk, feat = w3.shape[1:]
    half = feat // 2
    nr = g_rows.shape[0]
    nc = g_cols.shape[1]
    scal = coef.reshape(1)
    smem = pl.BlockSpec(memory_space=pltpu.SMEM)

    def specs_rows(kern, extra, out_w, outs, alias):
        return pl.pallas_call(
            kern,
            grid_spec=pltpu.PrefetchScalarGridSpec(
                num_scalar_prefetch=1,
                grid=(nr,),
                in_specs=[
                    smem,
                    pl.BlockSpec((1, blk, feat), lambda j, wh: (j ^ wh[0], 0, 0)),
                    pl.BlockSpec((1, blk, feat), lambda j, wh: (j, 0, 0)),
                    pl.BlockSpec((1, feat), lambda j, wh: (0, 0)),
                ]
                + extra,
                out_specs=pl.BlockSpec((1, blk, out_w), lambda j, wh: (j, 0, 0)),
            ),
            out_shape=outs,
            input_output_aliases=alias,
        )

    def specs_cols(kern, extra, out_spec, outs, alias):
        return pl.pallas_call(
            kern,
            grid_spec=pltpu.PrefetchScalarGridSpec(
                num_scalar_prefetch=1,
                grid=(nc, 2),
                in_specs=[
                    smem,
                    pl.BlockSpec((1, 1, blk, half), lambda j, c, wh: (c ^ wh[1], j ^ wh[2], 0, 0)),
                    pl.BlockSpec((1, blk, half), lambda j, c, wh: (nr + j, 0, c)),
                    pl.BlockSpec((1, half), lambda j, c, wh: (0, c)),
                ]
                + extra,
                out_specs=out_spec,
            ),
            out_shape=outs,
            input_output_aliases=alias,
        )

    top_r = specs_rows(peak_kernel, [], 128, jax.ShapeDtypeStruct((nr, blk, 128), F32), {})(
        where, scal, g_rows, w3, gain_row
    )
    top_c = specs_cols(
        peak_kernel,
        [],
        pl.BlockSpec((1, 1, blk, 128), lambda j, c, wh: (c, j, 0, 0)),
        jax.ShapeDtypeStruct((2, nc, blk, 128), F32),
        {},
    )(where, scal, g_cols, w3, gain_row)
    top = jnp.concatenate([top_r, jnp.maximum(top_c[0], top_c[1])], axis=0)
    peak = jnp.maximum(top, swap_cores(top)) + EPS
    shape = jax.ShapeDtypeStruct(w3.shape, BF16)
    part = specs_rows(
        code_kernel, [pl.BlockSpec((1, blk, 128), lambda j, wh: (j, 0, 0))], feat, shape, {}
    )(where, scal, g_rows, w3, gain_row, peak)
    return specs_cols(
        code_kernel,
        [
            pl.BlockSpec((1, blk, 128), lambda j, c, wh: (nr + j, 0, 0)),
            pl.BlockSpec(memory_space=pl.ANY),
        ],
        pl.BlockSpec((1, blk, half), lambda j, c, wh: (nr + j, 0, c)),
        shape,
        {6: 0},
    )(where, scal, g_cols, w3, gain_row, peak, part)


def paired_shards(hidden, targets, group_lengths, dest_ids, input_gain, latent_gain, kv_weight):
    rows, feat = hidden.shape
    width = kv_weight.shape[1]
    model_width = 2 * feat
    groups = group_lengths.shape[1]
    roll = lax.axis_index("roll")
    core = lax.axis_index("tp")
    x_bit, y_bit, lo_bit, hi_bit = roll & 1, (roll >> 1) & 1, (roll >> 2) & 1, (roll >> 3) & 1
    first = jnp.where(core == 0, x_bit, y_bit)
    second = jnp.where(core == 0, y_bit, x_bit)
    row_mask = first * 8 + second * 4 + lo_bit * 2 + hi_bit
    col_mask = first * 4 + second * 2 + hi_bit
    where = jnp.stack([row_mask, lo_bit, col_mask]).astype(jnp.int32)

    w_t = kv_weight.T
    gained = (w_t.astype(F32) * input_gain[None, :]).astype(BF16)
    part = lax.dot_general(gained, hidden, (((1,), (1,)), ((), ())), preferred_element_type=F32)
    wide = hidden.astype(F32)
    squares = jnp.sum(wide * wide, axis=1)
    other = swap_cores(part.astype(BF16))
    squares = squares + swap_cores(squares)
    scale = lax.rsqrt(squares / model_width + EPS)
    latent = (part + other.astype(F32)) * scale[None, :]
    row_terms, d_latent = head(latent, targets.T, row_weights(group_lengths[0], rows), latent_gain, groups)
    d_scaled = (d_latent * scale[None, :]).astype(BF16)
    dest = dest_ids[:, 0]
    losses = jnp.sum(jnp.where(dest[None, :] == lax.iota(jnp.int32, 16)[:, None], row_terms[None, :], 0.0), axis=1)

    blk = width // 24
    d3 = d_scaled.reshape(24, blk, rows)
    d_rows = jnp.take(d3[:16], lax.iota(jnp.int32, 16) ^ row_mask, axis=0)
    d_cols = jnp.take(d3[16:], lax.iota(jnp.int32, 8) ^ col_mask, axis=0)
    half = feat // 2
    g_rows = jnp.dot(d_rows.reshape(16 * blk, rows), hidden, preferred_element_type=F32)
    g_rows = g_rows.astype(BF16).reshape(16, blk, feat)
    g_cols = jnp.dot(d_cols.reshape(8 * blk, rows), hidden, preferred_element_type=F32).astype(BF16)
    g_cols = g_cols.reshape(8, blk, feat)
    left, right = g_cols[:, :, :half], g_cols[:, :, half:]
    swap = lo_bit == 1
    g_cols = jnp.stack([jnp.where(swap, right, left), jnp.where(swap, left, right)])

    for step_r, step_c in zip(ROW_ORDER, COL_ORDER):
        g_rows = scatter_step(g_rows, step_r)
        if g_cols.ndim == 4:
            g_cols = scatter_step(g_cols, step_c)[0]
        else:
            g_cols = scatter_step(g_cols, step_c)

    gain_half = lax.dynamic_slice(input_gain, (lo_bit * half,), (half,))
    own_r = g_rows.astype(F32) * input_gain
    own_c = g_cols.astype(F32) * gain_half
    power = jnp.sum(own_r * own_r) + jnp.sum(own_c * own_c)
    small = jnp.concatenate([0.5 * losses, power[None], jnp.zeros((111,), F32)]).reshape(1, 128)
    for step in ROW_ORDER:
        small = small + exchange(small, step)
    small = small + swap_cores(small)

    for step_r, step_c in zip(reversed(ROW_ORDER), reversed(COL_ORDER)):
        g_rows = gather_step(g_rows, step_r)
        if step_c == "z_lo":
            g_cols = g_cols[None]
        g_cols = gather_step(g_cols, step_c)

    coef = RATE * lax.rsqrt(small[0, 16] / (model_width * width) + EPS)
    codes = finish(g_rows, g_cols, w_t.reshape(24, blk, feat), input_gain[None, :], coef, where)
    loss = lax.dynamic_slice(small, (0, roll), (1, 1))
    return loss.reshape(1), codes.reshape(width, feat).T


def any_shards(hidden, targets, group_lengths, dest_ids, input_gain, latent_gain, kv_weight):
    rows, feat = hidden.shape
    width = kv_weight.shape[1]
    roll_count = lax.axis_size("roll")
    model_width = feat * lax.axis_size("tp")
    wide = hidden.astype(F32)
    scale = lax.rsqrt(lax.psum(jnp.sum(wide * wide, axis=1), "tp") / model_width + EPS)
    normed = (wide * scale[:, None] * input_gain).astype(BF16)
    latent = lax.psum(jnp.dot(normed, kv_weight, preferred_element_type=F32), "tp")
    weights = row_weights(group_lengths[0], rows)
    row_terms, d_latent = head(latent.T, targets.T, weights, latent_gain, group_lengths.shape[1])
    grad = lax.dot_general(
        d_latent.astype(BF16), normed, (((1,), (0,)), ((), ())), preferred_element_type=F32
    )
    grad = lax.psum(grad.astype(BF16), "roll").astype(F32)
    dest = dest_ids[:, 0]
    named = dest[None, :] == lax.iota(jnp.int32, roll_count)[:, None]
    losses = lax.psum(jnp.sum(jnp.where(named, row_terms[None, :], 0.0), axis=1), "roll")
    power = lax.psum(jnp.sum(grad * grad), "tp")
    updated = kv_weight.T.astype(F32) - RATE * grad * lax.rsqrt(power / (model_width * width) + EPS)
    peak = lax.pmax(jnp.max(jnp.abs(updated), axis=1), "tp") + EPS
    codes = (updated / peak[:, None]).astype(BF16)
    loss = lax.dynamic_slice(losses, (lax.axis_index("roll"),), (1,))
    return loss, codes.T


def solution(mesh):
    in_specs = (
        P("roll", "tp"),
        P("roll", None),
        P("roll", None),
        P("roll", None),
        P("tp"),
        P(),
        P("tp", None),
    )
    out_specs = (P("roll"), P("tp", None))
    paired = mesh.shape["roll"] == 16 and mesh.shape["tp"] == 2
    body = paired_shards if paired else any_shards
    return jax.shard_map(body, mesh=mesh, in_specs=in_specs, out_specs=out_specs, check_vma=False)
```

time: 345 us -> 211 us (0.61)
  waiting for transfers between devices: 264 us -> 71.4 us
  Pallas kernels: 0 us -> 44.1 us
  starting transfers between devices: 6.87 us -> 33.7 us
  between operations: 14.9 us -> 3.01 us
  blocking collectives: 8.14 us -> 0 us
  local copies, waits for them, and re-layouts: 6.04 us -> 12.5 us
    psum x2 -> x0, waiting for transfers between devices: 264 us -> none  [the longest x1 241 us: shards(): grad = lax.psum(grad_part, 'roll')]
    ppermute x0 -> x24, waiting for transfers between devices: none -> 71.4 us  [the longest x20 69.9 us: exchange(): return lax.ppermute(value, ('roll', 'tp'), pairs)]
    pallas_call x0 -> x4, Pallas kernels: none -> 44.1 us  [the longest x1 11.5 us: finish(): specs_rows(code_kernel, [pl.BlockSpec((1, blk, 128), lambda j, wh: (j, 0,...]
    ppermute x0 -> x24, starting transfers between devices: none -> 33.7 us  [the longest x20 33.1 us: exchange(): return lax.ppermute(value, ('roll', 'tp'), pairs)]
    all_to_all x1 -> x0, starting transfers between devices: 6.79 us -> none  [shards(): lax.all_to_all(sent_terms.reshape(roll_count, capacity), 'roll', split_ax...]
    concatenate x0 -> x7, other arithmetic: none -> 6.48 us  [the longest x6 5.54 us: gather_step(): return jnp.concatenate([value, exchange(value, step)], axis=0)]
    reduce_max x1 -> x0, other arithmetic: 5.91 us -> none  [shards(): peak = lax.pmax(jnp.max(jnp.abs(updated), axis=0), 'tp') + EPS]
    psum x2 -> x0, blocking collectives: 5.67 us -> none  [the longest x1 3.08 us: shards(): power = lax.psum(jnp.sum(grad * grad), 'tp')]
  transfers between devices with their start and end apart: 3 -> 24, of which waited for: 2 -> 12; matrix products, arithmetic and copies ran while one was open for 3% -> 19% of each run, Pallas kernels for 0% -> 5%
where the time goes in v1:
time: 211 us; the launch traced here: 209 us
  waiting for transfers between devices  71.4 us (34%)
  Pallas kernels  44.1 us (21%)
  starting transfers between devices  33.7 us (16%)
  other arithmetic  28.7 us (14%)
  matrix products  15.6 us (7%)
  local copies, waits for them, and re-layouts  12.5 us (6%)
  between operations  3.01 us (1%)
    ppermute x20, waiting for transfers between devices, exchange(): return lax.ppermute(value, ('roll', 'tp'), pairs)  69.9 us
    ppermute x20, starting transfers between devices, exchange(): return lax.ppermute(value, ('roll', 'tp'), pairs)  33.1 us
    pallas_call x1, Pallas kernels, finish(): specs_rows(code_kernel, [pl.BlockSpec((1, blk, 128), lambda j, wh: (j, 0,...  11.5 us
    pallas_call x1, Pallas kernels, finish(): specs_rows(peak_kernel, [], 128, jax.ShapeDtypeStruct((nr, blk, 128), F32...  11.3 us
    pallas_call x1, Pallas kernels, finish(): specs_cols(code_kernel, [pl.BlockSpec((1, blk, 128), lambda j, c, wh: (nr...  10.7 us
    pallas_call x1, Pallas kernels, finish(): specs_cols(peak_kernel, [], pl.BlockSpec((1, 1, blk, 128), lambda j, c, w...  10.6 us
    dot_general x1, matrix products, paired_shards(): lax.dot_general(gained, hidden, (((1,), (1,)), ((), ())), preferred_eleme...  6.93 us
    concatenate x6, other arithmetic, gather_step(): return jnp.concatenate([value, exchange(value, step)], axis=0)  5.54 us
  transfers between devices with their start and end apart: 24, of which 12 were waited for; matrix products, arithmetic and copies ran while one was open for 19% of the time, Pallas kernels for 5%

profile of v1, /device:TPU:0, one launch (start us, length us, event | category | flops | bytes accessed | tf_op | source)
XLA Modules:
  0.0 209.1 jit_solution(15754501747369768896)
XLA Ops:
  0.7 4.4 %multiply_reduce_fusion = f32[768]{0:T(1024)} fusion(bf16[768,3584]{1,0:T(8,128)(2,1)} %param.7), kind=kLoop, calls=%fused_computation.2 | loop fusion | flops 8256768 | bytes 5508096 | tf_op jit(solution)/shard_map/reduce_sum | solution.py:181
  5.6 6.9 %fusion.14 = (bf16[576,768]{1,0:T(8,128)(2,1)}, f32[576,768]{1,0:T(8,128)S(1)}) fusion(bf16[768,3584]{1,0:T(8,128)(2,1)} %param.7, bf16[3584,576]{0,1:T(8,128)(2,1)S(1)} %copy-done, f32[3584]{0:T(1024)S(1)} %copy-done.5), kind=kOutput, calls=%fused_computation.85 | convolution fusion | flops 3177529344 | bytes 12302336 | tf_op jit(solution)/shard_map/dot_general | solution.py:179
  12.9 0.6 pad_clamp_fusion
  14.0 0.6 fusion.9
  14.6 1.3 convert_bitcast_fusion
  16.5 1.2 broadcast_in_dim.92
  17.7 1.3 broadcast_in_dim.93
  19.0 1.2 broadcast_in_dim.88
  20.2 1.3 broadcast_in_dim.89
  21.5 0.7 add_rsqrt_fusion.1
  22.2 1.3 add_multiply_fusion
  25.4 0.7 gather_fusion.1
  26.2 3.8 %convolution_convert_fusion.1 = bf16[192,3584]{1,0:T(8,128)(2,1)S(1)} fusion(bf16[192,768]{1,0:T(8,128)(2,1)S(1)} %bitcast_select_fusion.1, bf16[768,3584]{1,0:T(8,128)(2,1)} %param.7), kind=kOutput, calls=%fused_computation.5 | convolution fusion | flops 1057652736 | bytes 7176192 | tf_op jit(solution)/shard_map/dot_general | solution.py:198
  30.1 3.1 %collective-permute-start.6 = (bf16[1,8,24,1792]{3,2,1,0:T(8,128)(2,1)S(1)}, bf16[1,8,24,1792]{3,2,1,0:T(8,128)(2,1)}, u32[]{:S(2)}, u32[]{:S(2)}) collective-permute-start(bf16[1,8,24,1792]{3,2,1,0:T(8,128)(2,1)S(1)} %select_bitcast_fusion), channel_id=1, source_target_pairs={{0,8},{1,9},{2,10},{3,11},{4,12},{5,13},{6,14},{7,15},{8,0},{9,1},... | collective-permute-start | bytes 2064392 | tf_op jit(solution)/shard_map/ppermute | solution.py:32
  33.2 0.7 gather_fusion
  34.1 4.9 %convolution_convert_fusion = bf16[384,3584]{1,0:T(8,128)(2,1)S(1)} fusion(bf16[384,768]{1,0:T(8,128)(2,1)S(1)} %bitcast_select_fusion, bf16[768,3584]{1,0:T(8,128)(2,1)} %param.7), kind=kOutput, calls=%fused_computation.4 | convolution fusion | flops 2115305472 | bytes 8847360 | tf_op jit(solution)/shard_map/dot_general | solution.py:196
  39.0 1.3 fusion.12
  40.2 1.5 collective-permute-start.2
  41.7 7.2 %collective-permute-done.6 = bf16[1,8,24,1792]{3,2,1,0:T(8,128)(2,1)} collective-permute-done((bf16[1,8,24,1792]{3,2,1,0:T(8,128)(2,1)S(1)}, bf16[1,8,24,1792]{3,2,1,0:T(8,128)(2,1)}, u32[]{:S(2)}, u32[]{:S(2)}) %collective-permute-start.6) | collective-permute-done | bytes 688160 | tf_op jit(solution)/shard_map/ppermute | solution.py:32
  48.9 1.3 fusion.5
  50.3 1.7 collective-permute-start.7
  52.1 10.3 %collective-permute-done.7 = bf16[4,24,1792]{2,1,0:T(8,128)(2,1)S(1)} collective-permute-done((bf16[4,24,1792]{2,1,0:T(8,128)(2,1)S(1)}, bf16[4,24,1792]{2,1,0:T(8,128)(2,1)S(1)}, u32[]{:S(2)}, u32[]{:S(2)}) %collective-permute-start.7) | collective-permute-done | bytes 344096 | tf_op jit(solution)/shard_map/ppermute | solution.py:32
  62.5 1.6 collective-permute-start.8
  64.1 1.7 fusion.3
  66.4 1.6 collective-permute-done.8
  68.1 2.7 %collective-permute-start.9 = (bf16[1,24,1792]{2,1,0:T(8,128)(2,1)S(1)}, bf16[1,24,1792]{2,1,0:T(8,128)(2,1)S(1)}, u32[]{:S(2)}, u32[]{:S(2)}) collective-permute-start(bf16[1,24,1792]{2,1,0:T(8,128)(2,1)S(1)} %slice.143), channel_id=1, source_target_pairs={{0,16},{1,17},{2,18},{3,19},{4,20},{5,21},{6,22},{7,23},{8,24},{9,... | collective-permute-start | bytes 258056 | tf_op jit(solution)/shard_map/ppermute | solution.py:32
  70.8 3.7 %collective-permute-done.9 = bf16[1,24,1792]{2,1,0:T(8,128)(2,1)S(1)} collective-permute-done((bf16[1,24,1792]{2,1,0:T(8,128)(2,1)S(1)}, bf16[1,24,1792]{2,1,0:T(8,128)(2,1)S(1)}, u32[]{:S(2)}, u32[]{:S(2)}) %collective-permute-start.9) | collective-permute-done | bytes 86048 | tf_op jit(solution)/shard_map/ppermute | solution.py:32
  74.5 0.7 multiply_reduce_fusion.6
  75.2 1.7 collective-permute-start.15
  77.1 1.8 collective-permute-start.4
  78.9 2.7 %collective-permute-done.15 = bf16[1,24,1792]{2,1,0:T(8,128)(2,1)S(1)} collective-permute-done((bf16[1,24,1792]{2,1,0:T(8,128)(2,1)S(1)}, bf16[1,24,1792]{2,1,0:T(8,128)(2,1)S(1)}, u32[]{:S(2)}, u32[]{:S(2)}) %collective-permute-start.15) | collective-permute-done | bytes 86048 | tf_op jit(solution)/shard_map/ppermute | solution.py:32
  81.6 1.6 collective-permute-start.16
  83.2 2.5 %collective-permute-done.4 = bf16[2,24,3584]{2,1,0:T(8,128)(2,1)S(1)} collective-permute-done((bf16[2,24,3584]{2,1,0:T(8,128)(2,1)S(1)}, bf16[2,24,3584]{2,1,0:T(8,128)(2,1)S(1)}, u32[]{:S(2)}, u32[]{:S(2)}) %collective-permute-start.4) | collective-permute-done | bytes 344096 | tf_op jit(solution)/shard_map/ppermute | solution.py:32
  85.8 2.8 %collective-permute-start.5 = (bf16[1,24,3584]{2,1,0:T(8,128)(2,1)S(1)}, bf16[1,24,3584]{2,1,0:T(8,128)(2,1)S(1)}, u32[]{:S(2)}, u32[]{:S(2)}) collective-permute-start(bf16[1,24,3584]{2,1,0:T(8,128)(2,1)S(1)} %slice.134), channel_id=1, source_target_pairs={{0,16},{1,17},{2,18},{3,19},{4,20},{5,21},{6,22},{7,23},{8,24},{9,... | collective-permute-start | bytes 516104 | tf_op jit(solution)/shard_map/ppermute | solution.py:32
  88.6 0.8 pad_maximum_fusion.3
  89.9 4.5 %collective-permute-done.5 = bf16[1,24,3584]{2,1,0:T(8,128)(2,1)S(1)} collective-permute-done((bf16[1,24,3584]{2,1,0:T(8,128)(2,1)S(1)}, bf16[1,24,3584]{2,1,0:T(8,128)(2,1)S(1)}, u32[]{:S(2)}, u32[]{:S(2)}) %collective-permute-start.5) | collective-permute-done | bytes 172064 | tf_op jit(solution)/shard_map/ppermute | solution.py:32
  94.5 0.6 collective-permute-start.19
  95.1 0.7 multiply_reduce_fusion.4
  97.1 2.1 collective-permute-start.10
  99.2 5.3 %collective-permute-done.19 = bf16[1,24,3584]{2,1,0:T(8,128)(2,1)S(1)} collective-permute-done((bf16[1,24,3584]{2,1,0:T(8,128)(2,1)S(1)}, bf16[1,24,3584]{2,1,0:T(8,128)(2,1)S(1)}, u32[]{:S(2)}, u32[]{:S(2)}) %collective-permute-start.19) | collective-permute-done | bytes 172064 | tf_op jit(solution)/shard_map/ppermute | solution.py:32
  104.7 2.0 maximum_bitcast_fusion
  106.7 2.0 collective-permute-start.18
  108.8 2.4 %collective-permute-start.11 = (f32[1,128]{1,0:T(1,128)S(1)}, f32[1,128]{1,0:T(1,128)S(1)}, u32[]{:S(2)}, u32[]{:S(2)}) collective-permute-start(f32[1,128]{1,0:T(1,128)S(1)} %fusion.20), channel_id=1, source_target_pairs={{0,4},{1,3},{2,6},{3,1},{4,0},{5,7},{6,2},{7,5},{8,12},{9,11},{10,... | collective-permute-start | bytes 1544 | tf_op jit(solution)/shard_map/ppermute | solution.py:32
  111.2 1.5 collective-permute-done.11
  112.7 13.4 %collective-permute-done.12 = f32[1,128]{1,0:T(1,128)S(1)} collective-permute-done((f32[1,128]{1,0:T(1,128)S(1)}, f32[1,128]{1,0:T(1,128)S(1)}, u32[]{:S(2)}, u32[]{:S(2)}) %collective-permute-start.12) | collective-permute-done | bytes 544 | tf_op jit(solution)/shard_map/ppermute | solution.py:32
  126.2 1.9 collective-permute-start.13
  128.1 0.9 pad_maximum_fusion.2
  129.0 4.4 %collective-permute-start.21 = (bf16[4,24,3584]{2,1,0:T(8,128)(2,1)}, bf16[4,24,3584]{2,1,0:T(8,128)(2,1)}, u32[]{:S(2)}, u32[]{:S(2)}) collective-permute-start(bf16[4,24,3584]{2,1,0:T(8,128)(2,1)} %pad_maximum_fusion.2), channel_id=1, source_target_pairs={{0,4},{1,3},{2,6},{3,1},{4,0},{5,7},{6,2},{7,5},{8,12},{9,11},{10,... | collective-permute-start | bytes 2064392 | tf_op jit(solution)/shard_map/ppermute | solution.py:32
  133.4 0.6 pad_add_fusion.where_ref
  134.0 0.6 broadcast_in_dim.99.gain_ref
  134.6 2.5 %pad_maximum_fusion.g_ref = bf16[2,8,24,1792]{3,2,1,0:T(8,128)(2,1)} fusion(bf16[1,8,24,1792]{3,2,1,0:T(8,128)(2,1)} %collective-permute-done.18, bf16[1,8,24,1792]{3,2,1,0:T(8,128)(2,1)} %maximum_bitcast_fusion), kind=kLoop, calls=%fused_computation.21 | loop fusion | flops 688128 | bytes 2752512 | tf_op jit(solution)/shard_map/concatenate | solution.py:50
  137.2 0.6 fusion.13
  138.5 10.6 %shard_map.87 = f32[2,8,24,128]{3,2,1,0:T(8,128)} custom-call(s32[3]{0:T(128)} %pad_add_fusion.where_ref, f32[1]{0:T(128)} %bitcast.24.coef_ref, bf16[2,8,24,1792]{3,2,1,0:T(8,128)(2,1)} %pad_maximum_fusion.g_ref, bf16[24,24,3584]{2,1,0:T(8,128)(2,1)} %bitcast.62, f32[1,3584]{1,0:T(1,128)} %broadcast_in_dim.99.gain_ref), custom_call_target="tpu_custom_call" | custom-call | tf_op jit(solution)/shard_map/pallas_call | solution.py:138
  149.1 1.0 fusion.7
  150.0 1.2 pad_maximum_fusion.1
  151.4 1.1 constant_dynamic-update-slice_fusion.1
  152.6 17.1 %collective-permute-done.22 = bf16[8,24,3584]{2,1,0:T(8,128)(2,1)S(1)} collective-permute-done((bf16[8,24,3584]{2,1,0:T(8,128)(2,1)S(1)}, bf16[8,24,3584]{2,1,0:T(8,128)(2,1)S(1)}, u32[]{:S(2)}, u32[]{:S(2)}) %collective-permute-start.22) | collective-permute-done | bytes 1376288 | tf_op jit(solution)/shard_map/ppermute | solution.py:32
  169.8 1.5 copy-done.1
  171.3 11.3 %shard_map.86 = f32[16,24,128]{2,1,0:T(8,128)} custom-call(s32[3]{0:T(128)} %pad_add_fusion.where_ref, f32[1]{0:T(128)} %bitcast.24.coef_ref, bf16[16,24,3584]{2,1,0:T(8,128)(2,1)} %copy-done.1, bf16[24,24,3584]{2,1,0:T(8,128)(2,1)} %bitcast.63, f32[1,3584]{1,0:T(1,128)} %broadcast_in_dim.99.gain_ref), custom_call_target="tpu_custom_call" | custom-call | tf_op jit(solution)/shard_map/pallas_call | solution.py:135
  182.6 0.9 pad_maximum_fusion.5
  183.6 1.6 collective-permute-done.23
  185.2 1.7 maximum_add_fusion.peak_ref
  186.8 11.5 %shard_map.88.rest_0_ = bf16[24,24,3584]{2,1,0:T(8,128)(2,1)} custom-call(s32[3]{0:T(128)} %pad_add_fusion.where_ref, f32[1]{0:T(128)} %bitcast.24.coef_ref, bf16[16,24,3584]{2,1,0:T(8,128)(2,1)} %copy-done.1, bf16[24,24,3584]{2,1,0:T(8,128)(2,1)} %bitcast.64, f32[1,3584]{1,0:T(1,128)} %broadcast_in_dim.99.gain_ref, f32[24,24,128]{2,1,0:T(8,128)} %maximum_add_fusion.peak_ref), custom_call_target="tpu_custom_call" | custom-call | tf_op jit(solution)/shard_map/pallas_call | solution.py:148
  198.4 10.7 %shard_map.89 = bf16[24,24,3584]{2,1,0:T(8,128)(2,1)} custom-call(s32[3]{0:T(128)} %pad_add_fusion.where_ref, f32[1]{0:T(128)} %bitcast.24.coef_ref, bf16[2,8,24,1792]{3,2,1,0:T(8,128)(2,1)} %pad_maximum_fusion.g_ref, bf16[24,24,3584]{2,1,0:T(8,128)(2,1)} %bitcast.65, f32[1,3584]{1,0:T(1,128)} %broadcast_in_dim.99.gain_ref, ...), custom_call_target="tpu_custom_call", output_to_operand_aliasing={{}: (6, {})} | custom-call | tf_op jit(solution)/shard_map/pallas_call | solution.py:151
  (95 shorter events, 6.6 us)
Async XLA Ops:
  0.6 4.9 %copy-start.5 = (f32[3584]{0:T(1024)S(1)}, f32[3584]{0:T(1024)}, u32[]{:S(2)}) copy-start(f32[3584]{0:T(1024)} %param.11) | copy-start | bytes 43012
  0.6 4.9 %copy-start = (bf16[3584,576]{0,1:T(8,128)(2,1)S(1)}, bf16[3584,576]{0,1:T(8,128)(2,1)}, u32[]{:S(2)}) copy-start(bf16[3584,576]{0,1:T(8,128)(2,1)} %param.13) | copy-start | bytes 12386308
  5.1 7.4 %copy-start.12 = (s32[1,8]{1,0:T(1,128)S(1)}, s32[1,8]{1,0:T(1,128)}, u32[]{:S(2)}) copy-start(s32[1,8]{1,0:T(1,128)} %param.9) | copy-start | bytes 100
  5.1 16.4 %collective-permute-start.1 = (f32[768]{0:T(1024)}, f32[768]{0:T(1024)}, u32[]{:S(2)}, u32[]{:S(2)}) collective-permute-start(f32[768]{0:T(1024)} %multiply_reduce_fusion), channel_id=1, source_target_pairs={{0,1},{1,0},{2,3},{3,2},{4,5},{5,4},{6,7},{7,6},{8,9},{9,8},{10,11... | collective-permute-start | bytes 9224 | tf_op jit(solution)/shard_map/ppermute | solution.py:36
  12.5 9.7 %collective-permute-start = (bf16[576,768]{1,0:T(8,128)(2,1)}, bf16[576,768]{1,0:T(8,128)(2,1)}, u32[]{:S(2)}, u32[]{:S(2)}) collective-permute-start(bf16[576,768]{1,0:T(8,128)(2,1)} %get-tuple-element.15), channel_id=1, source_target_pairs={{0,1},{1,0},{2,3},{3,2},{4,5},{5,4},{6,7},{7,6},{8,9},{9,8},{10,11... | collective-permute-start | bytes 2654216 | tf_op jit(solution)/shard_map/ppermute | solution.py:36
  12.9 1.1 copy-start.7
  22.2 1.5 copy-start.6
  23.5 0.7 copy-start.9
  24.2 0.7 copy-start.8
  25.4 4.7 %copy-start.2 = (bf16[576,768]{1,0:T(8,128)(2,1)}, bf16[576,768]{1,0:T(8,128)(2,1)S(1)}, u32[]{:S(2)}) copy-start(bf16[576,768]{1,0:T(8,128)(2,1)S(1)} %fusion.4) | copy-start | bytes 2654212
  25.4 0.7 copy-start.13
  30.0 3.9 %copy-start.11 = (pred[384]{0:T(512)(128)(4,1)S(1)}, pred[384]{0:T(512)(128)(4,1)}, u32[]{:S(2)}) copy-start(pred[384]{0:T(512)(128)(4,1)} %broadcast_in_dim.89) | copy-start | bytes 1156
  30.0 3.2 %slice-start = ((bf16[576,768]{1,0:T(8,128)(2,1)}), bf16[384,768]{1,0:T(8,128)(2,1)S(1)}, s32[]{:S(2)}) async-start(bf16[576,768]{1,0:T(8,128)(2,1)} %copy-done.2), calls=%async_computation | async-start | bytes 1179648 | tf_op jit(solution)/shard_map/slice | solution.py:193
  30.1 18.8 %collective-permute-start.6 = (bf16[1,8,24,1792]{3,2,1,0:T(8,128)(2,1)S(1)}, bf16[1,8,24,1792]{3,2,1,0:T(8,128)(2,1)}, u32[]{:S(2)}, u32[]{:S(2)}) collective-permute-start(bf16[1,8,24,1792]{3,2,1,0:T(8,128)(2,1)S(1)} %select_bitcast_fusion), channel_id=1, source_target_pairs={{0,8},{1,9},{2,10},{3,11},{4,12},{5,13},{6,14},{7,15},{8,0},{9,1},... | collective-permute-start | bytes 2064392 | tf_op jit(solution)/shard_map/ppermute | solution.py:32
  40.2 11.8 %copy-start.10 = (s32[768,1]{0,1:T(1,128)S(1)}, s32[768,1]{0,1:T(1,128)}, u32[]{:S(2)}) copy-start(s32[768,1]{0,1:T(1,128)} %param.10) | copy-start | bytes 9220
  40.2 23.9 %collective-permute-start.2 = (bf16[8,24,3584]{2,1,0:T(8,128)(2,1)}, bf16[8,24,3584]{2,1,0:T(8,128)(2,1)}, u32[]{:S(2)}, u32[]{:S(2)}) collective-permute-start(bf16[8,24,3584]{2,1,0:T(8,128)(2,1)} %bitcast.9), channel_id=1, source_target_pairs={{0,2},{1,5},{2,0},{3,7},{4,6},{5,1},{6,4},{7,3},{8,10},{9,13},{10,... | collective-permute-start | bytes 4128776 | tf_op jit(solution)/shard_map/ppermute | solution.py:32
  50.3 12.1 %collective-permute-start.7 = (bf16[4,24,1792]{2,1,0:T(8,128)(2,1)S(1)}, bf16[4,24,1792]{2,1,0:T(8,128)(2,1)S(1)}, u32[]{:S(2)}, u32[]{:S(2)}) collective-permute-start(bf16[4,24,1792]{2,1,0:T(8,128)(2,1)S(1)} %slice_bitcast_fusion), channel_id=1, source_target_pairs={{0,2},{1,5},{2,0},{3,7},{4,6},{5,1},{6,4},{7,3},{8,10},{9,13},{10,... | collective-permute-start | bytes 1032200 | tf_op jit(solution)/shard_map/ppermute | solution.py:32
  62.5 5.5 %collective-permute-start.8 = (bf16[2,24,1792]{2,1,0:T(8,128)(2,1)S(1)}, bf16[2,24,1792]{2,1,0:T(8,128)(2,1)S(1)}, u32[]{:S(2)}, u32[]{:S(2)}) collective-permute-start(bf16[2,24,1792]{2,1,0:T(8,128)(2,1)S(1)} %slice.141), channel_id=1, source_target_pairs={{0,4},{1,3},{2,6},{3,1},{4,0},{5,7},{6,2},{7,5},{8,12},{9,11},{10,... | collective-permute-start | bytes 516104 | tf_op jit(solution)/shard_map/ppermute | solution.py:32
  65.8 11.0 %collective-permute-start.3 = (bf16[4,24,3584]{2,1,0:T(8,128)(2,1)S(1)}, bf16[4,24,3584]{2,1,0:T(8,128)(2,1)S(1)}, u32[]{:S(2)}, u32[]{:S(2)}) collective-permute-start(bf16[4,24,3584]{2,1,0:T(8,128)(2,1)S(1)} %slice.130), channel_id=1, source_target_pairs={{0,4},{1,3},{2,6},{3,1},{4,0},{5,7},{6,2},{7,5},{8,12},{9,11},{10,... | collective-permute-start | bytes 2064392 | tf_op jit(solution)/shard_map/ppermute | solution.py:32
  68.1 6.4 %collective-permute-start.9 = (bf16[1,24,1792]{2,1,0:T(8,128)(2,1)S(1)}, bf16[1,24,1792]{2,1,0:T(8,128)(2,1)S(1)}, u32[]{:S(2)}, u32[]{:S(2)}) collective-permute-start(bf16[1,24,1792]{2,1,0:T(8,128)(2,1)S(1)} %slice.143), channel_id=1, source_target_pairs={{0,16},{1,17},{2,18},{3,19},{4,20},{5,21},{6,22},{7,23},{8,24},{9,... | collective-permute-start | bytes 258056 | tf_op jit(solution)/shard_map/ppermute | solution.py:32
  75.2 6.4 %collective-permute-start.15 = (bf16[1,24,1792]{2,1,0:T(8,128)(2,1)S(1)}, bf16[1,24,1792]{2,1,0:T(8,128)(2,1)S(1)}, u32[]{:S(2)}, u32[]{:S(2)}) collective-permute-start(bf16[1,24,1792]{2,1,0:T(8,128)(2,1)S(1)} %get-tuple-element.7), channel_id=1, source_target_pairs={{0,16},{1,17},{2,18},{3,19},{4,20},{5,21},{6,22},{7,23},{8,24},{9,... | collective-permute-start | bytes 258056 | tf_op jit(solution)/shard_map/ppermute | solution.py:32
  77.1 8.6 %collective-permute-start.4 = (bf16[2,24,3584]{2,1,0:T(8,128)(2,1)S(1)}, bf16[2,24,3584]{2,1,0:T(8,128)(2,1)S(1)}, u32[]{:S(2)}, u32[]{:S(2)}) collective-permute-start(bf16[2,24,3584]{2,1,0:T(8,128)(2,1)S(1)} %slice.132), channel_id=1, source_target_pairs={{0,8},{1,9},{2,10},{3,11},{4,12},{5,13},{6,14},{7,15},{8,0},{9,1},... | collective-permute-start | bytes 1032200 | tf_op jit(solution)/shard_map/ppermute | solution.py:32
  81.6 12.9 %copy-start.3 = (bf16[1,24,1792]{2,1,0:T(8,128)(2,1)}, bf16[1,24,1792]{2,1,0:T(8,128)(2,1)S(1)}, u32[]{:S(2)}) copy-start(bf16[1,24,1792]{2,1,0:T(8,128)(2,1)S(1)} %collective-permute-done.15) | copy-start | bytes 258052
  81.6 7.0 %collective-permute-start.16 = (bf16[2,24,1792]{2,1,0:T(8,128)(2,1)S(1)}, bf16[2,24,1792]{2,1,0:T(8,128)(2,1)S(1)}, u32[]{:S(2)}, u32[]{:S(2)}) collective-permute-start(bf16[2,24,1792]{2,1,0:T(8,128)(2,1)S(1)} %pad_maximum_fusion.6), channel_id=1, source_target_pairs={{0,4},{1,3},{2,6},{3,1},{4,0},{5,7},{6,2},{7,5},{8,12},{9,11},{10,... | collective-permute-start | bytes 516104 | tf_op jit(solution)/shard_map/ppermute | solution.py:32
  85.8 8.6 %collective-permute-start.5 = (bf16[1,24,3584]{2,1,0:T(8,128)(2,1)S(1)}, bf16[1,24,3584]{2,1,0:T(8,128)(2,1)S(1)}, u32[]{:S(2)}, u32[]{:S(2)}) collective-permute-start(bf16[1,24,3584]{2,1,0:T(8,128)(2,1)S(1)} %slice.134), channel_id=1, source_target_pairs={{0,16},{1,17},{2,18},{3,19},{4,20},{5,21},{6,22},{7,23},{8,24},{9,... | collective-permute-start | bytes 516104 | tf_op jit(solution)/shard_map/ppermute | solution.py:32
  88.6 5.9 %copy-start.4 = (bf16[2,24,1792]{2,1,0:T(8,128)(2,1)}, bf16[2,24,1792]{2,1,0:T(8,128)(2,1)S(1)}, u32[]{:S(2)}) copy-start(bf16[2,24,1792]{2,1,0:T(8,128)(2,1)S(1)} %collective-permute-done.16) | copy-start | bytes 516100
  89.4 15.3 %collective-permute-start.17 = (bf16[4,24,1792]{2,1,0:T(8,128)(2,1)}, bf16[4,24,1792]{2,1,0:T(8,128)(2,1)}, u32[]{:S(2)}, u32[]{:S(2)}) collective-permute-start(bf16[4,24,1792]{2,1,0:T(8,128)(2,1)} %pad_maximum_fusion.3), channel_id=1, source_target_pairs={{0,2},{1,5},{2,0},{3,7},{4,6},{5,1},{6,4},{7,3},{8,10},{9,13},{10,... | collective-permute-start | bytes 1032200 | tf_op jit(solution)/shard_map/ppermute | solution.py:32
  94.5 10.1 %collective-permute-start.19 = (bf16[1,24,3584]{2,1,0:T(8,128)(2,1)S(1)}, bf16[1,24,3584]{2,1,0:T(8,128)(2,1)S(1)}, u32[]{:S(2)}, u32[]{:S(2)}) collective-permute-start(bf16[1,24,3584]{2,1,0:T(8,128)(2,1)S(1)} %get-tuple-element.5), channel_id=1, source_target_pairs={{0,16},{1,17},{2,18},{3,19},{4,20},{5,21},{6,22},{7,23},{8,24},{9,... | collective-permute-start | bytes 516104 | tf_op jit(solution)/shard_map/ppermute | solution.py:32
  97.1 11.5 %collective-permute-start.10 = (f32[1,128]{1,0:T(1,128)S(1)}, f32[1,128]{1,0:T(1,128)S(1)}, u32[]{:S(2)}, u32[]{:S(2)}) collective-permute-start(f32[1,128]{1,0:T(1,128)S(1)} %maximum_bitcast_fusion.1), channel_id=1, source_target_pairs={{0,2},{1,5},{2,0},{3,7},{4,6},{5,1},{6,4},{7,3},{8,10},{9,13},{10,... | collective-permute-start | bytes 1544 | tf_op jit(solution)/shard_map/ppermute | solution.py:32
  104.6 23.5 %collective-permute-start.20 = (bf16[2,24,3584]{2,1,0:T(8,128)(2,1)S(1)}, bf16[2,24,3584]{2,1,0:T(8,128)(2,1)S(1)}, u32[]{:S(2)}, u32[]{:S(2)}) collective-permute-start(bf16[2,24,3584]{2,1,0:T(8,128)(2,1)S(1)} %pad_maximum_fusion.4), channel_id=1, source_target_pairs={{0,8},{1,9},{2,10},{3,11},{4,12},{5,13},{6,14},{7,15},{8,0},{9,1},... | collective-permute-start | bytes 1032200 | tf_op jit(solution)/shard_map/ppermute | solution.py:32
  106.7 28.0 %collective-permute-start.18 = (bf16[1,8,24,1792]{3,2,1,0:T(8,128)(2,1)}, bf16[1,8,24,1792]{3,2,1,0:T(8,128)(2,1)}, u32[]{:S(2)}, u32[]{:S(2)}) collective-permute-start(bf16[1,8,24,1792]{3,2,1,0:T(8,128)(2,1)} %maximum_bitcast_fusion), channel_id=1, source_target_pairs={{0,8},{1,9},{2,10},{3,11},{4,12},{5,13},{6,14},{7,15},{8,0},{9,1},... | collective-permute-start | bytes 2064392 | tf_op jit(solution)/shard_map/ppermute | solution.py:32
  108.8 3.9 %collective-permute-start.11 = (f32[1,128]{1,0:T(1,128)S(1)}, f32[1,128]{1,0:T(1,128)S(1)}, u32[]{:S(2)}, u32[]{:S(2)}) collective-permute-start(f32[1,128]{1,0:T(1,128)S(1)} %fusion.20), channel_id=1, source_target_pairs={{0,4},{1,3},{2,6},{3,1},{4,0},{5,7},{6,2},{7,5},{8,12},{9,11},{10,... | collective-permute-start | bytes 1544 | tf_op jit(solution)/shard_map/ppermute | solution.py:32
  112.7 13.4 %collective-permute-start.12 = (f32[1,128]{1,0:T(1,128)S(1)}, f32[1,128]{1,0:T(1,128)S(1)}, u32[]{:S(2)}, u32[]{:S(2)}) collective-permute-start(f32[1,128]{1,0:T(1,128)S(1)} %add.154), channel_id=1, source_target_pairs={{0,8},{1,9},{2,10},{3,11},{4,12},{5,13},{6,14},{7,15},{8,0},{9,1},... | collective-permute-start | bytes 1544 | tf_op jit(solution)/shard_map/ppermute | solution.py:32
  126.2 8.5 %collective-permute-start.13 = (f32[1,128]{1,0:T(1,128)S(1)}, f32[1,128]{1,0:T(1,128)S(1)}, u32[]{:S(2)}, u32[]{:S(2)}) collective-permute-start(f32[1,128]{1,0:T(1,128)S(1)} %add.155), channel_id=1, source_target_pairs={{0,16},{1,17},{2,18},{3,19},{4,20},{5,21},{6,22},{7,23},{8,24},{9,... | collective-permute-start | bytes 1544 | tf_op jit(solution)/shard_map/ppermute | solution.py:32
  129.0 21.0 %collective-permute-start.21 = (bf16[4,24,3584]{2,1,0:T(8,128)(2,1)}, bf16[4,24,3584]{2,1,0:T(8,128)(2,1)}, u32[]{:S(2)}, u32[]{:S(2)}) collective-permute-start(bf16[4,24,3584]{2,1,0:T(8,128)(2,1)} %pad_maximum_fusion.2), channel_id=1, source_target_pairs={{0,4},{1,3},{2,6},{3,1},{4,0},{5,7},{6,2},{7,5},{8,12},{9,11},{10,... | collective-permute-start | bytes 2064392 | tf_op jit(solution)/shard_map/ppermute | solution.py:32
  134.6 2.6 %collective-permute-start.14 = (f32[1,128]{1,0:T(1,128)S(1)}, f32[1,128]{1,0:T(1,128)S(1)}, u32[]{:S(2)}, u32[]{:S(2)}) collective-permute-start(f32[1,128]{1,0:T(1,128)S(1)} %add.156), channel_id=1, source_target_pairs={{0,1},{1,0},{2,3},{3,2},{4,5},{5,4},{6,7},{7,6},{8,9},{9,8},{10,11... | collective-permute-start | bytes 1544 | tf_op jit(solution)/shard_map/ppermute | solution.py:36
  151.3 18.4 %collective-permute-start.22 = (bf16[8,24,3584]{2,1,0:T(8,128)(2,1)S(1)}, bf16[8,24,3584]{2,1,0:T(8,128)(2,1)S(1)}, u32[]{:S(2)}, u32[]{:S(2)}) collective-permute-start(bf16[8,24,3584]{2,1,0:T(8,128)(2,1)S(1)} %pad_maximum_fusion.1), channel_id=1, source_target_pairs={{0,2},{1,5},{2,0},{3,7},{4,6},{5,1},{6,4},{7,3},{8,10},{9,13},{10,... | collective-permute-start | bytes 4128776 | tf_op jit(solution)/shard_map/ppermute | solution.py:32
  169.8 1.5 copy-start.1
  183.5 1.6 collective-permute-start.23

commit v2 on v1

v2 whole, which is shorter than its diff:
```python
import functools

import jax
import jax.numpy as jnp
from jax import lax
from jax.experimental import pallas as pl
from jax.experimental.pallas import tpu as pltpu
from jax.sharding import PartitionSpec as P

EPS = 1e-06
RATE = 0.5
F32 = jnp.float32
BF16 = jnp.bfloat16

STEPS = {"xy": (1, 2), "yx": (2, 1), "lo": (4, 4), "hi": (8, 8)}

SCATTER = (("xy", "yx", "hi", "lo"), ("xy", "lo", "yx", "hi"), ("lo", "xy", "yx", "hi"))
GATHER = ((3, 2, 1, 0), (3, 2, 0, 1), (3, 2, 0, 1))


def row_weights(lengths, row_count):
    bounds = jnp.cumsum(lengths)
    position = lax.iota(jnp.int32, row_count)
    group_index = jnp.sum((position[None, :] >= bounds[:, None]).astype(jnp.int32), axis=0)
    member = group_index[None, :] == lax.iota(jnp.int32, lengths.shape[0])[:, None]
    length = jnp.sum(jnp.where(member, lengths[:, None], 0), axis=0)
    return (1.0 / length.astype(F32)).astype(BF16)


def exchange(value, step):
    pairs = []
    for roll in range(16):
        for core in range(2):
            pairs.append((2 * roll + core, 2 * (roll ^ STEPS[step][core]) + core))
    return lax.ppermute(value, ("roll", "tp"), pairs)


def swap_cores(value):
    return lax.ppermute(value, "tp", [(0, 1), (1, 0)])


def add(a, b):
    return (a.astype(F32) + b.astype(F32)).astype(a.dtype)


def head(latent, targets, weights, gain_vec, groups):
    width = gain_vec.shape[0]
    compressed = latent[:width]
    factor = lax.rsqrt(jnp.mean(compressed * compressed, axis=0) + EPS)
    gain_col = gain_vec[:, None]
    weight_f = weights.astype(F32)
    targets = targets.astype(F32)
    res_c = compressed * factor[None, :] * gain_col - targets[:width]
    res_r = latent[width:] - targets[width:]
    total = jnp.sum(res_c * res_c, axis=0) + jnp.sum(res_r * res_r, axis=0)
    row_terms = weight_f * (0.5 * total / latent.shape[0]) / groups
    scaled = weight_f[None, :] * res_c * gain_col
    inner = jnp.mean(scaled * compressed, axis=0)
    d_c = factor[None, :] * scaled - compressed * (factor * factor * factor * inner)[None, :]
    return row_terms, jnp.concatenate([d_c, weight_f[None, :] * res_r], axis=0)


def forward_kernel(x_ref, w_ref, gain_ref, part_ref, sent_ref, sq_ref, sq_acc):
    step = pl.program_id(0)
    x = x_ref[...]
    gained = (w_ref[...].astype(F32) * gain_ref[...]).astype(BF16)
    part = lax.dot_general(gained, x, (((1,), (1,)), ((), ())), preferred_element_type=F32)
    wide = x.astype(F32)
    wide = wide * wide
    sq = wide[:, :128]
    for c in range(1, x.shape[1] // 128):
        sq = sq + wide[:, c * 128 : (c + 1) * 128]

    @pl.when(step == 0)
    def _():
        part_ref[...] = part
        sq_acc[...] = sq

    @pl.when(step > 0)
    def _():
        part_ref[...] += part
        sq_acc[...] += sq

    @pl.when(step == pl.num_programs(0) - 1)
    def _():
        ones = jnp.ones((8, 128), F32)
        total = lax.dot_general(
            ones, sq_acc[...], (((1,), (1,)), ((), ())), preferred_element_type=F32, precision=lax.Precision.HIGHEST
        )
        sq_ref[...] = total
        width = part_ref.shape[0]
        sent_ref[:width] = part_ref[...].astype(BF16)
        row = total[:1]
        top = row.astype(BF16)
        rest = row - top.astype(F32)
        mid = rest.astype(BF16)
        low = (rest - mid.astype(F32)).astype(BF16)
        index = lax.broadcasted_iota(jnp.int32, (16, row.shape[1]), 0)
        terms = jnp.where(
            index == 0,
            top.astype(F32),
            jnp.where(index == 1, mid.astype(F32), jnp.where(index == 2, low.astype(F32), 0.0)),
        )
        sent_ref[width:] = terms.astype(BF16)


def forward(x, w_t, gain_row):
    rows, feat = x.shape
    width = w_t.shape[0]
    cols = 512
    return pl.pallas_call(
        forward_kernel,
        grid=(feat // cols,),
        in_specs=[
            pl.BlockSpec((rows, cols), lambda k: (0, k)),
            pl.BlockSpec((width, cols), lambda k: (0, k)),
            pl.BlockSpec((1, cols), lambda k: (0, k)),
        ],
        out_specs=[
            pl.BlockSpec((width, rows), lambda k: (0, 0)),
            pl.BlockSpec((width + 16, rows), lambda k: (0, 0)),
            pl.BlockSpec((8, rows), lambda k: (0, 0)),
        ],
        out_shape=[
            jax.ShapeDtypeStruct((width, rows), F32),
            jax.ShapeDtypeStruct((width + 16, rows), BF16),
            jax.ShapeDtypeStruct((8, rows), F32),
        ],
        scratch_shapes=[pltpu.VMEM((rows, 128), F32)],
        compiler_params=pltpu.CompilerParams(vmem_limit_bytes=24 * 1024 * 1024),
        cost_estimate=pl.CostEstimate(flops=2 * rows * feat * width, bytes_accessed=10_000_000, transcendentals=0),
    )(x, w_t, gain_row)


def head_kernel(model_width, masks_ref, lens_ref, part_ref, got_ref, sq_ref, target_ref, dest_ref, gain_ref, d_ref, loss_ref):
    step = pl.program_id(0)
    width, lanes = part_ref.shape
    lat = gain_ref.shape[0]
    groups = lens_ref.shape[0]
    terms = got_ref[width:].astype(F32)
    squares = sq_ref[:1] + (terms[0:1] + terms[1:2] + terms[2:3])
    scale = lax.rsqrt(squares / model_width + EPS)
    position = lax.broadcasted_iota(jnp.int32, (1, lanes), 1) + step * lanes
    length = jnp.zeros((1, lanes), jnp.int32)
    start = 0
    for g in range(groups):
        size = lens_ref[g]
        length = jnp.where((position >= start) & (position < start + size), size, length)
        start = start + size
    weight = (1.0 / length.astype(F32)).astype(BF16).astype(F32)

    gain = gain_ref[...]
    comp = (part_ref[:lat] + got_ref[:lat].astype(F32)) * scale
    factor = lax.rsqrt(jnp.mean(comp * comp, axis=0, keepdims=True) + EPS)
    res_c = comp * factor * gain - target_ref[:lat].astype(F32)
    res_r = (part_ref[lat:] + got_ref[lat:width].astype(F32)) * scale - target_ref[lat:].astype(F32)
    total = jnp.sum(res_c * res_c, axis=0, keepdims=True) + jnp.sum(res_r * res_r, axis=0, keepdims=True)
    row_terms = weight * (0.5 * (total / width)) / groups
    scaled = weight * res_c * gain
    inner = jnp.mean(scaled * comp, axis=0, keepdims=True)
    d_c = (factor * scale) * scaled - comp * (factor * factor * factor * inner * scale)
    d_r = (weight * scale) * res_r

    blk = d_ref.shape[1]
    for j in range(d_ref.shape[0]):
        lo, hi = j * blk, (j + 1) * blk
        if hi <= lat:
            piece = d_c[lo:hi]
        elif lo >= lat:
            piece = d_r[lo - lat : hi - lat]
        else:
            piece = jnp.concatenate([d_c[lo:], d_r[: hi - lat]], axis=0)
        d_ref[(j // 4) * 4 + ((j % 4) ^ masks_ref[j // 4])] = piece.astype(BF16)

    trainers = loss_ref.shape[0]
    named = dest_ref[...] == lax.broadcasted_iota(jnp.int32, (trainers, lanes), 0)
    sums = jnp.sum(jnp.where(named, row_terms, 0.0), axis=1, keepdims=True)
    sums = jnp.broadcast_to(sums, loss_ref.shape)

    @pl.when(step == 0)
    def _():
        loss_ref[...] = sums

    @pl.when(step > 0)
    def _():
        loss_ref[...] += sums


def head_call(part, got, sq, targets_t, dest_row, lengths, gain_col, row_masks, model_width, trainers):
    width, rows = part.shape
    lanes = 256
    smem = pl.BlockSpec(memory_space=pltpu.SMEM)
    return pl.pallas_call(
        functools.partial(head_kernel, model_width),
        grid=(rows // lanes,),
        in_specs=[
            smem,
            smem,
            pl.BlockSpec((width, lanes), lambda i: (0, i)),
            pl.BlockSpec((width + 16, lanes), lambda i: (0, i)),
            pl.BlockSpec((8, lanes), lambda i: (0, i)),
            pl.BlockSpec((width, lanes), lambda i: (0, i)),
            pl.BlockSpec((1, lanes), lambda i: (0, i)),
            pl.BlockSpec(gain_col.shape, lambda i: (0, 0)),
        ],
        out_specs=[
            pl.BlockSpec((12, width // 12, lanes), lambda i: (0, 0, i)),
            pl.BlockSpec((trainers, 128), lambda i: (0, 0)),
        ],
        out_shape=[
            jax.ShapeDtypeStruct((12, width // 12, rows), BF16),
            jax.ShapeDtypeStruct((trainers, 128), F32),
        ],
        compiler_params=pltpu.CompilerParams(vmem_limit_bytes=24 * 1024 * 1024),
        cost_estimate=pl.CostEstimate(flops=20 * width * rows, bytes_accessed=4_000_000, transcendentals=0),
    )(row_masks, lengths, part, got, sq, targets_t, dest_row, gain_col)


def grad_kernel(first, count, where_ref, d_ref, x_ref, *out_refs):
    blocks, blk, rows = d_ref.shape
    lhs = d_ref[first * 4 : (first + count) * 4].reshape(count * 4 * blk, rows)
    out = jnp.dot(lhs, x_ref[...], preferred_element_type=F32).astype(BF16)
    for c in range(count):
        part = out[c * 4 * blk : (c + 1) * 4 * blk]
        out_refs[c][...] = part.reshape(out_refs[c].shape)


def grad_half(first, count, d, x, half, low_masks):
    rows, feat = x.shape
    cols = feat // 4
    blk = d.shape[1]
    where = jnp.stack([half, *low_masks]).astype(jnp.int32)
    return pl.pallas_call(
        functools.partial(grad_kernel, first, count),
        grid_spec=pltpu.PrefetchScalarGridSpec(
            num_scalar_prefetch=1,
            grid=(2,),
            in_specs=[
                pl.BlockSpec(d.shape, lambda i, wh: (0, 0, 0)),
                pl.BlockSpec((rows, cols), lambda i, wh: (0, wh[0] * 2 + i)),
            ],
            out_specs=[
                pl.BlockSpec((1, 4, blk, cols), lambda i, wh, c=c: (i ^ wh[1 + c], 0, 0, 0)) for c in range(count)
            ],
        ),
        out_shape=[jax.ShapeDtypeStruct((2, 4, blk, cols), BF16)] * count,
        compiler_params=pltpu.CompilerParams(vmem_limit_bytes=24 * 1024 * 1024),
        cost_estimate=pl.CostEstimate(
            flops=2 * count * 4 * blk * rows * feat // 2, bytes_accessed=rows * feat, transcendentals=0
        ),
    )(where, d, x)


def code_kernel(where_ref, coef_ref, g_ref, w_ref, gain_ref, peak_ref, *rest):
    out_ref = rest[-1]
    blk = g_ref.shape[2]
    factor = coef_ref[0] * gain_ref[...]
    for j in range(4):
        rows = slice(j * blk, (j + 1) * blk)
        g = g_ref[0, j ^ where_ref[2]].astype(F32)
        inv = 1.0 / peak_ref[rows, :1]
        out_ref[rows] = ((w_ref[rows].astype(F32) - factor * g) * inv).astype(BF16)


def code_piece(chain, piece, w_t, gain_row, coef, peak, columns, row_mask, codes):
    blk, cols = piece.shape[-2:]
    piece = piece.reshape(2, 4, blk, cols)
    where = jnp.stack([*columns, row_mask]).astype(jnp.int32)
    extra = [] if codes is None else [codes]
    return pl.pallas_call(
        code_kernel,
        grid_spec=pltpu.PrefetchScalarGridSpec(
            num_scalar_prefetch=1,
            grid=(2,),
            in_specs=[
                pl.BlockSpec(memory_space=pltpu.SMEM),
                pl.BlockSpec((1, 4, blk, cols), lambda i, wh: (i, 0, 0, 0)),
                pl.BlockSpec((4 * blk, cols), lambda i, wh: (chain, wh[i])),
                pl.BlockSpec((1, cols), lambda i, wh: (0, wh[i])),
                pl.BlockSpec((4 * blk, 128), lambda i, wh: (chain, 0)),
            ]
            + [pl.BlockSpec(memory_space=pl.ANY)] * len(extra),
            out_specs=pl.BlockSpec((4 * blk, cols), lambda i, wh: (chain, wh[i])),
        ),
        out_shape=jax.ShapeDtypeStruct(w_t.shape, BF16),
        input_output_aliases={6: 0} if extra else {},
        compiler_params=pltpu.CompilerParams(vmem_limit_bytes=24 * 1024 * 1024),
        cost_estimate=pl.CostEstimate(flops=16 * blk * cols, bytes_accessed=48 * blk * cols, transcendentals=0),
    )(where, coef, piece, w_t, gain_row, peak, *extra)


def paired_shards(hidden, targets, group_lengths, dest_ids, input_gain, latent_gain, kv_weight):
    rows, feat = hidden.shape
    width = kv_weight.shape[1]
    model_width = 2 * feat
    blk, cols = width // 12, feat // 4
    roll = lax.axis_index("roll")
    core = lax.axis_index("tp")
    x_bit, y_bit = roll & 1, (roll >> 1) & 1
    bit = {
        "xy": jnp.where(core == 0, x_bit, y_bit),
        "yx": jnp.where(core == 0, y_bit, x_bit),
        "lo": (roll >> 2) & 1,
        "hi": (roll >> 3) & 1,
    }
    bits = [[bit[step] for step in order] for order in SCATTER]
    row_masks = [b[2] * 2 + b[3] for b in bits]

    w_t = kv_weight.T
    gain_row = input_gain[None, :]
    part, sent, squares = forward(hidden, w_t, gain_row)
    got = swap_cores(sent)
    d, losses = head_call(
        part,
        got,
        squares,
        targets.T,
        dest_ids.T,
        group_lengths[0],
        latent_gain[:, None],
        jnp.stack(row_masks).astype(jnp.int32),
        model_width,
        16,
    )

    out_a, out_b = grad_half(0, 2, d, hidden, 1 - bits[0][0], [bits[0][1], bits[1][1]])
    (out_c,) = grad_half(2, 1, d, hidden, 1 - bits[2][0], [bits[2][1]])
    in_a, in_b = grad_half(0, 2, d, hidden, bits[0][0], [bits[0][1], bits[1][1]])
    (in_c,) = grad_half(2, 1, d, hidden, bits[2][0], [bits[2][1]])
    shape = (2, 2, 2, blk, cols)
    sums = []
    for order, away, keep in zip(SCATTER, (out_a, out_b, out_c), (in_a, in_b, in_c)):
        value = add(keep.reshape(shape), exchange(away.reshape(shape), order[0]))
        for step in order[1:]:
            value = add(value[0], exchange(value[1], step))
        sums.append(value)

    own_cols = [b[0] * 2 + b[1] for b in bits]
    own_gain = [lax.dynamic_slice(gain_row, (0, c * cols), (1, cols)) for c in own_cols]
    power = sum(jnp.sum(jnp.square(v.astype(F32) * g)) for v, g in zip(sums, own_gain))
    small = jnp.concatenate([0.5 * losses, jnp.broadcast_to(power, (8, 128))], axis=0)
    for step in ("xy", "yx", "lo", "hi"):
        small = small + exchange(small, step)
    small = small + swap_cores(small)
    coef = RATE * lax.rsqrt(small[16, :1] / (model_width * width) + EPS)

    peak = jnp.zeros((3, 4, blk), F32)
    for chain in range(3):
        own_w = lax.dynamic_slice(
            w_t, (chain * 4 * blk + row_masks[chain] * blk, own_cols[chain] * cols), (blk, cols)
        )
        updated = own_w.astype(F32) - coef * own_gain[chain] * sums[chain].astype(F32)
        top = jnp.max(jnp.abs(updated), axis=1)
        peak = lax.dynamic_update_slice(peak, top[None, None], (chain, row_masks[chain], 0))
    for step in ("xy", "yx", "lo", "hi"):
        peak = jnp.maximum(peak, exchange(peak, step))
    peak = jnp.maximum(peak, swap_cores(peak)) + EPS
    peak = jnp.broadcast_to(peak.reshape(width, 1), (width, 128))

    pieces = []
    for chain in range(3):
        value = sums[chain].reshape(1, 1, 1, 1, blk, cols)
        for axis in GATHER[chain][:3]:
            value = jnp.concatenate([value, exchange(value, SCATTER[chain][axis])], axis=axis)
        pieces.append((value, exchange(value, SCATTER[chain][GATHER[chain][3]])))

    codes = None
    for p in range(2):
        for chain in (2, 1, 0):
            last = GATHER[chain][3]
            mine = own_cols[chain]
            columns = [(2 * p + i if last == 0 else 2 * i + p) ^ mine for i in range(2)]
            codes = code_piece(
                chain, pieces[chain][p], w_t, gain_row, coef, peak, columns, row_masks[chain], codes
            )
    loss = lax.dynamic_slice(small, (roll, 0), (1, 1))
    return loss.reshape(1), codes.T


def any_shards(hidden, targets, group_lengths, dest_ids, input_gain, latent_gain, kv_weight):
    rows, feat = hidden.shape
    width = kv_weight.shape[1]
    roll_count = lax.axis_size("roll")
    model_width = feat * lax.axis_size("tp")
    wide = hidden.astype(F32)
    scale = lax.rsqrt(lax.psum(jnp.sum(wide * wide, axis=1), "tp") / model_width + EPS)
    normed = (wide * scale[:, None] * input_gain).astype(BF16)
    latent = lax.psum(jnp.dot(normed, kv_weight, preferred_element_type=F32), "tp")
    weights = row_weights(group_lengths[0], rows)
    row_terms, d_latent = head(latent.T, targets.T, weights, latent_gain, group_lengths.shape[1])
    grad = lax.dot_general(
        d_latent.astype(BF16), normed, (((1,), (0,)), ((), ())), preferred_element_type=F32
    )
    grad = lax.psum(grad.astype(BF16), "roll").astype(F32)
    dest = dest_ids[:, 0]
    named = dest[None, :] == lax.iota(jnp.int32, roll_count)[:, None]
    losses = lax.psum(jnp.sum(jnp.where(named, row_terms[None, :], 0.0), axis=1), "roll")
    power = lax.psum(jnp.sum(grad * grad), "tp")
    updated = kv_weight.T.astype(F32) - RATE * grad * lax.rsqrt(power / (model_width * width) + EPS)
    peak = lax.pmax(jnp.max(jnp.abs(updated), axis=1), "tp") + EPS
    codes = (updated / peak[:, None]).astype(BF16)
    loss = lax.dynamic_slice(losses, (lax.axis_index("roll"),), (1,))
    return loss, codes.T


def solution(mesh):
    in_specs = (
        P("roll", "tp"),
        P("roll", None),
        P("roll", None),
        P("roll", None),
        P("tp"),
        P(),
        P("tp", None),
    )
    out_specs = (P("roll"), P("tp", None))
    paired = mesh.shape["roll"] == 16 and mesh.shape["tp"] == 2
    body = paired_shards if paired else any_shards
    return jax.shard_map(body, mesh=mesh, in_specs=in_specs, out_specs=out_specs, check_vma=False)
```

time: 211 us -> 164 us (0.78)
  other arithmetic: 28.7 us -> 7.88 us
  matrix products: 15.6 us -> 0 us
  Pallas kernels: 44.1 us -> 30.9 us
  starting transfers between devices: 33.7 us -> 41.4 us
  waiting for transfers between devices: 71.4 us -> 67.1 us
    dot_general x3 -> x0, matrix products: 15.6 us -> none  [the longest x1 6.93 us: paired_shards(): lax.dot_general(gained, hidden, (((1,), (1,)), ((), ())), preferred_eleme...]
    pallas_call x4 -> x12, Pallas kernels: 44.1 us -> 30.9 us  [the longest x6 11.8 us: code_piece(): pl.pallas_call(code_kernel, grid_spec=pltpu.PrefetchScalarGridSpec(num_sc...]
    ppermute x20 -> x32, starting transfers between devices: 33.1 us -> 40.9 us  [exchange(): return lax.ppermute(value, ('roll', 'tp'), pairs)]
    unnamed x31 -> x18, local copies, waits for them, and re-layouts: 3.33 us -> 10.6 us
    ppermute x20 -> x32, waiting for transfers between devices: 69.9 us -> 63 us  [exchange(): return lax.ppermute(value, ('roll', 'tp'), pairs)]
    reduce_sum x9 -> x3, other arithmetic: 6.87 us -> 1.95 us  [paired_shards(): jnp.sum(jnp.square(v.astype(F32) * g))]
    broadcast_in_dim x6 -> x5, local copies, waits for them, and re-layouts: 5.57 us -> 1.09 us  [the longest x1 0.73 us: paired_shards(): gain_row = input_gain[None, :]]
    concatenate x7 -> x9, other arithmetic: 6.48 us -> 2.91 us  [paired_shards(): jnp.concatenate([value, exchange(value, SCATTER[chain][axis])], axis=axis)]
  transfers between devices with their start and end apart: 24 -> 35, of which waited for: 12 -> 24; matrix products, arithmetic and copies ran while one was open for 19% -> 4% of each run, Pallas kernels for 5% -> 10%
where the time goes in v2:
time: 164 us
  waiting for transfers between devices  67.1 us (41%)
  starting transfers between devices  41.4 us (25%)
  Pallas kernels  30.9 us (19%)
  local copies, waits for them, and re-layouts  12.6 us (8%)
  other arithmetic  7.88 us (5%)
  between operations  3.62 us (2%)
    ppermute x32, waiting for transfers between devices, exchange(): return lax.ppermute(value, ('roll', 'tp'), pairs)  63 us
    ppermute x32, starting transfers between devices, exchange(): return lax.ppermute(value, ('roll', 'tp'), pairs)  40.9 us
    pallas_call x6, Pallas kernels, code_piece(): pl.pallas_call(code_kernel, grid_spec=pltpu.PrefetchScalarGridSpec(num_sc...  11.8 us
    unnamed x18, local copies, waits for them, and re-layouts  10.6 us
    pallas_call x4, Pallas kernels, grad_half(): pl.pallas_call(functools.partial(grad_kernel, first, count), grid_spec=pl...  8.36 us
    pallas_call x1, Pallas kernels, forward(): pl.pallas_call(forward_kernel, grid=(feat // cols,), in_specs=[pl.BlockSp...  8.24 us
    ppermute x3, waiting for transfers between devices, swap_cores(): return lax.ppermute(value, 'tp', [(0, 1), (1, 0)])  4.11 us
  transfers between devices with their start and end apart: 35, of which 24 were waited for; matrix products, arithmetic and copies ran while one was open for 4% of the time, Pallas kernels for 10%

profile of v2, /device:TPU:0, one launch (start us, length us, event | category | flops | bytes accessed | tf_op | source)
XLA Modules:
  0.0 163.5 jit_solution(7574016087154328516)
XLA Ops:
  1.4 2.2 %copy-done = bf16[3584,576]{0,1:T(8,128)(2,1)S(1)} copy-done((bf16[3584,576]{0,1:T(8,128)(2,1)S(1)}, bf16[3584,576]{0,1:T(8,128)(2,1)}, u32[]{:S(2)}) %copy-start) | copy-done | bytes 4128792
  3.5 2.6 %copy-done.2 = bf16[768,3584]{1,0:T(8,128)(2,1)S(1)} copy-done((bf16[768,3584]{1,0:T(8,128)(2,1)S(1)}, bf16[768,3584]{1,0:T(8,128)(2,1)}, u32[]{:S(2)}) %copy-start.2) | copy-done | bytes 5505048
  6.1 8.2 %shard_map.86 = (f32[576,768]{1,0:T(8,128)S(1)}, bf16[592,768]{1,0:T(8,128)(2,1)}, f32[8,768]{1,0:T(8,128)S(1)}) custom-call(bf16[768,3584]{1,0:T(8,128)(2,1)S(1)} %copy-done.2, bf16[576,3584]{1,0:T(8,128)(2,1)S(1)} %bitcast.139, f32[1,3584]{1,0:T(1,128)S(1)} %broadcast_in_dim.29.gain_ref), custom_call_target="tpu_custom_call" | custom-call | flops 3170893824 | bytes 10000000 | tf_op jit(solution)/shard_map/pallas_call | solution.py:111
  15.2 1.8 %collective-permute-done.got_ref = bf16[592,768]{1,0:T(8,128)(2,1)S(1)} collective-permute-done((bf16[592,768]{1,0:T(8,128)(2,1)}, bf16[592,768]{1,0:T(8,128)(2,1)S(1)}, u32[]{:S(2)}, u32[]{:S(2)}) %collective-permute-start) | collective-permute-done | bytes 909344 | tf_op jit(solution)/shard_map/ppermute | solution.py:39
  17.1 1.2 copy-done.4
  18.3 2.5 %shard_map.87 = (bf16[12,48,768]{2,1,0:T(8,128)(2,1)S(1)}, f32[16,128]{1,0:T(8,128)S(1)}) custom-call(s32[3]{0:T(128)S(1)} %add_add_fusion.masks_ref, s32[8]{0:T(128)S(1)} %bitcast.156, f32[576,768]{1,0:T(8,128)S(1)} %get-tuple-element.11.part_ref, bf16[592,768]{1,0:T(8,128)(2,1)S(1)} %collective-permute-done.got_ref, ...), custom_call_target="tpu_custom_call" | custom-call | flops 8847360 | bytes 4000000 | tf_op jit(solution)/shard_map/pallas_call | solution.py:193
  20.8 2.6 %copy-done.3 = bf16[768,3584]{1,0:T(8,128)(2,1)S(1)} copy-done((bf16[768,3584]{1,0:T(8,128)(2,1)S(1)}, bf16[768,3584]{1,0:T(8,128)(2,1)}, u32[]{:S(2)}) %copy-start.3) | copy-done | bytes 5505048
  23.3 1.8 %shard_map.91 = bf16[2,4,48,896]{3,2,1,0:T(8,128)(2,1)S(1)} custom-call(s32[2]{0:T(128)S(1)} %pad_add_fusion.2.where_ref, bf16[12,48,768]{2,1,0:T(8,128)(2,1)S(1)} %get-tuple-element.15.d_ref, bf16[768,3584]{1,0:T(8,128)(2,1)S(1)} %copy-done.3), custom_call_target="tpu_custom_call" | custom-call | flops 528482304 | bytes 2752512 | tf_op jit(solution)/shard_map/pallas_call | solution.py:233
  25.1 3.0 %collective-permute-start.9 = (bf16[2,2,2,48,896]{4,3,2,1,0:T(8,128)(2,1)S(1)}, bf16[2,2,2,48,896]{4,3,2,1,0:T(8,128)(2,1)S(1)}, u32[]{:S(2)}, u32[]{:S(2)}) collective-permute-start(bf16[2,2,2,48,896]{4,3,2,1,0:T(8,128)(2,1)S(1)} %bitcast.151), channel_id=1, source_target_pairs={{0,8},{1,9},{2,10},{3,11},{4,12},{5,13},{6,14},{7,15},{8,0},{9,1},... | collective-permute-start | bytes 2064392 | tf_op jit(solution)/shard_map/ppermute | solution.py:35
  28.3 2.4 %shard_map.89 = (bf16[2,4,48,896]{3,2,1,0:T(8,128)(2,1)S(1)}, bf16[2,4,48,896]{3,2,1,0:T(8,128)(2,1)S(1)}) custom-call(s32[3]{0:T(128)S(1)} %add_add_fusion.2.where_ref, bf16[12,48,768]{2,1,0:T(8,128)(2,1)S(1)} %get-tuple-element.15.d_ref, bf16[768,3584]{1,0:T(8,128)(2,1)S(1)} %copy-done.3), custom_call_target="tpu_custom_call" | custom-call | flops 1056964608 | bytes 2752512 | tf_op jit(solution)/shard_map/pallas_call | solution.py:233
  30.7 1.6 collective-permute-start.5
  32.8 1.8 %shard_map.90 = bf16[2,4,48,896]{3,2,1,0:T(8,128)(2,1)S(1)} custom-call(s32[2]{0:T(128)S(1)} %pad_add_fusion.1.where_ref, bf16[12,48,768]{2,1,0:T(8,128)(2,1)S(1)} %get-tuple-element.15.d_ref, bf16[768,3584]{1,0:T(8,128)(2,1)S(1)} %copy-done.3), custom_call_target="tpu_custom_call" | custom-call | flops 528482304 | bytes 2752512 | tf_op jit(solution)/shard_map/pallas_call | solution.py:233
  34.6 2.4 %shard_map.88 = (bf16[2,4,48,896]{3,2,1,0:T(8,128)(2,1)S(1)}, bf16[2,4,48,896]{3,2,1,0:T(8,128)(2,1)S(1)}) custom-call(s32[3]{0:T(128)S(1)} %add_add_fusion.1.where_ref, bf16[12,48,768]{2,1,0:T(8,128)(2,1)S(1)} %get-tuple-element.15.d_ref, bf16[768,3584]{1,0:T(8,128)(2,1)S(1)} %copy-done.3), custom_call_target="tpu_custom_call" | custom-call | flops 1056964608 | bytes 2752512 | tf_op jit(solution)/shard_map/pallas_call | solution.py:233
  37.0 6.9 %collective-permute-done.9 = bf16[2,2,2,48,896]{4,3,2,1,0:T(8,128)(2,1)S(1)} collective-permute-done((bf16[2,2,2,48,896]{4,3,2,1,0:T(8,128)(2,1)S(1)}, bf16[2,2,2,48,896]{4,3,2,1,0:T(8,128)(2,1)S(1)}, u32[]{:S(2)}, u32[]{:S(2)}) %collective-permute-start.9) | collective-permute-done | bytes 688160 | tf_op jit(solution)/shard_map/ppermute | solution.py:35
  44.1 1.7 %collective-permute-start.10 = (bf16[2,2,48,896]{3,2,1,0:T(8,128)(2,1)S(1)}, bf16[2,2,48,896]{3,2,1,0:T(8,128)(2,1)S(1)}, u32[]{:S(2)}, u32[]{:S(2)}) collective-permute-start(bf16[2,2,48,896]{3,2,1,0:T(8,128)(2,1)S(1)} %slice_bitcast_fusion), channel_id=1, source_target_pairs={{0,2},{1,5},{2,0},{3,7},{4,6},{5,1},{6,4},{7,3},{8,10},{9,13},{10,... | collective-permute-start | bytes 1032200 | tf_op jit(solution)/shard_map/ppermute | solution.py:35
  46.0 1.6 collective-permute-start.6
  47.7 1.4 collective-permute-done.1
  49.3 1.6 collective-permute-start.2
  50.9 3.7 %collective-permute-done.10 = bf16[2,2,48,896]{3,2,1,0:T(8,128)(2,1)S(1)} collective-permute-done((bf16[2,2,48,896]{3,2,1,0:T(8,128)(2,1)S(1)}, bf16[2,2,48,896]{3,2,1,0:T(8,128)(2,1)S(1)}, u32[]{:S(2)}, u32[]{:S(2)}) %collective-permute-start.10) | collective-permute-done | bytes 344096 | tf_op jit(solution)/shard_map/ppermute | solution.py:35
  54.7 1.6 collective-permute-start.11
  57.0 2.6 %collective-permute-start.3 = (bf16[2,48,896]{2,1,0:T(8,128)(2,1)S(1)}, bf16[2,48,896]{2,1,0:T(8,128)(2,1)S(1)}, u32[]{:S(2)}, u32[]{:S(2)}) collective-permute-start(bf16[2,48,896]{2,1,0:T(8,128)(2,1)S(1)} %slice_bitcast_fusion.10), channel_id=1, source_target_pairs={{0,16},{1,17},{2,18},{3,19},{4,20},{5,21},{6,22},{7,23},{8,24},{9,... | collective-permute-start | bytes 516104 | tf_op jit(solution)/shard_map/ppermute | solution.py:35
  60.2 2.6 %collective-permute-start.12 = (bf16[48,896]{1,0:T(8,128)(2,1)S(1)}, bf16[48,896]{1,0:T(8,128)(2,1)S(1)}, u32[]{:S(2)}, u32[]{:S(2)}) collective-permute-start(bf16[48,896]{1,0:T(8,128)(2,1)S(1)} %slice_bitcast_fusion.12), channel_id=1, source_target_pairs={{0,16},{1,17},{2,18},{3,19},{4,20},{5,21},{6,22},{7,23},{8,24},{9,... | collective-permute-start | bytes 258056 | tf_op jit(solution)/shard_map/ppermute | solution.py:35
  62.9 1.8 %collective-permute-start.8 = (bf16[48,896]{1,0:T(8,128)(2,1)S(1)}, bf16[48,896]{1,0:T(8,128)(2,1)S(1)}, u32[]{:S(2)}, u32[]{:S(2)}) collective-permute-start(bf16[48,896]{1,0:T(8,128)(2,1)S(1)} %slice_bitcast_fusion.14), channel_id=1, source_target_pairs={{0,16},{1,17},{2,18},{3,19},{4,20},{5,21},{6,22},{7,23},{8,24},{9,... | collective-permute-start | bytes 258056 | tf_op jit(solution)/shard_map/ppermute | solution.py:35
  64.7 6.8 %collective-permute-done.3 = bf16[2,48,896]{2,1,0:T(8,128)(2,1)S(1)} collective-permute-done((bf16[2,48,896]{2,1,0:T(8,128)(2,1)S(1)}, bf16[2,48,896]{2,1,0:T(8,128)(2,1)S(1)}, u32[]{:S(2)}, u32[]{:S(2)}) %collective-permute-start.3) | collective-permute-done | bytes 172064 | tf_op jit(solution)/shard_map/ppermute | solution.py:35
  72.2 2.9 %collective-permute-done.8 = bf16[48,896]{1,0:T(8,128)(2,1)S(1)} collective-permute-done((bf16[48,896]{1,0:T(8,128)(2,1)S(1)}, bf16[48,896]{1,0:T(8,128)(2,1)S(1)}, u32[]{:S(2)}, u32[]{:S(2)}) %collective-permute-start.8) | collective-permute-done | bytes 86048 | tf_op jit(solution)/shard_map/ppermute | solution.py:35
  75.8 1.1 collective-permute-done.4
  80.1 1.4 collective-permute-start.13
  81.6 2.3 %collective-permute-done.13 = f32[24,128]{1,0:T(8,128)S(1)} collective-permute-done((f32[24,128]{1,0:T(8,128)S(1)}, f32[24,128]{1,0:T(8,128)S(1)}, u32[]{:S(2)}, u32[]{:S(2)}) %collective-permute-start.13) | collective-permute-done | bytes 12320 | tf_op jit(solution)/shard_map/ppermute | solution.py:35
  83.9 1.4 collective-permute-start.14
  85.3 2.3 %collective-permute-done.14 = f32[24,128]{1,0:T(8,128)S(1)} collective-permute-done((f32[24,128]{1,0:T(8,128)S(1)}, f32[24,128]{1,0:T(8,128)S(1)}, u32[]{:S(2)}, u32[]{:S(2)}) %collective-permute-start.14) | collective-permute-done | bytes 12320 | tf_op jit(solution)/shard_map/ppermute | solution.py:35
  87.6 3.7 %collective-permute-done.15 = f32[24,128]{1,0:T(8,128)S(1)} collective-permute-done((f32[24,128]{1,0:T(8,128)S(1)}, f32[24,128]{1,0:T(8,128)S(1)}, u32[]{:S(2)}, u32[]{:S(2)}) %collective-permute-start.15) | collective-permute-done | bytes 12320 | tf_op jit(solution)/shard_map/ppermute | solution.py:35
  91.3 1.2 collective-permute-start.16
  92.5 3.4 %collective-permute-done.16 = f32[24,128]{1,0:T(8,128)S(1)} collective-permute-done((f32[24,128]{1,0:T(8,128)S(1)}, f32[24,128]{1,0:T(8,128)S(1)}, u32[]{:S(2)}, u32[]{:S(2)}) %collective-permute-start.16) | collective-permute-done | bytes 12320 | tf_op jit(solution)/shard_map/ppermute | solution.py:35
  95.9 1.2 collective-permute-done.17
  98.3 1.3 fusion.23
  99.6 1.3 collective-permute-start.31
  100.9 1.7 %collective-permute-start.27 = (bf16[1,1,1,1,48,896]{5,4,3,2,1,0:T(8,128)(2,1)S(1)}, bf16[1,1,1,1,48,896]{5,4,3,2,1,0:T(8,128)(2,1)S(1)}, u32[]{:S(2)}, u32[]{:S(2)}) collective-permute-start(bf16[1,1,1,1,48,896]{5,4,3,2,1,0:T(8,128)(2,1)S(1)} %get-tuple-element.24), channel_id=1, source_target_pairs={{0,16},{1,17},{2,18},{3,19},{4,20},{5,21},{6,22},{7,23},{8,24},{9,... | collective-permute-start | bytes 258056 | tf_op jit(solution)/shard_map/ppermute | solution.py:35
  103.0 6.0 %collective-permute-done.31 = bf16[1,1,1,1,48,896]{5,4,3,2,1,0:T(8,128)(2,1)S(1)} collective-permute-done((bf16[1,1,1,1,48,896]{5,4,3,2,1,0:T(8,128)(2,1)S(1)}, bf16[1,1,1,1,48,896]{5,4,3,2,1,0:T(8,128)(2,1)S(1)}, u32[]{:S(2)}, u32[]{:S(2)}) %collective-permute-start.31) | collective-permute-done | bytes 86048 | tf_op jit(solution)/shard_map/ppermute | solution.py:35
  109.0 1.6 collective-permute-start.32
  110.7 1.5 collective-permute-start.28
  112.3 2.2 %collective-permute-done.32 = bf16[1,1,1,2,48,896]{5,4,3,2,1,0:T(8,128)(2,1)S(1)} collective-permute-done((bf16[1,1,1,2,48,896]{5,4,3,2,1,0:T(8,128)(2,1)S(1)}, bf16[1,1,1,2,48,896]{5,4,3,2,1,0:T(8,128)(2,1)S(1)}, u32[]{:S(2)}, u32[]{:S(2)}) %collective-permute-start.32) | collective-permute-done | bytes 172064 | tf_op jit(solution)/shard_map/ppermute | solution.py:35
  114.5 0.9 collective-permute-start.33
  115.4 0.9 collective-permute-done.28
  116.3 0.8 pad_maximum_fusion.4
  117.1 1.5 collective-permute-start.29
  118.6 4.1 %collective-permute-done.19 = bf16[1,1,1,2,48,896]{5,4,3,2,1,0:T(8,128)(2,1)S(1)} collective-permute-done((bf16[1,1,1,2,48,896]{5,4,3,2,1,0:T(8,128)(2,1)S(1)}, bf16[1,1,1,2,48,896]{5,4,3,2,1,0:T(8,128)(2,1)S(1)}, u32[]{:S(2)}, u32[]{:S(2)}) %collective-permute-start.19) | collective-permute-done | bytes 172064 | tf_op jit(solution)/shard_map/ppermute | solution.py:35
  123.5 1.4 collective-permute-start.20
  125.8 1.4 collective-permute-done.33
  127.2 1.2 collective-permute-start.34
  128.6 5.4 %collective-permute-done.20 = bf16[1,1,2,2,48,896]{5,4,3,2,1,0:T(8,128)(2,1)} collective-permute-done((bf16[1,1,2,2,48,896]{5,4,3,2,1,0:T(8,128)(2,1)}, bf16[1,1,2,2,48,896]{5,4,3,2,1,0:T(8,128)(2,1)}, u32[]{:S(2)}, u32[]{:S(2)}) %collective-permute-start.20) | collective-permute-done | bytes 344096 | tf_op jit(solution)/shard_map/ppermute | solution.py:35
  134.0 1.1 pad_maximum_fusion
  135.2 2.1 %collective-permute-start.23 = (f32[3,4,48]{2,1,0:T(4,128)S(1)}, f32[3,4,48]{2,1,0:T(4,128)S(1)}, u32[]{:S(2)}, u32[]{:S(2)}) collective-permute-start(f32[3,4,48]{2,1,0:T(4,128)S(1)} %max.15), channel_id=1, source_target_pairs={{0,4},{1,3},{2,6},{3,1},{4,0},{5,7},{6,2},{7,5},{8,12},{9,11},{10,... | collective-permute-start | bytes 6920 | tf_op jit(solution)/shard_map/ppermute | solution.py:35
  137.4 1.7 %collective-permute-done.23 = f32[3,4,48]{2,1,0:T(4,128)S(1)} collective-permute-done((f32[3,4,48]{2,1,0:T(4,128)S(1)}, f32[3,4,48]{2,1,0:T(4,128)S(1)}, u32[]{:S(2)}, u32[]{:S(2)}) %collective-permute-start.23) | collective-permute-done | bytes 2336 | tf_op jit(solution)/shard_map/ppermute | solution.py:35
  139.2 4.4 %collective-permute-done.24 = f32[3,4,48]{2,1,0:T(4,128)S(1)} collective-permute-done((f32[3,4,48]{2,1,0:T(4,128)S(1)}, f32[3,4,48]{2,1,0:T(4,128)S(1)}, u32[]{:S(2)}, u32[]{:S(2)}) %collective-permute-start.24) | collective-permute-done | bytes 2336 | tf_op jit(solution)/shard_map/ppermute | solution.py:35
  143.6 2.5 %collective-permute-start.25 = (f32[3,4,48]{2,1,0:T(4,128)S(1)}, f32[3,4,48]{2,1,0:T(4,128)S(1)}, u32[]{:S(2)}, u32[]{:S(2)}) collective-permute-start(f32[3,4,48]{2,1,0:T(4,128)S(1)} %max.17), channel_id=1, source_target_pairs={{0,16},{1,17},{2,18},{3,19},{4,20},{5,21},{6,22},{7,23},{8,24},{9,... | collective-permute-start | bytes 6920 | tf_op jit(solution)/shard_map/ppermute | solution.py:35
  146.2 1.9 %collective-permute-done.25 = f32[3,4,48]{2,1,0:T(4,128)S(1)} collective-permute-done((f32[3,4,48]{2,1,0:T(4,128)S(1)}, f32[3,4,48]{2,1,0:T(4,128)S(1)}, u32[]{:S(2)}, u32[]{:S(2)}) %collective-permute-start.25) | collective-permute-done | bytes 2336 | tf_op jit(solution)/shard_map/ppermute | solution.py:35
  148.2 1.1 collective-permute-done.26
  149.5 2.2 %copy-done.1 = bf16[3584,576]{0,1:T(8,128)(2,1)S(1)} copy-done((bf16[3584,576]{0,1:T(8,128)(2,1)S(1)}, bf16[3584,576]{0,1:T(8,128)(2,1)}, u32[]{:S(2)}) %copy-start.1) | copy-done | bytes 4128792
  151.7 1.7 %shard_map.92.rest_0_ = bf16[576,3584]{1,0:T(8,128)(2,1)} custom-call(s32[3]{0:T(128)S(1)} %add_add_fusion.8.where_ref, f32[1]{0:T(128)} %bitcast.39.coef_ref, bf16[2,4,48,896]{3,2,1,0:T(8,128)(2,1)S(1)} %bitcast.147, bf16[576,3584]{1,0:T(8,128)(2,1)S(1)} %bitcast.140, f32[1,3584]{1,0:T(1,128)S(1)} %broadcast_in_dim.29.gain_ref, ...), custom_call_target="tpu_custom_call" | custom-call | flops 688128 | bytes 2064384 | tf_op jit(solution)/shard_map/pallas_call | solution.py:270
  153.4 1.7 %shard_map.93.rest_0_ = bf16[576,3584]{1,0:T(8,128)(2,1)} custom-call(s32[3]{0:T(128)S(1)} %add_add_fusion.7.where_ref, f32[1]{0:T(128)} %bitcast.39.coef_ref, bf16[2,4,48,896]{3,2,1,0:T(8,128)(2,1)S(1)} %bitcast.148, bf16[576,3584]{1,0:T(8,128)(2,1)S(1)} %bitcast.141, f32[1,3584]{1,0:T(1,128)S(1)} %broadcast_in_dim.29.gain_ref, ...), custom_call_target="tpu_custom_call", output_to_operand_aliasing={{}: (6, {})} | custom-call | flops 688128 | bytes 2064384 | tf_op jit(solution)/shard_map/pallas_call | solution.py:270
  155.0 1.7 %shard_map.94.rest_0_ = bf16[576,3584]{1,0:T(8,128)(2,1)} custom-call(s32[3]{0:T(128)S(1)} %add_add_fusion.6.where_ref, f32[1]{0:T(128)} %bitcast.39.coef_ref, bf16[2,4,48,896]{3,2,1,0:T(8,128)(2,1)S(1)} %bitcast.149, bf16[576,3584]{1,0:T(8,128)(2,1)S(1)} %bitcast.142, f32[1,3584]{1,0:T(1,128)S(1)} %broadcast_in_dim.29.gain_ref, ...), custom_call_target="tpu_custom_call", output_to_operand_aliasing={{}: (6, {})} | custom-call | flops 688128 | bytes 2064384 | tf_op jit(solution)/shard_map/pallas_call | solution.py:270
  156.7 1.7 %shard_map.95.rest_0_ = bf16[576,3584]{1,0:T(8,128)(2,1)} custom-call(s32[3]{0:T(128)S(1)} %add_add_fusion.5.where_ref, f32[1]{0:T(128)} %bitcast.39.coef_ref, bf16[2,4,48,896]{3,2,1,0:T(8,128)(2,1)S(1)} %bitcast.154, bf16[576,3584]{1,0:T(8,128)(2,1)S(1)} %bitcast.143, f32[1,3584]{1,0:T(1,128)S(1)} %broadcast_in_dim.29.gain_ref, ...), custom_call_target="tpu_custom_call", output_to_operand_aliasing={{}: (6, {})} | custom-call | flops 688128 | bytes 2064384 | tf_op jit(solution)/shard_map/pallas_call | solution.py:270
  158.4 2.6 %shard_map.96.rest_0_ = bf16[576,3584]{1,0:T(8,128)(2,1)} custom-call(s32[3]{0:T(128)S(1)} %add_add_fusion.4.where_ref, f32[1]{0:T(128)} %bitcast.39.coef_ref, bf16[2,4,48,896]{3,2,1,0:T(8,128)(2,1)} %bitcast.52.g_ref, bf16[576,3584]{1,0:T(8,128)(2,1)S(1)} %bitcast.144, f32[1,3584]{1,0:T(1,128)S(1)} %broadcast_in_dim.29.gain_ref, ...), custom_call_target="tpu_custom_call", output_to_operand_aliasing={{}: (6, {})} | custom-call | flops 688128 | bytes 2064384 | tf_op jit(solution)/shard_map/pallas_call | solution.py:270
  160.9 2.6 %shard_map.97 = bf16[576,3584]{1,0:T(8,128)(2,1)} custom-call(s32[3]{0:T(128)S(1)} %add_add_fusion.3.where_ref, f32[1]{0:T(128)} %bitcast.39.coef_ref, bf16[2,4,48,896]{3,2,1,0:T(8,128)(2,1)} %bitcast.41.g_ref, bf16[576,3584]{1,0:T(8,128)(2,1)S(1)} %bitcast.145, f32[1,3584]{1,0:T(1,128)S(1)} %broadcast_in_dim.29.gain_ref, ...), custom_call_target="tpu_custom_call", output_to_operand_aliasing={{}: (6, {})} | custom-call | flops 688128 | bytes 2064384 | tf_op jit(solution)/shard_map/pallas_call | solution.py:270
  (102 shorter events, 10.8 us)
Async XLA Ops:
  1.4 2.2 %copy-start = (bf16[3584,576]{0,1:T(8,128)(2,1)S(1)}, bf16[3584,576]{0,1:T(8,128)(2,1)}, u32[]{:S(2)}) copy-start(bf16[3584,576]{0,1:T(8,128)(2,1)} %param.13) | copy-start | bytes 12386308
  3.5 2.6 %copy-start.2 = (bf16[768,3584]{1,0:T(8,128)(2,1)S(1)}, bf16[768,3584]{1,0:T(8,128)(2,1)}, u32[]{:S(2)}) copy-start(bf16[768,3584]{1,0:T(8,128)(2,1)} %x_ref.9) | copy-start | bytes 16515076
  6.1 8.7 %copy-start.8 = (f32[512]{0:T(512)S(1)}, f32[512]{0:T(512)}, u32[]{:S(2)}) copy-start(f32[512]{0:T(512)} %param.12) | copy-start | bytes 6148
  6.1 11.0 %copy-start.5 = (s32[768,1]{0,1:T(1,128)S(1)}, s32[768,1]{0,1:T(1,128)}, u32[]{:S(2)}) copy-start(s32[768,1]{0,1:T(1,128)} %param.10) | copy-start | bytes 9220
  6.1 11.0 %copy-start.6 = (s32[1,8]{1,0:T(1,128)S(1)}, s32[1,8]{1,0:T(1,128)}, u32[]{:S(2)}) copy-start(s32[1,8]{1,0:T(1,128)} %param.9) | copy-start | bytes 100
  14.3 2.7 %collective-permute-start = (bf16[592,768]{1,0:T(8,128)(2,1)}, bf16[592,768]{1,0:T(8,128)(2,1)S(1)}, u32[]{:S(2)}, u32[]{:S(2)}) collective-permute-start(bf16[592,768]{1,0:T(8,128)(2,1)} %get-tuple-element.12), channel_id=1, source_target_pairs={{0,1},{1,0},{2,3},{3,2},{4,5},{5,4},{6,7},{7,6},{8,9},{9,8},{10,11... | collective-permute-start | bytes 2727944 | tf_op jit(solution)/shard_map/ppermute | solution.py:39
  17.1 1.2 copy-start.4
  20.8 2.6 %copy-start.3 = (bf16[768,3584]{1,0:T(8,128)(2,1)S(1)}, bf16[768,3584]{1,0:T(8,128)(2,1)}, u32[]{:S(2)}) copy-start(bf16[768,3584]{1,0:T(8,128)(2,1)} %x_ref.9) | copy-start | bytes 16515076
  23.3 4.9 %copy-start.7 = (f32[3584]{0:T(1024)S(1)}, f32[3584]{0:T(1024)}, u32[]{:S(2)}) copy-start(f32[3584]{0:T(1024)} %param.11) | copy-start | bytes 43012
  25.1 18.7 %collective-permute-start.9 = (bf16[2,2,2,48,896]{4,3,2,1,0:T(8,128)(2,1)S(1)}, bf16[2,2,2,48,896]{4,3,2,1,0:T(8,128)(2,1)S(1)}, u32[]{:S(2)}, u32[]{:S(2)}) collective-permute-start(bf16[2,2,2,48,896]{4,3,2,1,0:T(8,128)(2,1)S(1)} %bitcast.151), channel_id=1, source_target_pairs={{0,8},{1,9},{2,10},{3,11},{4,12},{5,13},{6,14},{7,15},{8,0},{9,1},... | collective-permute-start | bytes 2064392 | tf_op jit(solution)/shard_map/ppermute | solution.py:35
  30.7 15.1 %collective-permute-start.5 = (bf16[2,2,2,48,896]{4,3,2,1,0:T(8,128)(2,1)S(1)}, bf16[2,2,2,48,896]{4,3,2,1,0:T(8,128)(2,1)S(1)}, u32[]{:S(2)}, u32[]{:S(2)}) collective-permute-start(bf16[2,2,2,48,896]{4,3,2,1,0:T(8,128)(2,1)S(1)} %bitcast.158), channel_id=1, source_target_pairs={{0,2},{1,5},{2,0},{3,7},{4,6},{5,1},{6,4},{7,3},{8,10},{9,13},{10,... | collective-permute-start | bytes 2064392 | tf_op jit(solution)/shard_map/ppermute | solution.py:35
  32.3 16.8 %collective-permute-start.1 = (bf16[2,2,2,48,896]{4,3,2,1,0:T(8,128)(2,1)S(1)}, bf16[2,2,2,48,896]{4,3,2,1,0:T(8,128)(2,1)S(1)}, u32[]{:S(2)}, u32[]{:S(2)}) collective-permute-start(bf16[2,2,2,48,896]{4,3,2,1,0:T(8,128)(2,1)S(1)} %bitcast.157), channel_id=1, source_target_pairs={{0,2},{1,5},{2,0},{3,7},{4,6},{5,1},{6,4},{7,3},{8,10},{9,13},{10,... | collective-permute-start | bytes 2064392 | tf_op jit(solution)/shard_map/ppermute | solution.py:35
  44.1 10.5 %collective-permute-start.10 = (bf16[2,2,48,896]{3,2,1,0:T(8,128)(2,1)S(1)}, bf16[2,2,48,896]{3,2,1,0:T(8,128)(2,1)S(1)}, u32[]{:S(2)}, u32[]{:S(2)}) collective-permute-start(bf16[2,2,48,896]{3,2,1,0:T(8,128)(2,1)S(1)} %slice_bitcast_fusion), channel_id=1, source_target_pairs={{0,2},{1,5},{2,0},{3,7},{4,6},{5,1},{6,4},{7,3},{8,10},{9,13},{10,... | collective-permute-start | bytes 1032200 | tf_op jit(solution)/shard_map/ppermute | solution.py:35
  46.0 10.2 %collective-permute-start.6 = (bf16[2,2,48,896]{3,2,1,0:T(8,128)(2,1)S(1)}, bf16[2,2,48,896]{3,2,1,0:T(8,128)(2,1)S(1)}, u32[]{:S(2)}, u32[]{:S(2)}) collective-permute-start(bf16[2,2,48,896]{3,2,1,0:T(8,128)(2,1)S(1)} %slice_bitcast_fusion.2), channel_id=1, source_target_pairs={{0,8},{1,9},{2,10},{3,11},{4,12},{5,13},{6,14},{7,15},{8,0},{9,1},... | collective-permute-start | bytes 1032200 | tf_op jit(solution)/shard_map/ppermute | solution.py:35
  49.3 7.6 %collective-permute-start.2 = (bf16[2,2,48,896]{3,2,1,0:T(8,128)(2,1)S(1)}, bf16[2,2,48,896]{3,2,1,0:T(8,128)(2,1)S(1)}, u32[]{:S(2)}, u32[]{:S(2)}) collective-permute-start(bf16[2,2,48,896]{3,2,1,0:T(8,128)(2,1)S(1)} %slice_bitcast_fusion.4), channel_id=1, source_target_pairs={{0,4},{1,3},{2,6},{3,1},{4,0},{5,7},{6,2},{7,5},{8,12},{9,11},{10,... | collective-permute-start | bytes 1032200 | tf_op jit(solution)/shard_map/ppermute | solution.py:35
  54.7 5.5 %collective-permute-start.11 = (bf16[2,48,896]{2,1,0:T(8,128)(2,1)S(1)}, bf16[2,48,896]{2,1,0:T(8,128)(2,1)S(1)}, u32[]{:S(2)}, u32[]{:S(2)}) collective-permute-start(bf16[2,48,896]{2,1,0:T(8,128)(2,1)S(1)} %slice_bitcast_fusion.6), channel_id=1, source_target_pairs={{0,4},{1,3},{2,6},{3,1},{4,0},{5,7},{6,2},{7,5},{8,12},{9,11},{10,... | collective-permute-start | bytes 516104 | tf_op jit(solution)/shard_map/ppermute | solution.py:35
  56.3 6.5 %collective-permute-start.7 = (bf16[2,48,896]{2,1,0:T(8,128)(2,1)S(1)}, bf16[2,48,896]{2,1,0:T(8,128)(2,1)S(1)}, u32[]{:S(2)}, u32[]{:S(2)}) collective-permute-start(bf16[2,48,896]{2,1,0:T(8,128)(2,1)S(1)} %slice_bitcast_fusion.8), channel_id=1, source_target_pairs={{0,4},{1,3},{2,6},{3,1},{4,0},{5,7},{6,2},{7,5},{8,12},{9,11},{10,... | collective-permute-start | bytes 516104 | tf_op jit(solution)/shard_map/ppermute | solution.py:35
  57.0 14.5 %collective-permute-start.3 = (bf16[2,48,896]{2,1,0:T(8,128)(2,1)S(1)}, bf16[2,48,896]{2,1,0:T(8,128)(2,1)S(1)}, u32[]{:S(2)}, u32[]{:S(2)}) collective-permute-start(bf16[2,48,896]{2,1,0:T(8,128)(2,1)S(1)} %slice_bitcast_fusion.10), channel_id=1, source_target_pairs={{0,16},{1,17},{2,18},{3,19},{4,20},{5,21},{6,22},{7,23},{8,24},{9,... | collective-permute-start | bytes 516104 | tf_op jit(solution)/shard_map/ppermute | solution.py:35
  60.2 18.6 %collective-permute-start.12 = (bf16[48,896]{1,0:T(8,128)(2,1)S(1)}, bf16[48,896]{1,0:T(8,128)(2,1)S(1)}, u32[]{:S(2)}, u32[]{:S(2)}) collective-permute-start(bf16[48,896]{1,0:T(8,128)(2,1)S(1)} %slice_bitcast_fusion.12), channel_id=1, source_target_pairs={{0,16},{1,17},{2,18},{3,19},{4,20},{5,21},{6,22},{7,23},{8,24},{9,... | collective-permute-start | bytes 258056 | tf_op jit(solution)/shard_map/ppermute | solution.py:35
  62.9 12.2 %collective-permute-start.8 = (bf16[48,896]{1,0:T(8,128)(2,1)S(1)}, bf16[48,896]{1,0:T(8,128)(2,1)S(1)}, u32[]{:S(2)}, u32[]{:S(2)}) collective-permute-start(bf16[48,896]{1,0:T(8,128)(2,1)S(1)} %slice_bitcast_fusion.14), channel_id=1, source_target_pairs={{0,16},{1,17},{2,18},{3,19},{4,20},{5,21},{6,22},{7,23},{8,24},{9,... | collective-permute-start | bytes 258056 | tf_op jit(solution)/shard_map/ppermute | solution.py:35
  71.6 5.3 %collective-permute-start.4 = (bf16[48,896]{1,0:T(8,128)(2,1)S(1)}, bf16[48,896]{1,0:T(8,128)(2,1)S(1)}, u32[]{:S(2)}, u32[]{:S(2)}) collective-permute-start(bf16[48,896]{1,0:T(8,128)(2,1)S(1)} %slice_bitcast_fusion.16), channel_id=1, source_target_pairs={{0,8},{1,9},{2,10},{3,11},{4,12},{5,13},{6,14},{7,15},{8,0},{9,1},... | collective-permute-start | bytes 258056 | tf_op jit(solution)/shard_map/ppermute | solution.py:35
  80.1 3.8 %collective-permute-start.13 = (f32[24,128]{1,0:T(8,128)S(1)}, f32[24,128]{1,0:T(8,128)S(1)}, u32[]{:S(2)}, u32[]{:S(2)}) collective-permute-start(f32[24,128]{1,0:T(8,128)S(1)} %concatenate.30), channel_id=1, source_target_pairs={{0,2},{1,5},{2,0},{3,7},{4,6},{5,1},{6,4},{7,3},{8,10},{9,13},{10,... | collective-permute-start | bytes 36872 | tf_op jit(solution)/shard_map/ppermute | solution.py:35
  83.9 3.7 %collective-permute-start.14 = (f32[24,128]{1,0:T(8,128)S(1)}, f32[24,128]{1,0:T(8,128)S(1)}, u32[]{:S(2)}, u32[]{:S(2)}) collective-permute-start(f32[24,128]{1,0:T(8,128)S(1)} %pad_add_fusion), channel_id=1, source_target_pairs={{0,4},{1,3},{2,6},{3,1},{4,0},{5,7},{6,2},{7,5},{8,12},{9,11},{10,... | collective-permute-start | bytes 36872 | tf_op jit(solution)/shard_map/ppermute | solution.py:35
  87.6 3.7 %collective-permute-start.15 = (f32[24,128]{1,0:T(8,128)S(1)}, f32[24,128]{1,0:T(8,128)S(1)}, u32[]{:S(2)}, u32[]{:S(2)}) collective-permute-start(f32[24,128]{1,0:T(8,128)S(1)} %add.143), channel_id=1, source_target_pairs={{0,8},{1,9},{2,10},{3,11},{4,12},{5,13},{6,14},{7,15},{8,0},{9,1},... | collective-permute-start | bytes 36872 | tf_op jit(solution)/shard_map/ppermute | solution.py:35
  91.3 4.6 %collective-permute-start.16 = (f32[24,128]{1,0:T(8,128)S(1)}, f32[24,128]{1,0:T(8,128)S(1)}, u32[]{:S(2)}, u32[]{:S(2)}) collective-permute-start(f32[24,128]{1,0:T(8,128)S(1)} %add.144), channel_id=1, source_target_pairs={{0,16},{1,17},{2,18},{3,19},{4,20},{5,21},{6,22},{7,23},{8,24},{9,... | collective-permute-start | bytes 36872 | tf_op jit(solution)/shard_map/ppermute | solution.py:35
  95.9 1.2 collective-permute-start.17
  99.6 9.4 %collective-permute-start.31 = (bf16[1,1,1,1,48,896]{5,4,3,2,1,0:T(8,128)(2,1)S(1)}, bf16[1,1,1,1,48,896]{5,4,3,2,1,0:T(8,128)(2,1)S(1)}, u32[]{:S(2)}, u32[]{:S(2)}) collective-permute-start(bf16[1,1,1,1,48,896]{5,4,3,2,1,0:T(8,128)(2,1)S(1)} %get-tuple-element.23), channel_id=1, source_target_pairs={{0,16},{1,17},{2,18},{3,19},{4,20},{5,21},{6,22},{7,23},{8,24},{9,... | collective-permute-start | bytes 258056 | tf_op jit(solution)/shard_map/ppermute | solution.py:35
  100.9 9.8 %collective-permute-start.27 = (bf16[1,1,1,1,48,896]{5,4,3,2,1,0:T(8,128)(2,1)S(1)}, bf16[1,1,1,1,48,896]{5,4,3,2,1,0:T(8,128)(2,1)S(1)}, u32[]{:S(2)}, u32[]{:S(2)}) collective-permute-start(bf16[1,1,1,1,48,896]{5,4,3,2,1,0:T(8,128)(2,1)S(1)} %get-tuple-element.24), channel_id=1, source_target_pairs={{0,16},{1,17},{2,18},{3,19},{4,20},{5,21},{6,22},{7,23},{8,24},{9,... | collective-permute-start | bytes 258056 | tf_op jit(solution)/shard_map/ppermute | solution.py:35
  102.6 9.6 %collective-permute-start.18 = (bf16[1,1,1,1,48,896]{5,4,3,2,1,0:T(8,128)(2,1)S(1)}, bf16[1,1,1,1,48,896]{5,4,3,2,1,0:T(8,128)(2,1)S(1)}, u32[]{:S(2)}, u32[]{:S(2)}) collective-permute-start(bf16[1,1,1,1,48,896]{5,4,3,2,1,0:T(8,128)(2,1)S(1)} %get-tuple-element.25), channel_id=1, source_target_pairs={{0,8},{1,9},{2,10},{3,11},{4,12},{5,13},{6,14},{7,15},{8,0},{9,1},... | collective-permute-start | bytes 258056 | tf_op jit(solution)/shard_map/ppermute | solution.py:35
  109.0 5.5 %collective-permute-start.32 = (bf16[1,1,1,2,48,896]{5,4,3,2,1,0:T(8,128)(2,1)S(1)}, bf16[1,1,1,2,48,896]{5,4,3,2,1,0:T(8,128)(2,1)S(1)}, u32[]{:S(2)}, u32[]{:S(2)}) collective-permute-start(bf16[1,1,1,2,48,896]{5,4,3,2,1,0:T(8,128)(2,1)S(1)} %pad_maximum_fusion.8), channel_id=1, source_target_pairs={{0,4},{1,3},{2,6},{3,1},{4,0},{5,7},{6,2},{7,5},{8,12},{9,11},{10,... | collective-permute-start | bytes 516104 | tf_op jit(solution)/shard_map/ppermute | solution.py:35
  110.7 5.6 %collective-permute-start.28 = (bf16[1,1,1,2,48,896]{5,4,3,2,1,0:T(8,128)(2,1)S(1)}, bf16[1,1,1,2,48,896]{5,4,3,2,1,0:T(8,128)(2,1)S(1)}, u32[]{:S(2)}, u32[]{:S(2)}) collective-permute-start(bf16[1,1,1,2,48,896]{5,4,3,2,1,0:T(8,128)(2,1)S(1)} %pad_maximum_fusion.7), channel_id=1, source_target_pairs={{0,4},{1,3},{2,6},{3,1},{4,0},{5,7},{6,2},{7,5},{8,12},{9,11},{10,... | collective-permute-start | bytes 516104 | tf_op jit(solution)/shard_map/ppermute | solution.py:35
  112.2 10.5 %collective-permute-start.19 = (bf16[1,1,1,2,48,896]{5,4,3,2,1,0:T(8,128)(2,1)S(1)}, bf16[1,1,1,2,48,896]{5,4,3,2,1,0:T(8,128)(2,1)S(1)}, u32[]{:S(2)}, u32[]{:S(2)}) collective-permute-start(bf16[1,1,1,2,48,896]{5,4,3,2,1,0:T(8,128)(2,1)S(1)} %pad_maximum_fusion.6), channel_id=1, source_target_pairs={{0,16},{1,17},{2,18},{3,19},{4,20},{5,21},{6,22},{7,23},{8,24},{9,... | collective-permute-start | bytes 516104 | tf_op jit(solution)/shard_map/ppermute | solution.py:35
  114.5 12.6 %collective-permute-start.33 = (bf16[1,1,2,2,48,896]{5,4,3,2,1,0:T(8,128)(2,1)S(1)}, bf16[1,1,2,2,48,896]{5,4,3,2,1,0:T(8,128)(2,1)S(1)}, u32[]{:S(2)}, u32[]{:S(2)}) collective-permute-start(bf16[1,1,2,2,48,896]{5,4,3,2,1,0:T(8,128)(2,1)S(1)} %pad_maximum_fusion.5), channel_id=1, source_target_pairs={{0,8},{1,9},{2,10},{3,11},{4,12},{5,13},{6,14},{7,15},{8,0},{9,1},... | collective-permute-start | bytes 1032200 | tf_op jit(solution)/shard_map/ppermute | solution.py:35
  117.1 11.3 %collective-permute-start.29 = (bf16[1,1,2,2,48,896]{5,4,3,2,1,0:T(8,128)(2,1)}, bf16[1,1,2,2,48,896]{5,4,3,2,1,0:T(8,128)(2,1)S(1)}, u32[]{:S(2)}, u32[]{:S(2)}) collective-permute-start(bf16[1,1,2,2,48,896]{5,4,3,2,1,0:T(8,128)(2,1)} %pad_maximum_fusion.4), channel_id=1, source_target_pairs={{0,2},{1,5},{2,0},{3,7},{4,6},{5,1},{6,4},{7,3},{8,10},{9,13},{10,... | collective-permute-start | bytes 1032200 | tf_op jit(solution)/shard_map/ppermute | solution.py:35
  123.5 10.5 %collective-permute-start.20 = (bf16[1,1,2,2,48,896]{5,4,3,2,1,0:T(8,128)(2,1)}, bf16[1,1,2,2,48,896]{5,4,3,2,1,0:T(8,128)(2,1)}, u32[]{:S(2)}, u32[]{:S(2)}) collective-permute-start(bf16[1,1,2,2,48,896]{5,4,3,2,1,0:T(8,128)(2,1)} %pad_maximum_fusion.3), channel_id=1, source_target_pairs={{0,4},{1,3},{2,6},{3,1},{4,0},{5,7},{6,2},{7,5},{8,12},{9,11},{10,... | collective-permute-start | bytes 1032200 | tf_op jit(solution)/shard_map/ppermute | solution.py:35
  125.1 10.1 %collective-permute-start.22 = (f32[3,4,48]{2,1,0:T(4,128)S(1)}, f32[3,4,48]{2,1,0:T(4,128)S(1)}, u32[]{:S(2)}, u32[]{:S(2)}) collective-permute-start(f32[3,4,48]{2,1,0:T(4,128)S(1)} %dynamic_update_slice.11), channel_id=1, source_target_pairs={{0,2},{1,5},{2,0},{3,7},{4,6},{5,1},{6,4},{7,3},{8,10},{9,13},{10,... | collective-permute-start | bytes 6920 | tf_op jit(solution)/shard_map/ppermute | solution.py:35
  127.2 29.4 %collective-permute-start.34 = (bf16[2,1,2,2,48,896]{5,4,3,2,1,0:T(8,128)(2,1)S(1)}, bf16[2,1,2,2,48,896]{5,4,3,2,1,0:T(8,128)(2,1)S(1)}, u32[]{:S(2)}, u32[]{:S(2)}) collective-permute-start(bf16[2,1,2,2,48,896]{5,4,3,2,1,0:T(8,128)(2,1)S(1)} %pad_maximum_fusion.2), channel_id=1, source_target_pairs={{0,2},{1,5},{2,0},{3,7},{4,6},{5,1},{6,4},{7,3},{8,10},{9,13},{10,... | collective-permute-start | bytes 2064392 | tf_op jit(solution)/shard_map/ppermute | solution.py:35
  128.5 29.9 %collective-permute-start.30 = (bf16[2,1,2,2,48,896]{5,4,3,2,1,0:T(8,128)(2,1)S(1)}, bf16[2,1,2,2,48,896]{5,4,3,2,1,0:T(8,128)(2,1)}, u32[]{:S(2)}, u32[]{:S(2)}) collective-permute-start(bf16[2,1,2,2,48,896]{5,4,3,2,1,0:T(8,128)(2,1)S(1)} %pad_maximum_fusion.1), channel_id=1, source_target_pairs={{0,8},{1,9},{2,10},{3,11},{4,12},{5,13},{6,14},{7,15},{8,0},{9,1},... | collective-permute-start | bytes 2064392 | tf_op jit(solution)/shard_map/ppermute | solution.py:35
  135.0 25.9 %collective-permute-start.21 = (bf16[1,2,2,2,48,896]{5,4,3,2,1,0:T(8,128)(2,1)S(1)}, bf16[1,2,2,2,48,896]{5,4,3,2,1,0:T(8,128)(2,1)}, u32[]{:S(2)}, u32[]{:S(2)}) collective-permute-start(bf16[1,2,2,2,48,896]{5,4,3,2,1,0:T(8,128)(2,1)S(1)} %pad_maximum_fusion), channel_id=1, source_target_pairs={{0,2},{1,5},{2,0},{3,7},{4,6},{5,1},{6,4},{7,3},{8,10},{9,13},{10,... | collective-permute-start | bytes 2064392 | tf_op jit(solution)/shard_map/ppermute | solution.py:35
  135.2 3.9 %collective-permute-start.23 = (f32[3,4,48]{2,1,0:T(4,128)S(1)}, f32[3,4,48]{2,1,0:T(4,128)S(1)}, u32[]{:S(2)}, u32[]{:S(2)}) collective-permute-start(f32[3,4,48]{2,1,0:T(4,128)S(1)} %max.15), channel_id=1, source_target_pairs={{0,4},{1,3},{2,6},{3,1},{4,0},{5,7},{6,2},{7,5},{8,12},{9,11},{10,... | collective-permute-start | bytes 6920 | tf_op jit(solution)/shard_map/ppermute | solution.py:35
  139.1 4.5 %collective-permute-start.24 = (f32[3,4,48]{2,1,0:T(4,128)S(1)}, f32[3,4,48]{2,1,0:T(4,128)S(1)}, u32[]{:S(2)}, u32[]{:S(2)}) collective-permute-start(f32[3,4,48]{2,1,0:T(4,128)S(1)} %max.16), channel_id=1, source_target_pairs={{0,8},{1,9},{2,10},{3,11},{4,12},{5,13},{6,14},{7,15},{8,0},{9,1},... | collective-permute-start | bytes 6920 | tf_op jit(solution)/shard_map/ppermute | solution.py:35
  143.6 4.5 %collective-permute-start.25 = (f32[3,4,48]{2,1,0:T(4,128)S(1)}, f32[3,4,48]{2,1,0:T(4,128)S(1)}, u32[]{:S(2)}, u32[]{:S(2)}) collective-permute-start(f32[3,4,48]{2,1,0:T(4,128)S(1)} %max.17), channel_id=1, source_target_pairs={{0,16},{1,17},{2,18},{3,19},{4,20},{5,21},{6,22},{7,23},{8,24},{9,... | collective-permute-start | bytes 6920 | tf_op jit(solution)/shard_map/ppermute | solution.py:35
  148.1 1.2 collective-permute-start.26
  149.5 2.2 %copy-start.1 = (bf16[3584,576]{0,1:T(8,128)(2,1)S(1)}, bf16[3584,576]{0,1:T(8,128)(2,1)}, u32[]{:S(2)}) copy-start(bf16[3584,576]{0,1:T(8,128)(2,1)} %param.13) | copy-start | bytes 12386308

commit v3 on v0

v3 whole, which is shorter than its diff:
```python
import functools

import jax
import jax.numpy as jnp
from jax import lax
from jax.experimental import pallas as pl
from jax.experimental.pallas import tpu as pltpu
from jax.sharding import PartitionSpec as P

EPS = 1e-06
RATE = 0.5
F32 = jnp.float32
BF16 = jnp.bfloat16

STEPS = {"xy": (1, 2), "yx": (2, 1), "lo": (4, 4), "hi": (8, 8)}

SCATTER = (("xy", "yx", "hi", "lo"), ("xy", "lo", "yx", "hi"), ("lo", "xy", "yx", "hi"))
GATHER = ((3, 2, 1, 0), (3, 2, 0, 1), (3, 0, 2, 1))
PLAN = (0, 2, 1, 0, 0, 1, 2, 1, 2, 0, 0, 2, 2, 1, 1, 2, 2, 0, 1, 0, 1, 2, 2, 0, 0, 1, 1, 2, 0, 0, 2, 1, 1, 3, 1, 1, 3, 3, 2, 2, 0, 3, 1, 0, 3, 1, 2, 2, 3, 3, 0, 3, 3, 0, 3, 1, 0, 2)
SMALL = ("xy", "yx", "lo", "hi")


def row_weights(lengths, row_count):
    bounds = jnp.cumsum(lengths)
    position = lax.iota(jnp.int32, row_count)
    group_index = jnp.sum((position[None, :] >= bounds[:, None]).astype(jnp.int32), axis=0)
    member = group_index[None, :] == lax.iota(jnp.int32, lengths.shape[0])[:, None]
    length = jnp.sum(jnp.where(member, lengths[:, None], 0), axis=0)
    return (1.0 / length.astype(F32)).astype(BF16)


def exchange(value, step):
    pairs = []
    for roll in range(16):
        for core in range(2):
            pairs.append((2 * roll + core, 2 * (roll ^ STEPS[step][core]) + core))
    return lax.ppermute(value, ("roll", "tp"), pairs)


def swap_cores(value):
    return lax.ppermute(value, "tp", [(0, 1), (1, 0)])


def add(a, b):
    return (a.astype(F32) + b.astype(F32)).astype(a.dtype)


def head(latent, targets, weights, gain_vec, groups):
    width = gain_vec.shape[0]
    compressed = latent[:width]
    factor = lax.rsqrt(jnp.mean(compressed * compressed, axis=0) + EPS)
    gain_col = gain_vec[:, None]
    weight_f = weights.astype(F32)
    targets = targets.astype(F32)
    res_c = compressed * factor[None, :] * gain_col - targets[:width]
    res_r = latent[width:] - targets[width:]
    total = jnp.sum(res_c * res_c, axis=0) + jnp.sum(res_r * res_r, axis=0)
    row_terms = weight_f * (0.5 * total / latent.shape[0]) / groups
    scaled = weight_f[None, :] * res_c * gain_col
    inner = jnp.mean(scaled * compressed, axis=0)
    d_c = factor[None, :] * scaled - compressed * (factor * factor * factor * inner)[None, :]
    return row_terms, jnp.concatenate([d_c, weight_f[None, :] * res_r], axis=0)


def forward_kernel(
    chunks, x_hbm, w_hbm, gain_ref, part_ref, sent_ref, sq_ref, x_ref, w_ref, sems
):
    rows, feat = x_ref.shape
    width = w_ref.shape[0]
    cols = feat // chunks
    copies = []
    for k in range(chunks):
        span = slice(k * cols, (k + 1) * cols)
        pairs = ((w_hbm, w_ref), (x_hbm, x_ref))
        copies.append(
            [pltpu.make_async_copy(a.at[:, span], b.at[:, span], sems.at[n, k]) for n, (a, b) in enumerate(pairs)]
        )
    for pair in copies:
        for copy in pair:
            copy.start()
    sq = None
    for k in range(chunks):
        span = slice(k * cols, (k + 1) * cols)
        for copy in copies[k]:
            copy.wait()
        gained = (w_ref[:, span].astype(F32) * gain_ref[:, span]).astype(BF16)
        x = x_ref[:, span]
        part = lax.dot_general(gained, x, (((1,), (1,)), ((), ())), preferred_element_type=F32)
        if k > 0:
            part = part + part_ref[...]
        part_ref[...] = part
        if k == chunks - 1:
            sent_ref[:width] = part.astype(BF16)
        wide = x.astype(F32)
        wide = wide * wide
        for c in range(cols // 128):
            piece = wide[:, c * 128 : (c + 1) * 128]
            sq = piece if sq is None else sq + piece
    total = lax.dot_general(
        jnp.ones((8, 128), F32), sq, (((1,), (1,)), ((), ())), preferred_element_type=F32, precision=lax.Precision.HIGHEST
    )
    sq_ref[...] = total
    row = total[:1]
    top = row.astype(BF16)
    rest = row - top.astype(F32)
    mid = rest.astype(BF16)
    low = (rest - mid.astype(F32)).astype(BF16)
    index = lax.broadcasted_iota(jnp.int32, (16, rows), 0)
    terms = jnp.where(
        index == 0,
        top.astype(F32),
        jnp.where(index == 1, mid.astype(F32), jnp.where(index == 2, low.astype(F32), 0.0)),
    )
    sent_ref[width:] = terms.astype(BF16)


def whole():
    return pl.BlockSpec(memory_space=pltpu.VMEM)


def scalars():
    return pl.BlockSpec(memory_space=pltpu.SMEM)


def far():
    return pl.BlockSpec(memory_space=pltpu.HBM)


def in_hbm(value):
    return pltpu.with_memory_space_constraint(value, pltpu.HBM)


def vmem_limit(mib):
    return pltpu.CompilerParams(vmem_limit_bytes=mib * 1024 * 1024)


def forward(x, w_t, gain_row):
    rows, feat = x.shape
    width = w_t.shape[0]
    return pl.pallas_call(
        functools.partial(forward_kernel, 2),
        in_specs=[far(), far(), whole()],
        out_specs=[whole()] * 3,
        out_shape=[
            jax.ShapeDtypeStruct((width, rows), F32),
            jax.ShapeDtypeStruct((width + 16, rows), BF16),
            jax.ShapeDtypeStruct((8, rows), F32),
        ],
        scratch_shapes=[
            pltpu.VMEM(x.shape, BF16),
            pltpu.VMEM(w_t.shape, BF16),
            pltpu.SemaphoreType.DMA((2, 2)),
        ],
        compiler_params=vmem_limit(24),
        cost_estimate=pl.CostEstimate(flops=2 * rows * feat * width, bytes_accessed=10_000_000, transcendentals=0),
    )(in_hbm(x), in_hbm(w_t), gain_row)


def head_kernel(
    model_width,
    where_ref,
    masks_ref,
    lens_ref,
    part_ref,
    got_ref,
    sq_ref,
    t_hbm,
    dest_ref,
    gain_ref,
    x_hbm,
    d_ref,
    loss_ref,
    a_ref,
    b_ref,
    c_ref,
    target_ref,
    x_ref,
    sems,
):
    t_copy = pltpu.make_async_copy(t_hbm, target_ref, sems.at[0])
    x_copy = pltpu.make_async_copy(x_hbm, x_ref, sems.at[1])
    t_copy.start()
    x_copy.start()
    width, rows = part_ref.shape
    lat = gain_ref.shape[0]
    groups = lens_ref.shape[0]
    blk = d_ref.shape[1]
    trainers = loss_ref.shape[0]
    lanes = 256
    gain = gain_ref[...]
    sums = None
    t_copy.wait()
    for first in range(0, rows, lanes):
        cut = slice(first, first + lanes)
        terms = got_ref[width:, cut].astype(F32)
        squares = sq_ref[:1, cut] + (terms[0:1] + terms[1:2] + terms[2:3])
        scale = lax.rsqrt(squares / model_width + EPS)
        position = lax.broadcasted_iota(jnp.int32, (1, lanes), 1) + first
        length = jnp.zeros((1, lanes), jnp.int32)
        start = 0
        for g in range(groups):
            size = lens_ref[g]
            length = jnp.where((position >= start) & (position < start + size), size, length)
            start = start + size
        weight = (1.0 / length.astype(F32)).astype(BF16).astype(F32)

        comp = (part_ref[:lat, cut] + got_ref[:lat, cut].astype(F32)) * scale
        factor = lax.rsqrt(jnp.mean(comp * comp, axis=0, keepdims=True) + EPS)
        res_c = comp * factor * gain - target_ref[:lat, cut].astype(F32)
        res_r = (part_ref[lat:, cut] + got_ref[lat:width, cut].astype(F32)) * scale
        res_r = res_r - target_ref[lat:, cut].astype(F32)
        total = jnp.sum(res_c * res_c, axis=0, keepdims=True) + jnp.sum(res_r * res_r, axis=0, keepdims=True)
        row_terms = weight * (0.5 * (total / width)) / groups
        scaled = weight * res_c * gain
        inner = jnp.mean(scaled * comp, axis=0, keepdims=True)
        d_c = (factor * scale) * scaled - comp * (factor * factor * factor * inner * scale)
        d_r = (weight * scale) * res_r
        for j in range(d_ref.shape[0]):
            lo, hi = j * blk, (j + 1) * blk
            if hi <= lat:
                piece = d_c[lo:hi]
            elif lo >= lat:
                piece = d_r[lo - lat : hi - lat]
            else:
                piece = jnp.concatenate([d_c[lo:], d_r[: hi - lat]], axis=0)
            d_ref[(j // 4) * 4 + ((j % 4) ^ masks_ref[j // 4]), :, cut] = piece.astype(BF16)
        named = dest_ref[:, cut] == lax.broadcasted_iota(jnp.int32, (trainers, lanes), 0)
        named = jnp.where(named, row_terms, 0.0)
        for c in range(0, lanes, 128):
            sums = named[:, c : c + 128] if sums is None else sums + named[:, c : c + 128]
    loss_ref[...] = jnp.broadcast_to(jnp.sum(sums, axis=1, keepdims=True), loss_ref.shape)
    x_copy.wait()
    grad_halves(where_ref, d_ref, x_ref, (a_ref, b_ref, c_ref))


def grad_halves(where_ref, d_ref, x_ref, out_refs):
    blocks, blk, rows = d_ref.shape
    cols = out_refs[0].shape[-1]
    for first, count in ((2, 1), (0, 2)):
        lhs = d_ref[first * 4 : (first + count) * 4].reshape(count * 4 * blk, rows)
        for i in range(2):
            col = pl.multiple_of((where_ref[2 * first] * 2 + i) * cols, 128)
            out = jnp.dot(lhs, x_ref[:, pl.ds(col, cols)], preferred_element_type=F32).astype(BF16)
            for c in range(count):
                part = out[c * 4 * blk : (c + 1) * 4 * blk]
                out_refs[first + c][i ^ where_ref[2 * (first + c) + 1]] = part.reshape(4, blk, cols)


def head_call(part, got, sq, targets_t, dest_row, lengths, gain_col, x, where, row_masks, model_width, trainers):
    width, rows = part.shape
    blk, cols = width // 12, x.shape[1] // 4
    return pl.pallas_call(
        functools.partial(head_kernel, model_width),
        in_specs=[scalars()] * 3 + [whole()] * 3 + [far()] + [whole()] * 2 + [far()],
        out_specs=[whole()] * 5,
        out_shape=[
            jax.ShapeDtypeStruct((12, blk, rows), BF16),
            jax.ShapeDtypeStruct((trainers, 128), F32),
        ]
        + [jax.ShapeDtypeStruct((2, 4, blk, cols), BF16)] * 3,
        scratch_shapes=[
            pltpu.VMEM(targets_t.shape, BF16),
            pltpu.VMEM(x.shape, BF16),
            pltpu.SemaphoreType.DMA((2,)),
        ],
        compiler_params=vmem_limit(24),
        cost_estimate=pl.CostEstimate(flops=width * rows * cols * 4, bytes_accessed=12_000_000, transcendentals=0),
    )(where, row_masks, lengths, part, got, sq, in_hbm(targets_t), dest_row, gain_col, in_hbm(x))


def keep_kernel(where_ref, d_ref, x_hbm, a_ref, b_ref, c_ref, x_ref, sem):
    copy = pltpu.make_async_copy(x_hbm, x_ref, sem)
    copy.start()
    copy.wait()
    grad_halves(where_ref, d_ref, x_ref, (a_ref, b_ref, c_ref))


def keep_call(d, x, where):
    blk, cols = d.shape[1], x.shape[1] // 4
    return pl.pallas_call(
        keep_kernel,
        in_specs=[scalars(), whole(), far()],
        out_specs=[whole()] * 3,
        out_shape=[jax.ShapeDtypeStruct((2, 4, blk, cols), BF16)] * 3,
        scratch_shapes=[pltpu.VMEM(x.shape, BF16), pltpu.SemaphoreType.DMA],
        compiler_params=vmem_limit(24),
        cost_estimate=pl.CostEstimate(flops=12 * blk * d.shape[2] * cols * 4, bytes_accessed=10_000_000, transcendentals=0),
    )(where, d, in_hbm(x))


def w_copies(where_ref, w_hbm, w_buf, sem, count):
    rows, cols = w_buf.shape[1:]
    copies = []
    for s in range(count):
        chain = (s % 6) // 2
        col = pl.multiple_of(where_ref[s] * cols, 128)
        tile = w_hbm.at[pl.ds(chain * rows, rows), pl.ds(col, cols)]
        copies.append(pltpu.make_async_copy(tile, w_buf.at[s], sem.at[s]))
        copies[-1].start()
    return copies


def updated_block(where_ref, coef_ref, gain_ref, w_buf, g_ref, s, j, mask):
    blk, cols = g_ref.shape[2:]
    col = pl.multiple_of(where_ref[s] * cols, 128)
    factor = coef_ref[0] * gain_ref[:, pl.ds(col, cols)]
    g = g_ref[s % 2, j ^ mask].astype(F32)
    return w_buf[s, j * blk : (j + 1) * blk].astype(F32) - factor * g


def top_kernel(where_ref, coef_ref, gain_ref, w_hbm, start_ref, a_ref, b_ref, c_ref, out_ref, w_buf, sem):
    copies = w_copies(where_ref, w_hbm, w_buf, sem, 6)
    blk, cols = a_ref.shape[2:]
    for s in range(6):
        chain = s // 2
        copies[s].wait()
        for j in range(4):
            g_ref = (a_ref, b_ref, c_ref)[chain]
            size = jnp.abs(
                updated_block(where_ref, coef_ref, gain_ref, w_buf, g_ref, s, j, where_ref[6 + chain])
            )
            here = slice((chain * 4 + j) * blk, (chain * 4 + j + 1) * blk)
            top = start_ref[here] if s % 2 == 0 else out_ref[here]
            for k in range(cols // 128):
                top = jnp.maximum(top, size[:, k * 128 : (k + 1) * 128])
            out_ref[here] = top


def top_part(pieces, w_t, gain_row, coef, start, columns, row_masks):
    blk, cols = pieces[0].shape[-2:]
    where = jnp.stack([*columns, *row_masks]).astype(jnp.int32)
    return pl.pallas_call(
        top_kernel,
        in_specs=[scalars(), scalars(), whole(), far()] + [whole()] * 4,
        out_specs=whole(),
        out_shape=jax.ShapeDtypeStruct((w_t.shape[0], 128), F32),
        scratch_shapes=[pltpu.VMEM((6, 4 * blk, cols), BF16), pltpu.SemaphoreType.DMA((6,))],
        compiler_params=vmem_limit(24),
        cost_estimate=pl.CostEstimate(flops=4 * w_t.size, bytes_accessed=2 * w_t.size, transcendentals=0),
    )(where, coef, gain_row, in_hbm(w_t), start, *pieces)


def code_kernel(where_ref, coef_ref, gain_ref, w_hbm, mine_ref, other_ref, *rest):
    g_refs, (out_ref, buf, w_buf, inv_ref, sem, w_sem) = rest[:6], rest[6:]
    loads = w_copies(where_ref, w_hbm, w_buf, w_sem, 12)
    blk, cols = g_refs[0].shape[2:]
    rows = 4 * blk
    top = jnp.max(jnp.maximum(mine_ref[...], other_ref[...]), axis=1, keepdims=True)
    inv_ref[...] = jnp.broadcast_to(1.0 / (top + EPS), inv_ref.shape)
    copies = []
    for s in range(12):
        chain = (s % 6) // 2
        g_ref = g_refs[3 * (s // 6) + chain]
        loads[s].wait()
        for j in range(4):
            new = updated_block(where_ref, coef_ref, gain_ref, w_buf, g_ref, s, j, where_ref[12 + chain])
            first = chain * rows + j * blk
            inv = jnp.concatenate([inv_ref[first : first + blk]] * (cols // 128), axis=1)
            buf[s, j * blk : (j + 1) * blk] = (new * inv).astype(BF16)
        col = pl.multiple_of(where_ref[s] * cols, 128)
        tile = out_ref.at[pl.ds(chain * rows, rows), pl.ds(col, cols)]
        copies.append(pltpu.make_async_copy(buf.at[s], tile, sem.at[s]))
        copies[-1].start()
    for copy in copies:
        copy.wait()


def code_all(pieces, w_t, gain_row, coef, mine, other, columns, row_masks):
    blk, cols = pieces[0].shape[-2:]
    where = jnp.stack([*columns, *row_masks]).astype(jnp.int32)
    return pl.pallas_call(
        code_kernel,
        in_specs=[scalars(), scalars(), whole(), far()] + [whole()] * 8,
        out_specs=far(),
        out_shape=jax.ShapeDtypeStruct(w_t.shape, BF16),
        scratch_shapes=[
            pltpu.VMEM((12, 4 * blk, cols), BF16),
            pltpu.VMEM((12, 4 * blk, cols), BF16),
            pltpu.VMEM((w_t.shape[0], 128), F32),
            pltpu.SemaphoreType.DMA((12,)),
            pltpu.SemaphoreType.DMA((12,)),
        ],
        compiler_params=vmem_limit(24),
        cost_estimate=pl.CostEstimate(flops=8 * w_t.size, bytes_accessed=6 * w_t.size, transcendentals=0),
    )(where, coef, gain_row, in_hbm(w_t), mine, other, *pieces)


def paired_shards(hidden, targets, group_lengths, dest_ids, input_gain, latent_gain, kv_weight):
    rows, feat = hidden.shape
    width = kv_weight.shape[1]
    model_width = 2 * feat
    blk, cols = width // 12, feat // 4
    roll = lax.axis_index("roll")
    core = lax.axis_index("tp")
    x_bit, y_bit = roll & 1, (roll >> 1) & 1
    bit = {
        "xy": jnp.where(core == 0, x_bit, y_bit),
        "yx": jnp.where(core == 0, y_bit, x_bit),
        "lo": (roll >> 2) & 1,
        "hi": (roll >> 3) & 1,
    }
    bits = [[bit[step] for step in order] for order in SCATTER]
    row_masks = [b[2] * 2 + b[3] for b in bits]

    w_t = kv_weight.T
    gain_row = input_gain[None, :]
    part, sent, squares = forward(hidden, w_t, gain_row)
    got = swap_cores(sent)
    give = jnp.stack([v for b in bits for v in (1 - b[0], b[1])]).astype(jnp.int32)
    take = jnp.stack([v for b in bits for v in (b[0], b[1])]).astype(jnp.int32)
    d, losses, *away = head_call(
        part,
        got,
        squares,
        targets.T,
        dest_ids.T,
        group_lengths[0],
        latent_gain[:, None],
        hidden,
        give,
        jnp.stack(row_masks).astype(jnp.int32),
        model_width,
        16,
    )
    held = keep_call(d, hidden, take)
    own_cols = [b[0] * 2 + b[1] for b in bits]
    own_gain = [lax.dynamic_slice(gain_row, (0, c * cols), (1, cols)) for c in own_cols]
    shape = (1, 2, 2, 2, blk, cols)
    away = [v.reshape(shape) for v in away]
    held = [v.reshape(shape) for v in held]
    taken = [0] * 4
    flight = [None] * 4
    sums = [None] * 3
    settled = []
    small = None
    for lane in PLAN:
        step, taken[lane] = divmod(taken[lane], 2)[0], taken[lane] + 1
        if flight[lane] is None:
            if lane == 3:
                if step == 0:
                    power = sum(jnp.sum(jnp.square(v.astype(F32) * g)) for v, g in zip(sums, own_gain))
                    small = jnp.concatenate([0.5 * losses, jnp.broadcast_to(power, (8, 128))], axis=0)
                message = small
            elif step == 0:
                message = away[lane]
            elif step < 4:
                message = lax.index_in_dim(held[lane], 1, step, keepdims=True)
            else:
                message = held[lane]
            if settled:
                message, *_ = lax.optimization_barrier((message, *settled))
                settled = []
            if lane == 3:
                flight[lane] = exchange(message, SMALL[step]) if step < 4 else swap_cores(message)
            else:
                order = SCATTER[lane]
                flight[lane] = exchange(message, order[step] if step < 4 else order[GATHER[lane][step - 4]])
            continue
        got, flight[lane] = flight[lane], None
        if lane == 3:
            small = small + got
            settled.append(small)
        elif step < 4:
            keep = held[lane] if step == 0 else lax.index_in_dim(held[lane], 0, step, keepdims=True)
            held[lane] = sums[lane] = add(keep, got)
            settled.append(held[lane])
        elif step < 7:
            held[lane] = jnp.concatenate([held[lane], got], axis=GATHER[lane][step - 4])
            settled.append(held[lane])
        else:
            held[lane] = (held[lane], got)

    coef = RATE * lax.rsqrt(small[16, :1] / (model_width * width) + EPS)
    top = jnp.zeros((width, 128), F32)
    pieces, columns = [], []
    for n in range(2):
        part = [held[chain][n].reshape(2, 4, blk, cols) for chain in range(3)]
        spots = []
        for chain in range(3):
            inner = GATHER[chain][3] == 1
            spots += [(2 * i + n if inner else 2 * n + i) ^ own_cols[chain] for i in range(2)]
        top = top_part(part, w_t, gain_row, coef, top, spots, row_masks)
        pieces += part
        columns += spots
    codes = code_all(pieces, w_t, gain_row, coef, top, swap_cores(top), columns, row_masks)
    loss = lax.dynamic_slice(small, (roll, 0), (1, 1))
    return loss.reshape(1), codes.T


def any_shards(hidden, targets, group_lengths, dest_ids, input_gain, latent_gain, kv_weight):
    rows, feat = hidden.shape
    width = kv_weight.shape[1]
    roll_count = lax.axis_size("roll")
    model_width = feat * lax.axis_size("tp")
    wide = hidden.astype(F32)
    scale = lax.rsqrt(lax.psum(jnp.sum(wide * wide, axis=1), "tp") / model_width + EPS)
    normed = (wide * scale[:, None] * input_gain).astype(BF16)
    latent = lax.psum(jnp.dot(normed, kv_weight, preferred_element_type=F32), "tp")
    weights = row_weights(group_lengths[0], rows)
    row_terms, d_latent = head(latent.T, targets.T, weights, latent_gain, group_lengths.shape[1])
    grad = lax.dot_general(
        d_latent.astype(BF16), normed, (((1,), (0,)), ((), ())), preferred_element_type=F32
    )
    grad = lax.psum(grad.astype(BF16), "roll").astype(F32)
    dest = dest_ids[:, 0]
    named = dest[None, :] == lax.iota(jnp.int32, roll_count)[:, None]
    losses = lax.psum(jnp.sum(jnp.where(named, row_terms[None, :], 0.0), axis=1), "roll")
    power = lax.psum(jnp.sum(grad * grad), "tp")
    updated = kv_weight.T.astype(F32) - RATE * grad * lax.rsqrt(power / (model_width * width) + EPS)
    peak = lax.pmax(jnp.max(jnp.abs(updated), axis=1), "tp") + EPS
    codes = (updated / peak[:, None]).astype(BF16)
    loss = lax.dynamic_slice(losses, (lax.axis_index("roll"),), (1,))
    return loss, codes.T


def solution(mesh):
    in_specs = (
        P("roll", "tp"),
        P("roll", None),
        P("roll", None),
        P("roll", None),
        P("tp"),
        P(),
        P("tp", None),
    )
    out_specs = (P("roll"), P("tp", None))
    paired = mesh.shape["roll"] == 16 and mesh.shape["tp"] == 2
    body = paired_shards if paired else any_shards
    return jax.shard_map(body, mesh=mesh, in_specs=in_specs, out_specs=out_specs, check_vma=False)
```

time: 345 us -> 132 us (0.38)
  waiting for transfers between devices: 264 us -> 49.2 us
  starting transfers between devices: 6.87 us -> 39.2 us
  Pallas kernels: 0 us -> 30.1 us
  other arithmetic: 29.5 us -> 3.38 us
  matrix products: 14.5 us -> 0 us
  between operations: 14.9 us -> 3.68 us
  blocking collectives: 8.14 us -> 0 us
    psum x2 -> x0, waiting for transfers between devices: 264 us -> none  [the longest x1 241 us: shards(): grad = lax.psum(grad_part, 'roll')]
    ppermute x0 -> x31, waiting for transfers between devices: none -> 49.2 us  [the longest x28 44.6 us: exchange(): return lax.ppermute(value, ('roll', 'tp'), pairs)]
    ppermute x0 -> x31, starting transfers between devices: none -> 39.2 us  [the longest x28 38.5 us: exchange(): return lax.ppermute(value, ('roll', 'tp'), pairs)]
    pallas_call x0 -> x6, Pallas kernels: none -> 30.1 us  [the longest x1 7.62 us: forward(): pl.pallas_call(functools.partial(forward_kernel, 2), in_specs=[far(), far...]
    dot_general x2 -> x0, matrix products: 14.5 us -> none  [the longest x1 8.51 us: forward_backward(): jnp.dot(normed, kv_weight, preferred_element_type=jnp.float32)]
    reduce_sum x8 -> x3, other arithmetic: 12.4 us -> 1.94 us  [paired_shards(): jnp.sum(jnp.square(v.astype(F32) * g))]
    all_to_all x1 -> x0, starting transfers between devices: 6.79 us -> none  [shards(): lax.all_to_all(sent_terms.reshape(roll_count, capacity), 'roll', split_ax...]
    reduce_max x1 -> x0, other arithmetic: 5.91 us -> none  [shards(): peak = lax.pmax(jnp.max(jnp.abs(updated), axis=0), 'tp') + EPS]
  transfers between devices with their start and end apart: 3 -> 31, of which waited for: 2 -> 18; matrix products, arithmetic and copies ran while one was open for 3% -> 4% of each run, Pallas kernels for 0% -> 6%
where the time goes in v3:
time: 132 us; the launch traced here: 131 us
  waiting for transfers between devices  49.2 us (37%)
  starting transfers between devices  39.2 us (30%)
  Pallas kernels  30.1 us (23%)
  local copies, waits for them, and re-layouts  5.89 us (4%)
  between operations  3.68 us (3%)
  other arithmetic  3.38 us (3%)
    ppermute x28, waiting for transfers between devices, exchange(): return lax.ppermute(value, ('roll', 'tp'), pairs)  44.6 us
    ppermute x28, starting transfers between devices, exchange(): return lax.ppermute(value, ('roll', 'tp'), pairs)  38.5 us
    pallas_call x1, Pallas kernels, forward(): pl.pallas_call(functools.partial(forward_kernel, 2), in_specs=[far(), far...  7.62 us
    pallas_call x2, Pallas kernels, top_part(): pl.pallas_call(top_kernel, in_specs=[scalars(), scalars(), whole(), far()...  6.27 us
    pallas_call x1, Pallas kernels, head_call(): pl.pallas_call(functools.partial(head_kernel, model_width), in_specs=[sca...  6.09 us
    pallas_call x1, Pallas kernels, keep_call(): pl.pallas_call(keep_kernel, in_specs=[scalars(), whole(), far()], out_spe...  5.14 us
    pallas_call x1, Pallas kernels, code_all(): pl.pallas_call(code_kernel, in_specs=[scalars(), scalars(), whole(), far(...  4.93 us
    ppermute x3, waiting for transfers between devices, swap_cores(): return lax.ppermute(value, 'tp', [(0, 1), (1, 0)])  4.65 us
  transfers between devices with their start and end apart: 31, of which 18 were waited for; matrix products, arithmetic and copies ran while one was open for 4% of the time, Pallas kernels for 6%

profile of v3, /device:TPU:0, one launch (start us, length us, event | category | flops | bytes accessed | tf_op | source)
XLA Modules:
  0.0 131.5 jit_solution(14046074401554877797)
XLA Ops:
  0.6 0.7 broadcast_in_dim.6.gain_ref
  1.4 7.6 %shard_map.86 = (f32[576,768]{1,0:T(8,128)S(1)}, bf16[592,768]{1,0:T(8,128)(2,1)}, f32[8,768]{1,0:T(8,128)S(1)}) custom-call(bf16[768,3584]{1,0:T(8,128)(2,1)} %x_hbm.5, bf16[576,3584]{1,0:T(8,128)(2,1)} %bitcast.69, f32[1,3584]{1,0:T(1,128)S(1)} %broadcast_in_dim.6.gain_ref), custom_call_target="tpu_custom_call" | custom-call | flops 3170893824 | bytes 10000000 | tf_op jit(solution)/shard_map/pallas_call | solution.py:140
  9.0 0.5 collective-permute-start
  9.6 0.1 copy.13.gain_ref
  9.9 2.0 %collective-permute-done.got_ref = bf16[592,768]{1,0:T(8,128)(2,1)S(1)} collective-permute-done((bf16[592,768]{1,0:T(8,128)(2,1)}, bf16[592,768]{1,0:T(8,128)(2,1)S(1)}, u32[]{:S(2)}, u32[]{:S(2)}) %collective-permute-start) | collective-permute-done | bytes 909344 | tf_op jit(solution)/shard_map/ppermute | solution.py:41
  11.9 6.1 %shard_map.87 = (bf16[12,48,768]{2,1,0:T(8,128)(2,1)S(1)}, f32[16,128]{1,0:T(8,128)S(1)}, bf16[2,4,48,896]{3,2,1,0:T(8,128)(2,1)S(1)}, bf16[2,4,48,896]{3,2,1,0:T(8,128)(2,1)S(1)}, bf16[2,4,48,896]{3,2,1,0:T(8,128)(2,1)}) custom-call(s32[6]{0:T(128)S(1)} %stack.109.where_ref, s32[3]{0:T(128)S(1)} %pad_add_fusion.1.masks_ref, s32[8]{0:T(128)S(1)} %bitcast.66, ...), custom_call_target="tpu_custom_call" | custom-call | flops 1585446912 | bytes 12000000 | tf_op jit(solution)/shard_map/pallas_call | solution.py:252
  18.0 0.9 copy-done
  18.9 0.9 copy-done.4
  19.7 0.8 copy-done.5
  20.6 2.9 %collective-permute-start.5 = (bf16[1,2,2,2,48,896]{5,4,3,2,0,1:T(8,128)(2,1)}, bf16[1,2,2,2,48,896]{5,4,3,2,0,1:T(8,128)(2,1)S(1)}, u32[]{:S(2)}, u32[]{:S(2)}) collective-permute-start(bf16[1,2,2,2,48,896]{5,4,3,2,0,1:T(8,128)(2,1)} %bitcast.21), channel_id=1, source_target_pairs={{0,8},{1,9},{2,10},{3,11},{4,12},{5,13},{6,14},{7,15},{8,0},{9,1},... | collective-permute-start | bytes 2064392 | tf_op jit(solution)/shard_map/ppermute | solution.py:37
  23.5 1.5 %collective-permute-start.1 = (bf16[1,2,2,2,48,896]{5,4,3,2,1,0:T(8,128)(2,1)}, bf16[1,2,2,2,48,896]{5,4,3,2,1,0:T(8,128)(2,1)S(1)}, u32[]{:S(2)}, u32[]{:S(2)}) collective-permute-start(bf16[1,2,2,2,48,896]{5,4,3,2,1,0:T(8,128)(2,1)} %bitcast.68), channel_id=1, source_target_pairs={{0,2},{1,5},{2,0},{3,7},{4,6},{5,1},{6,4},{7,3},{8,10},{9,13},{10,... | collective-permute-start | bytes 2064392 | tf_op jit(solution)/shard_map/ppermute | solution.py:37
  25.2 0.5 collective-permute-start.4
  25.7 1.2 copy-done.1
  26.9 5.1 %shard_map.88 = (bf16[2,4,48,896]{3,2,1,0:T(8,128)(2,1)S(1)}, bf16[2,4,48,896]{3,2,1,0:T(8,128)(2,1)S(1)}, bf16[2,4,48,896]{3,2,1,0:T(8,128)(2,1)S(1)}) custom-call(s32[6]{0:T(128)S(1)} %stack.113.where_ref, bf16[12,48,768]{2,1,0:T(8,128)(2,1)S(1)} %copy-done.1, bf16[768,3584]{1,0:T(8,128)(2,1)} %x_hbm.5), custom_call_target="tpu_custom_call" | custom-call | flops 1585446912 | bytes 10000000 | tf_op jit(solution)/shard_map/pallas_call | solution.py:280
  32.0 7.4 %collective-permute-done.5 = bf16[1,2,2,2,48,896]{5,4,3,2,0,1:T(8,128)(2,1)S(1)} collective-permute-done((bf16[1,2,2,2,48,896]{5,4,3,2,0,1:T(8,128)(2,1)}, bf16[1,2,2,2,48,896]{5,4,3,2,0,1:T(8,128)(2,1)S(1)}, u32[]{:S(2)}, u32[]{:S(2)}) %collective-permute-start.5) | collective-permute-done | bytes 688160 | tf_op jit(solution)/shard_map/ppermute | solution.py:37
  39.5 0.2 fusion
  39.7 1.7 %collective-permute-start.10 = (bf16[1,1,2,2,48,896]{5,4,3,2,0,1:T(8,128)(2,1)S(1)}, bf16[1,1,2,2,48,896]{5,4,3,2,0,1:T(8,128)(2,1)S(1)}, u32[]{:S(2)}, u32[]{:S(2)}) collective-permute-start(bf16[1,1,2,2,48,896]{5,4,3,2,0,1:T(8,128)(2,1)S(1)} %slice.89), channel_id=1, source_target_pairs={{0,2},{1,5},{2,0},{3,7},{4,6},{5,1},{6,4},{7,3},{8,10},{9,13},{10,... | collective-permute-start | bytes 1032200 | tf_op jit(solution)/shard_map/ppermute | solution.py:37
  41.4 0.2 fusion.2
  41.6 1.6 %collective-permute-start.2 = (bf16[1,1,2,2,48,896]{5,4,3,2,1,0:T(8,128)(2,1)S(1)}, bf16[1,1,2,2,48,896]{5,4,3,2,1,0:T(8,128)(2,1)S(1)}, u32[]{:S(2)}, u32[]{:S(2)}) collective-permute-start(bf16[1,1,2,2,48,896]{5,4,3,2,1,0:T(8,128)(2,1)S(1)} %slice.77), channel_id=1, source_target_pairs={{0,4},{1,3},{2,6},{3,1},{4,0},{5,7},{6,2},{7,5},{8,12},{9,11},{10,... | collective-permute-start | bytes 1032200 | tf_op jit(solution)/shard_map/ppermute | solution.py:37
  43.2 0.2 fusion.1
  43.4 1.6 %collective-permute-start.6 = (bf16[1,1,2,2,48,896]{5,4,3,2,0,1:T(8,128)(2,1)S(1)}, bf16[1,1,2,2,48,896]{5,4,3,2,0,1:T(8,128)(2,1)S(1)}, u32[]{:S(2)}, u32[]{:S(2)}) collective-permute-start(bf16[1,1,2,2,48,896]{5,4,3,2,0,1:T(8,128)(2,1)S(1)} %slice.83), channel_id=1, source_target_pairs={{0,8},{1,9},{2,10},{3,11},{4,12},{5,13},{6,14},{7,15},{8,0},{9,1},... | collective-permute-start | bytes 1032200 | tf_op jit(solution)/shard_map/ppermute | solution.py:37
  45.0 5.6 %collective-permute-done.10 = bf16[1,1,2,2,48,896]{5,4,3,2,0,1:T(8,128)(2,1)S(1)} collective-permute-done((bf16[1,1,2,2,48,896]{5,4,3,2,0,1:T(8,128)(2,1)S(1)}, bf16[1,1,2,2,48,896]{5,4,3,2,0,1:T(8,128)(2,1)S(1)}, u32[]{:S(2)}, u32[]{:S(2)}) %collective-permute-start.10) | collective-permute-done | bytes 344096 | tf_op jit(solution)/shard_map/ppermute | solution.py:37
  50.8 1.3 collective-permute-start.11
  52.1 2.4 %collective-permute-start.3 = (bf16[1,1,1,2,48,896]{5,4,3,2,1,0:T(8,128)(2,1)S(1)}, bf16[1,1,1,2,48,896]{5,4,3,2,1,0:T(8,128)(2,1)S(1)}, u32[]{:S(2)}, u32[]{:S(2)}) collective-permute-start(bf16[1,1,1,2,48,896]{5,4,3,2,1,0:T(8,128)(2,1)S(1)} %slice.79), channel_id=1, source_target_pairs={{0,16},{1,17},{2,18},{3,19},{4,20},{5,21},{6,22},{7,23},{8,24},{9,... | collective-permute-start | bytes 516104 | tf_op jit(solution)/shard_map/ppermute | solution.py:37
  54.6 1.4 %collective-permute-start.7 = (bf16[1,1,1,2,48,896]{5,4,3,2,0,1:T(8,128)(2,1)S(1)}, bf16[1,1,1,2,48,896]{5,4,3,2,0,1:T(8,128)(2,1)S(1)}, u32[]{:S(2)}, u32[]{:S(2)}) collective-permute-start(bf16[1,1,1,2,48,896]{5,4,3,2,0,1:T(8,128)(2,1)S(1)} %slice.85), channel_id=1, source_target_pairs={{0,4},{1,3},{2,6},{3,1},{4,0},{5,7},{6,2},{7,5},{8,12},{9,11},{10,... | collective-permute-start | bytes 516104 | tf_op jit(solution)/shard_map/ppermute | solution.py:37
  56.0 0.2 collective-permute-done.11
  56.3 2.8 %collective-permute-start.12 = (bf16[1,1,1,1,48,896]{5,4,3,2,0,1:T(8,128)(2,1)S(1)}, bf16[1,1,1,1,48,896]{5,4,3,2,0,1:T(8,128)(2,1)S(1)}, u32[]{:S(2)}, u32[]{:S(2)}) collective-permute-start(bf16[1,1,1,1,48,896]{5,4,3,2,0,1:T(8,128)(2,1)S(1)} %slice.93), channel_id=1, source_target_pairs={{0,16},{1,17},{2,18},{3,19},{4,20},{5,21},{6,22},{7,23},{8,24},{9,... | collective-permute-start | bytes 258056 | tf_op jit(solution)/shard_map/ppermute | solution.py:37
  59.1 5.5 %collective-permute-done.3 = bf16[1,1,1,2,48,896]{5,4,3,2,1,0:T(8,128)(2,1)S(1)} collective-permute-done((bf16[1,1,1,2,48,896]{5,4,3,2,1,0:T(8,128)(2,1)S(1)}, bf16[1,1,1,2,48,896]{5,4,3,2,1,0:T(8,128)(2,1)S(1)}, u32[]{:S(2)}, u32[]{:S(2)}) %collective-permute-start.3) | collective-permute-done | bytes 172064 | tf_op jit(solution)/shard_map/ppermute | solution.py:37
  64.8 4.0 %collective-permute-start.8 = (bf16[1,1,1,1,48,896]{5,4,3,2,1,0:T(8,128)(2,1)S(1)}, bf16[1,1,1,1,48,896]{5,4,3,2,1,0:T(8,128)(2,1)S(1)}, u32[]{:S(2)}, u32[]{:S(2)}) collective-permute-start(bf16[1,1,1,1,48,896]{5,4,3,2,1,0:T(8,128)(2,1)S(1)} %slice.81), channel_id=1, source_target_pairs={{0,8},{1,9},{2,10},{3,11},{4,12},{5,13},{6,14},{7,15},{8,0},{9,1},... | collective-permute-start | bytes 258056 | tf_op jit(solution)/shard_map/ppermute | solution.py:37
  68.8 0.6 multiply_reduce_fusion
  69.6 2.4 %collective-permute-done.9 = bf16[1,1,1,1,48,896]{5,4,3,2,0,1:T(8,128)(2,1)S(1)} collective-permute-done((bf16[1,1,1,1,48,896]{5,4,3,2,0,1:T(8,128)(2,1)S(1)}, bf16[1,1,1,1,48,896]{5,4,3,2,0,1:T(8,128)(2,1)S(1)}, u32[]{:S(2)}, u32[]{:S(2)}) %collective-permute-start.9) | collective-permute-done | bytes 86048 | tf_op jit(solution)/shard_map/ppermute | solution.py:37
  71.9 0.6 multiply_reduce_fusion.1
  72.6 0.5 collective-permute-start.20
  73.1 0.6 multiply_reduce_fusion.2
  75.6 1.6 %collective-permute-start.13 = (f32[24,128]{1,0:T(8,128)S(1)}, f32[24,128]{1,0:T(8,128)S(1)}, u32[]{:S(2)}, u32[]{:S(2)}) collective-permute-start(f32[24,128]{1,0:T(8,128)S(1)} %concatenate.30), channel_id=1, source_target_pairs={{0,2},{1,5},{2,0},{3,7},{4,6},{5,1},{6,4},{7,3},{8,10},{9,13},{10,... | collective-permute-start | bytes 36872 | tf_op jit(solution)/shard_map/ppermute | solution.py:37
  77.1 1.9 %collective-permute-start.17 = (bf16[1,1,1,1,48,896]{5,4,3,2,1,0:T(8,128)(2,1)S(1)}, bf16[1,1,1,1,48,896]{5,4,3,2,1,0:T(8,128)(2,1)S(1)}, u32[]{:S(2)}, u32[]{:S(2)}) collective-permute-start(bf16[1,1,1,1,48,896]{5,4,3,2,1,0:T(8,128)(2,1)S(1)} %get-tuple-element.52), channel_id=1, source_target_pairs={{0,8},{1,9},{2,10},{3,11},{4,12},{5,13},{6,14},{7,15},{8,0},{9,1},... | collective-permute-start | bytes 258056 | tf_op jit(solution)/shard_map/ppermute | solution.py:37
  79.0 0.7 collective-permute-done.20
  79.7 0.9 collective-permute-start.21
  80.7 0.9 collective-permute-done.17
  81.6 2.8 %collective-permute-start.19 = (bf16[1,1,1,2,48,896]{5,4,3,2,1,0:T(8,128)(2,1)S(1)}, bf16[1,1,1,2,48,896]{5,4,3,2,1,0:T(8,128)(2,1)S(1)}, u32[]{:S(2)}, u32[]{:S(2)}) collective-permute-start(bf16[1,1,1,2,48,896]{5,4,3,2,1,0:T(8,128)(2,1)S(1)} %pad_maximum_fusion.6), channel_id=1, source_target_pairs={{0,16},{1,17},{2,18},{3,19},{4,20},{5,21},{6,22},{7,23},{8,24},{9,... | collective-permute-start | bytes 516104 | tf_op jit(solution)/shard_map/ppermute | solution.py:37
  84.5 0.8 collective-permute-done.21
  85.3 1.6 %collective-permute-start.22 = (bf16[1,1,2,2,48,896]{5,4,3,2,0,1:T(8,128)(2,1)S(1)}, bf16[1,1,2,2,48,896]{5,4,3,2,0,1:T(8,128)(2,1)S(1)}, u32[]{:S(2)}, u32[]{:S(2)}) collective-permute-start(bf16[1,1,2,2,48,896]{5,4,3,2,0,1:T(8,128)(2,1)S(1)} %pad_maximum_fusion.4), channel_id=1, source_target_pairs={{0,2},{1,5},{2,0},{3,7},{4,6},{5,1},{6,4},{7,3},{8,10},{9,13},{10,... | collective-permute-start | bytes 1032200 | tf_op jit(solution)/shard_map/ppermute | solution.py:37
  86.8 3.7 %collective-permute-done.14 = f32[24,128]{1,0:T(8,128)S(1)} collective-permute-done((f32[24,128]{1,0:T(8,128)S(1)}, f32[24,128]{1,0:T(8,128)S(1)}, u32[]{:S(2)}, u32[]{:S(2)}) %collective-permute-start.14) | collective-permute-done | bytes 12320 | tf_op jit(solution)/shard_map/ppermute | solution.py:37
  90.6 0.1 collective-permute-start.26
  90.7 1.0 collective-permute-done.19
  91.8 2.2 %collective-permute-done.22 = bf16[1,1,2,2,48,896]{5,4,3,2,0,1:T(8,128)(2,1)S(1)} collective-permute-done((bf16[1,1,2,2,48,896]{5,4,3,2,0,1:T(8,128)(2,1)S(1)}, bf16[1,1,2,2,48,896]{5,4,3,2,0,1:T(8,128)(2,1)S(1)}, u32[]{:S(2)}, u32[]{:S(2)}) %collective-permute-start.22) | collective-permute-done | bytes 344096 | tf_op jit(solution)/shard_map/ppermute | solution.py:37
  94.1 1.7 %collective-permute-start.23 = (bf16[1,1,2,2,48,896]{5,4,3,2,1,0:T(8,128)(2,1)S(1)}, bf16[1,1,2,2,48,896]{5,4,3,2,1,0:T(8,128)(2,1)S(1)}, u32[]{:S(2)}, u32[]{:S(2)}) collective-permute-start(bf16[1,1,2,2,48,896]{5,4,3,2,1,0:T(8,128)(2,1)S(1)} %pad_maximum_fusion.3), channel_id=1, source_target_pairs={{0,4},{1,3},{2,6},{3,1},{4,0},{5,7},{6,2},{7,5},{8,12},{9,11},{10,... | collective-permute-start | bytes 1032200 | tf_op jit(solution)/shard_map/ppermute | solution.py:37
  95.8 1.0 collective-permute-start.28
  96.8 1.0 collective-permute-done.26
  97.9 0.1 pad_maximum_fusion.2
  98.0 0.8 collective-permute-start.29
  98.8 5.2 %collective-permute-done.23 = bf16[1,1,2,2,48,896]{5,4,3,2,1,0:T(8,128)(2,1)S(1)} collective-permute-done((bf16[1,1,2,2,48,896]{5,4,3,2,1,0:T(8,128)(2,1)S(1)}, bf16[1,1,2,2,48,896]{5,4,3,2,1,0:T(8,128)(2,1)S(1)}, u32[]{:S(2)}, u32[]{:S(2)}) %collective-permute-start.23) | collective-permute-done | bytes 344096 | tf_op jit(solution)/shard_map/ppermute | solution.py:37
  104.0 3.3 %collective-permute-start.27 = (bf16[1,2,2,2,48,896]{5,4,3,2,1,0:T(8,128)(2,1)S(1)}, bf16[1,2,2,2,48,896]{5,4,3,2,1,0:T(8,128)(2,1)}, u32[]{:S(2)}, u32[]{:S(2)}) collective-permute-start(bf16[1,2,2,2,48,896]{5,4,3,2,1,0:T(8,128)(2,1)S(1)} %pad_maximum_fusion.1), channel_id=1, source_target_pairs={{0,2},{1,5},{2,0},{3,7},{4,6},{5,1},{6,4},{7,3},{8,10},{9,13},{10,... | collective-permute-start | bytes 2064392 | tf_op jit(solution)/shard_map/ppermute | solution.py:37
  107.4 3.7 %collective-permute-done.15 = f32[24,128]{1,0:T(8,128)S(1)} collective-permute-done((f32[24,128]{1,0:T(8,128)S(1)}, f32[24,128]{1,0:T(8,128)S(1)}, u32[]{:S(2)}, u32[]{:S(2)}) %collective-permute-start.15) | collective-permute-done | bytes 12320 | tf_op jit(solution)/shard_map/ppermute | solution.py:37
  111.0 0.3 collective-permute-start.16
  111.4 4.3 %collective-permute-done.16 = f32[24,128]{1,0:T(8,128)S(1)} collective-permute-done((f32[24,128]{1,0:T(8,128)S(1)}, f32[24,128]{1,0:T(8,128)S(1)}, u32[]{:S(2)}, u32[]{:S(2)}) %collective-permute-start.16) | collective-permute-done | bytes 12320 | tf_op jit(solution)/shard_map/ppermute | solution.py:37
  115.8 1.0 collective-permute-done.24
  116.8 0.5 fusion.4
  118.1 2.5 %shard_map.89.start_ref = f32[576,128]{1,0:T(8,128)S(1)} custom-call(s32[9]{0:T(128)S(1)} %stack.128.where_ref, f32[1]{0:T(128)} %bitcast.35.coef_ref, f32[1,3584]{1,0:T(1,128)S(1)} %broadcast_in_dim.6.gain_ref, bf16[576,3584]{1,0:T(8,128)(2,1)} %bitcast.70, f32[576,128]{1,0:T(8,128)S(1)} %broadcast_in_dim.15.start_ref, ...), custom_call_target="tpu_custom_call" | custom-call | flops 8257536 | bytes 4128768 | tf_op jit(solution)/shard_map/pallas_call | solution.py:332
  120.6 3.8 %shard_map.90.mine_ref = f32[576,128]{1,0:T(8,128)} custom-call(s32[9]{0:T(128)S(1)} %stack.127.where_ref, f32[1]{0:T(128)} %bitcast.35.coef_ref, f32[1,3584]{1,0:T(1,128)S(1)} %broadcast_in_dim.6.gain_ref, bf16[576,3584]{1,0:T(8,128)(2,1)} %bitcast.71, f32[576,128]{1,0:T(8,128)S(1)} %shard_map.89.start_ref, bf16[2,4,48,896]{3,2,1,0:T(8,128)(2,1)} %bitcast.39.a_ref.rest_3_, ...), custom_call_target="tpu_custom_call" | custom-call | flops 8257536 | bytes 4128768 | tf_op jit(solution)/shard_map/pallas_call | solution.py:332
  124.4 0.2 collective-permute-start.30
  124.6 0.1 stack.126.where_ref
  124.7 1.7 %collective-permute-done.30.other_ref = f32[576,128]{1,0:T(8,128)} collective-permute-done((f32[576,128]{1,0:T(8,128)}, f32[576,128]{1,0:T(8,128)}, u32[]{:S(2)}, u32[]{:S(2)}) %collective-permute-start.30) | collective-permute-done | bytes 294944 | tf_op jit(solution)/shard_map/ppermute | solution.py:41
  126.4 4.9 %shard_map.91 = bf16[576,3584]{1,0:T(8,128)(2,1)} custom-call(s32[15]{0:T(128)S(1)} %stack.126.where_ref, f32[1]{0:T(128)} %bitcast.35.coef_ref, f32[1,3584]{1,0:T(1,128)S(1)} %broadcast_in_dim.6.gain_ref, bf16[576,3584]{1,0:T(8,128)(2,1)} %bitcast.72, f32[576,128]{1,0:T(8,128)} %shard_map.90.mine_ref, f32[576,128]{1,0:T(8,128)} %collective-permute-done.30.other_ref, ...), custom_call_target="tpu_custom_call" | custom-call | flops 16515072 | bytes 12386304 | tf_op jit(solution)/shard_map/pallas_call | solution.py:371
  (68 shorter events, 1.8 us)
Async XLA Ops:
  1.4 8.2 %copy-start.7 = (f32[512]{0:T(512)S(1)}, f32[512]{0:T(512)}, u32[]{:S(2)}) copy-start(f32[512]{0:T(512)} %param.12) | copy-start | bytes 6148
  1.4 10.5 %copy-start.2 = (s32[768,1]{0,1:T(1,128)S(1)}, s32[768,1]{0,1:T(1,128)}, u32[]{:S(2)}) copy-start(s32[768,1]{0,1:T(1,128)} %param.10) | copy-start | bytes 9220
  1.4 10.5 %copy-start.3 = (s32[1,8]{1,0:T(1,128)S(1)}, s32[1,8]{1,0:T(1,128)}, u32[]{:S(2)}) copy-start(s32[1,8]{1,0:T(1,128)} %param.9) | copy-start | bytes 100
  9.0 2.8 %collective-permute-start = (bf16[592,768]{1,0:T(8,128)(2,1)}, bf16[592,768]{1,0:T(8,128)(2,1)S(1)}, u32[]{:S(2)}, u32[]{:S(2)}) collective-permute-start(bf16[592,768]{1,0:T(8,128)(2,1)} %get-tuple-element.33), channel_id=1, source_target_pairs={{0,1},{1,0},{2,3},{3,2},{4,5},{5,4},{6,7},{7,6},{8,9},{9,8},{10,11... | collective-permute-start | bytes 2727944 | tf_op jit(solution)/shard_map/ppermute | solution.py:41
  11.9 13.2 %copy-start.6 = (f32[3584]{0:T(1024)S(1)}, f32[3584]{0:T(1024)}, u32[]{:S(2)}) copy-start(f32[3584]{0:T(1024)} %param.11) | copy-start | bytes 43012
  18.0 0.9 copy-start
  18.9 0.9 copy-start.4
  19.7 0.8 copy-start.5
  20.6 18.9 %collective-permute-start.5 = (bf16[1,2,2,2,48,896]{5,4,3,2,0,1:T(8,128)(2,1)}, bf16[1,2,2,2,48,896]{5,4,3,2,0,1:T(8,128)(2,1)S(1)}, u32[]{:S(2)}, u32[]{:S(2)}) collective-permute-start(bf16[1,2,2,2,48,896]{5,4,3,2,0,1:T(8,128)(2,1)} %bitcast.21), channel_id=1, source_target_pairs={{0,8},{1,9},{2,10},{3,11},{4,12},{5,13},{6,14},{7,15},{8,0},{9,1},... | collective-permute-start | bytes 2064392 | tf_op jit(solution)/shard_map/ppermute | solution.py:37
  23.5 17.9 %collective-permute-start.1 = (bf16[1,2,2,2,48,896]{5,4,3,2,1,0:T(8,128)(2,1)}, bf16[1,2,2,2,48,896]{5,4,3,2,1,0:T(8,128)(2,1)S(1)}, u32[]{:S(2)}, u32[]{:S(2)}) collective-permute-start(bf16[1,2,2,2,48,896]{5,4,3,2,1,0:T(8,128)(2,1)} %bitcast.68), channel_id=1, source_target_pairs={{0,2},{1,5},{2,0},{3,7},{4,6},{5,1},{6,4},{7,3},{8,10},{9,13},{10,... | collective-permute-start | bytes 2064392 | tf_op jit(solution)/shard_map/ppermute | solution.py:37
  25.2 18.0 %collective-permute-start.4 = (bf16[1,2,2,2,48,896]{5,4,3,2,0,1:T(8,128)(2,1)}, bf16[1,2,2,2,48,896]{5,4,3,2,0,1:T(8,128)(2,1)S(1)}, u32[]{:S(2)}, u32[]{:S(2)}) collective-permute-start(bf16[1,2,2,2,48,896]{5,4,3,2,0,1:T(8,128)(2,1)} %bitcast.67), channel_id=1, source_target_pairs={{0,2},{1,5},{2,0},{3,7},{4,6},{5,1},{6,4},{7,3},{8,10},{9,13},{10,... | collective-permute-start | bytes 2064392 | tf_op jit(solution)/shard_map/ppermute | solution.py:37
  25.7 1.2 copy-start.1
  39.7 11.0 %collective-permute-start.10 = (bf16[1,1,2,2,48,896]{5,4,3,2,0,1:T(8,128)(2,1)S(1)}, bf16[1,1,2,2,48,896]{5,4,3,2,0,1:T(8,128)(2,1)S(1)}, u32[]{:S(2)}, u32[]{:S(2)}) collective-permute-start(bf16[1,1,2,2,48,896]{5,4,3,2,0,1:T(8,128)(2,1)S(1)} %slice.89), channel_id=1, source_target_pairs={{0,2},{1,5},{2,0},{3,7},{4,6},{5,1},{6,4},{7,3},{8,10},{9,13},{10,... | collective-permute-start | bytes 1032200 | tf_op jit(solution)/shard_map/ppermute | solution.py:37
  41.6 10.4 %collective-permute-start.2 = (bf16[1,1,2,2,48,896]{5,4,3,2,1,0:T(8,128)(2,1)S(1)}, bf16[1,1,2,2,48,896]{5,4,3,2,1,0:T(8,128)(2,1)S(1)}, u32[]{:S(2)}, u32[]{:S(2)}) collective-permute-start(bf16[1,1,2,2,48,896]{5,4,3,2,1,0:T(8,128)(2,1)S(1)} %slice.77), channel_id=1, source_target_pairs={{0,4},{1,3},{2,6},{3,1},{4,0},{5,7},{6,2},{7,5},{8,12},{9,11},{10,... | collective-permute-start | bytes 1032200 | tf_op jit(solution)/shard_map/ppermute | solution.py:37
  43.4 11.1 %collective-permute-start.6 = (bf16[1,1,2,2,48,896]{5,4,3,2,0,1:T(8,128)(2,1)S(1)}, bf16[1,1,2,2,48,896]{5,4,3,2,0,1:T(8,128)(2,1)S(1)}, u32[]{:S(2)}, u32[]{:S(2)}) collective-permute-start(bf16[1,1,2,2,48,896]{5,4,3,2,0,1:T(8,128)(2,1)S(1)} %slice.83), channel_id=1, source_target_pairs={{0,8},{1,9},{2,10},{3,11},{4,12},{5,13},{6,14},{7,15},{8,0},{9,1},... | collective-permute-start | bytes 1032200 | tf_op jit(solution)/shard_map/ppermute | solution.py:37
  50.8 5.5 %collective-permute-start.11 = (bf16[1,1,1,2,48,896]{5,4,3,2,0,1:T(8,128)(2,1)S(1)}, bf16[1,1,1,2,48,896]{5,4,3,2,0,1:T(8,128)(2,1)S(1)}, u32[]{:S(2)}, u32[]{:S(2)}) collective-permute-start(bf16[1,1,1,2,48,896]{5,4,3,2,0,1:T(8,128)(2,1)S(1)} %slice.91), channel_id=1, source_target_pairs={{0,4},{1,3},{2,6},{3,1},{4,0},{5,7},{6,2},{7,5},{8,12},{9,11},{10,... | collective-permute-start | bytes 516104 | tf_op jit(solution)/shard_map/ppermute | solution.py:37
  52.1 12.5 %collective-permute-start.3 = (bf16[1,1,1,2,48,896]{5,4,3,2,1,0:T(8,128)(2,1)S(1)}, bf16[1,1,1,2,48,896]{5,4,3,2,1,0:T(8,128)(2,1)S(1)}, u32[]{:S(2)}, u32[]{:S(2)}) collective-permute-start(bf16[1,1,1,2,48,896]{5,4,3,2,1,0:T(8,128)(2,1)S(1)} %slice.79), channel_id=1, source_target_pairs={{0,16},{1,17},{2,18},{3,19},{4,20},{5,21},{6,22},{7,23},{8,24},{9,... | collective-permute-start | bytes 516104 | tf_op jit(solution)/shard_map/ppermute | solution.py:37
  54.6 10.0 %collective-permute-start.7 = (bf16[1,1,1,2,48,896]{5,4,3,2,0,1:T(8,128)(2,1)S(1)}, bf16[1,1,1,2,48,896]{5,4,3,2,0,1:T(8,128)(2,1)S(1)}, u32[]{:S(2)}, u32[]{:S(2)}) collective-permute-start(bf16[1,1,1,2,48,896]{5,4,3,2,0,1:T(8,128)(2,1)S(1)} %slice.85), channel_id=1, source_target_pairs={{0,4},{1,3},{2,6},{3,1},{4,0},{5,7},{6,2},{7,5},{8,12},{9,11},{10,... | collective-permute-start | bytes 516104 | tf_op jit(solution)/shard_map/ppermute | solution.py:37
  56.3 12.5 %collective-permute-start.12 = (bf16[1,1,1,1,48,896]{5,4,3,2,0,1:T(8,128)(2,1)S(1)}, bf16[1,1,1,1,48,896]{5,4,3,2,0,1:T(8,128)(2,1)S(1)}, u32[]{:S(2)}, u32[]{:S(2)}) collective-permute-start(bf16[1,1,1,1,48,896]{5,4,3,2,0,1:T(8,128)(2,1)S(1)} %slice.93), channel_id=1, source_target_pairs={{0,16},{1,17},{2,18},{3,19},{4,20},{5,21},{6,22},{7,23},{8,24},{9,... | collective-permute-start | bytes 258056 | tf_op jit(solution)/shard_map/ppermute | solution.py:37
  64.7 7.2 %collective-permute-start.9 = (bf16[1,1,1,1,48,896]{5,4,3,2,0,1:T(8,128)(2,1)S(1)}, bf16[1,1,1,1,48,896]{5,4,3,2,0,1:T(8,128)(2,1)S(1)}, u32[]{:S(2)}, u32[]{:S(2)}) collective-permute-start(bf16[1,1,1,1,48,896]{5,4,3,2,0,1:T(8,128)(2,1)S(1)} %slice.87), channel_id=1, source_target_pairs={{0,16},{1,17},{2,18},{3,19},{4,20},{5,21},{6,22},{7,23},{8,24},{9,... | collective-permute-start | bytes 258056 | tf_op jit(solution)/shard_map/ppermute | solution.py:37
  64.8 8.2 %collective-permute-start.8 = (bf16[1,1,1,1,48,896]{5,4,3,2,1,0:T(8,128)(2,1)S(1)}, bf16[1,1,1,1,48,896]{5,4,3,2,1,0:T(8,128)(2,1)S(1)}, u32[]{:S(2)}, u32[]{:S(2)}) collective-permute-start(bf16[1,1,1,1,48,896]{5,4,3,2,1,0:T(8,128)(2,1)S(1)} %slice.81), channel_id=1, source_target_pairs={{0,8},{1,9},{2,10},{3,11},{4,12},{5,13},{6,14},{7,15},{8,0},{9,1},... | collective-permute-start | bytes 258056 | tf_op jit(solution)/shard_map/ppermute | solution.py:37
  69.5 11.2 %collective-permute-start.18 = (bf16[1,1,1,1,48,896]{5,4,3,2,0,1:T(8,128)(2,1)S(1)}, bf16[1,1,1,1,48,896]{5,4,3,2,0,1:T(8,128)(2,1)S(1)}, u32[]{:S(2)}, u32[]{:S(2)}) collective-permute-start(bf16[1,1,1,1,48,896]{5,4,3,2,0,1:T(8,128)(2,1)S(1)} %get-tuple-element.53), channel_id=1, source_target_pairs={{0,16},{1,17},{2,18},{3,19},{4,20},{5,21},{6,22},{7,23},{8,24},{9,... | collective-permute-start | bytes 258056 | tf_op jit(solution)/shard_map/ppermute | solution.py:37
  72.6 7.1 %collective-permute-start.20 = (bf16[1,1,1,1,48,896]{5,4,3,2,0,1:T(8,128)(2,1)S(1)}, bf16[1,1,1,1,48,896]{5,4,3,2,0,1:T(8,128)(2,1)S(1)}, u32[]{:S(2)}, u32[]{:S(2)}) collective-permute-start(bf16[1,1,1,1,48,896]{5,4,3,2,0,1:T(8,128)(2,1)S(1)} %get-tuple-element.55), channel_id=1, source_target_pairs={{0,16},{1,17},{2,18},{3,19},{4,20},{5,21},{6,22},{7,23},{8,24},{9,... | collective-permute-start | bytes 258056 | tf_op jit(solution)/shard_map/ppermute | solution.py:37
  75.6 11.2 %collective-permute-start.13 = (f32[24,128]{1,0:T(8,128)S(1)}, f32[24,128]{1,0:T(8,128)S(1)}, u32[]{:S(2)}, u32[]{:S(2)}) collective-permute-start(f32[24,128]{1,0:T(8,128)S(1)} %concatenate.30), channel_id=1, source_target_pairs={{0,2},{1,5},{2,0},{3,7},{4,6},{5,1},{6,4},{7,3},{8,10},{9,13},{10,... | collective-permute-start | bytes 36872 | tf_op jit(solution)/shard_map/ppermute | solution.py:37
  77.1 4.5 %collective-permute-start.17 = (bf16[1,1,1,1,48,896]{5,4,3,2,1,0:T(8,128)(2,1)S(1)}, bf16[1,1,1,1,48,896]{5,4,3,2,1,0:T(8,128)(2,1)S(1)}, u32[]{:S(2)}, u32[]{:S(2)}) collective-permute-start(bf16[1,1,1,1,48,896]{5,4,3,2,1,0:T(8,128)(2,1)S(1)} %get-tuple-element.52), channel_id=1, source_target_pairs={{0,8},{1,9},{2,10},{3,11},{4,12},{5,13},{6,14},{7,15},{8,0},{9,1},... | collective-permute-start | bytes 258056 | tf_op jit(solution)/shard_map/ppermute | solution.py:37
  79.7 5.5 %collective-permute-start.21 = (bf16[1,1,1,2,48,896]{5,4,3,2,0,1:T(8,128)(2,1)S(1)}, bf16[1,1,1,2,48,896]{5,4,3,2,0,1:T(8,128)(2,1)S(1)}, u32[]{:S(2)}, u32[]{:S(2)}) collective-permute-start(bf16[1,1,1,2,48,896]{5,4,3,2,0,1:T(8,128)(2,1)S(1)} %pad_maximum_fusion.8), channel_id=1, source_target_pairs={{0,4},{1,3},{2,6},{3,1},{4,0},{5,7},{6,2},{7,5},{8,12},{9,11},{10,... | collective-permute-start | bytes 516104 | tf_op jit(solution)/shard_map/ppermute | solution.py:37
  80.7 9.9 %collective-permute-start.25 = (bf16[1,1,1,2,48,896]{5,4,3,2,0,1:T(8,128)(2,1)S(1)}, bf16[1,1,1,2,48,896]{5,4,3,2,0,1:T(8,128)(2,1)S(1)}, u32[]{:S(2)}, u32[]{:S(2)}) collective-permute-start(bf16[1,1,1,2,48,896]{5,4,3,2,0,1:T(8,128)(2,1)S(1)} %pad_maximum_fusion.7), channel_id=1, source_target_pairs={{0,8},{1,9},{2,10},{3,11},{4,12},{5,13},{6,14},{7,15},{8,0},{9,1},... | collective-permute-start | bytes 516104 | tf_op jit(solution)/shard_map/ppermute | solution.py:37
  81.6 10.1 %collective-permute-start.19 = (bf16[1,1,1,2,48,896]{5,4,3,2,1,0:T(8,128)(2,1)S(1)}, bf16[1,1,1,2,48,896]{5,4,3,2,1,0:T(8,128)(2,1)S(1)}, u32[]{:S(2)}, u32[]{:S(2)}) collective-permute-start(bf16[1,1,1,2,48,896]{5,4,3,2,1,0:T(8,128)(2,1)S(1)} %pad_maximum_fusion.6), channel_id=1, source_target_pairs={{0,16},{1,17},{2,18},{3,19},{4,20},{5,21},{6,22},{7,23},{8,24},{9,... | collective-permute-start | bytes 516104 | tf_op jit(solution)/shard_map/ppermute | solution.py:37
  85.3 8.7 %collective-permute-start.22 = (bf16[1,1,2,2,48,896]{5,4,3,2,0,1:T(8,128)(2,1)S(1)}, bf16[1,1,2,2,48,896]{5,4,3,2,0,1:T(8,128)(2,1)S(1)}, u32[]{:S(2)}, u32[]{:S(2)}) collective-permute-start(bf16[1,1,2,2,48,896]{5,4,3,2,0,1:T(8,128)(2,1)S(1)} %pad_maximum_fusion.4), channel_id=1, source_target_pairs={{0,2},{1,5},{2,0},{3,7},{4,6},{5,1},{6,4},{7,3},{8,10},{9,13},{10,... | collective-permute-start | bytes 1032200 | tf_op jit(solution)/shard_map/ppermute | solution.py:37
  86.8 3.7 %collective-permute-start.14 = (f32[24,128]{1,0:T(8,128)S(1)}, f32[24,128]{1,0:T(8,128)S(1)}, u32[]{:S(2)}, u32[]{:S(2)}) collective-permute-start(f32[24,128]{1,0:T(8,128)S(1)} %pad_add_fusion), channel_id=1, source_target_pairs={{0,4},{1,3},{2,6},{3,1},{4,0},{5,7},{6,2},{7,5},{8,12},{9,11},{10,... | collective-permute-start | bytes 36872 | tf_op jit(solution)/shard_map/ppermute | solution.py:37
  90.6 7.3 %collective-permute-start.26 = (bf16[2,1,1,2,48,896]{5,4,3,2,0,1:T(8,128)(2,1)S(1)}, bf16[2,1,1,2,48,896]{5,4,3,2,0,1:T(8,128)(2,1)S(1)}, u32[]{:S(2)}, u32[]{:S(2)}) collective-permute-start(bf16[2,1,1,2,48,896]{5,4,3,2,0,1:T(8,128)(2,1)S(1)} %pad_maximum_fusion.5), channel_id=1, source_target_pairs={{0,4},{1,3},{2,6},{3,1},{4,0},{5,7},{6,2},{7,5},{8,12},{9,11},{10,... | collective-permute-start | bytes 1032200 | tf_op jit(solution)/shard_map/ppermute | solution.py:37
  94.1 9.9 %collective-permute-start.23 = (bf16[1,1,2,2,48,896]{5,4,3,2,1,0:T(8,128)(2,1)S(1)}, bf16[1,1,2,2,48,896]{5,4,3,2,1,0:T(8,128)(2,1)S(1)}, u32[]{:S(2)}, u32[]{:S(2)}) collective-permute-start(bf16[1,1,2,2,48,896]{5,4,3,2,1,0:T(8,128)(2,1)S(1)} %pad_maximum_fusion.3), channel_id=1, source_target_pairs={{0,4},{1,3},{2,6},{3,1},{4,0},{5,7},{6,2},{7,5},{8,12},{9,11},{10,... | collective-permute-start | bytes 1032200 | tf_op jit(solution)/shard_map/ppermute | solution.py:37
  95.8 24.8 %collective-permute-start.28 = (bf16[2,1,2,2,48,896]{5,4,3,2,0,1:T(8,128)(2,1)S(1)}, bf16[2,1,2,2,48,896]{5,4,3,2,0,1:T(8,128)(2,1)S(1)}, u32[]{:S(2)}, u32[]{:S(2)}) collective-permute-start(bf16[2,1,2,2,48,896]{5,4,3,2,0,1:T(8,128)(2,1)S(1)} %pad_maximum_fusion), channel_id=1, source_target_pairs={{0,8},{1,9},{2,10},{3,11},{4,12},{5,13},{6,14},{7,15},{8,0},{9,1},... | collective-permute-start | bytes 2064392 | tf_op jit(solution)/shard_map/ppermute | solution.py:37
  98.0 22.6 %collective-permute-start.29 = (bf16[2,1,2,2,48,896]{5,4,3,2,0,1:T(8,128)(2,1)S(1)}, bf16[2,1,2,2,48,896]{5,4,3,2,0,1:T(8,128)(2,1)S(1)}, u32[]{:S(2)}, u32[]{:S(2)}) collective-permute-start(bf16[2,1,2,2,48,896]{5,4,3,2,0,1:T(8,128)(2,1)S(1)} %pad_maximum_fusion.2), channel_id=1, source_target_pairs={{0,2},{1,5},{2,0},{3,7},{4,6},{5,1},{6,4},{7,3},{8,10},{9,13},{10,... | collective-permute-start | bytes 2064392 | tf_op jit(solution)/shard_map/ppermute | solution.py:37
  104.0 16.5 %collective-permute-start.27 = (bf16[1,2,2,2,48,896]{5,4,3,2,1,0:T(8,128)(2,1)S(1)}, bf16[1,2,2,2,48,896]{5,4,3,2,1,0:T(8,128)(2,1)}, u32[]{:S(2)}, u32[]{:S(2)}) collective-permute-start(bf16[1,2,2,2,48,896]{5,4,3,2,1,0:T(8,128)(2,1)S(1)} %pad_maximum_fusion.1), channel_id=1, source_target_pairs={{0,2},{1,5},{2,0},{3,7},{4,6},{5,1},{6,4},{7,3},{8,10},{9,13},{10,... | collective-permute-start | bytes 2064392 | tf_op jit(solution)/shard_map/ppermute | solution.py:37
  107.3 3.7 %collective-permute-start.15 = (f32[24,128]{1,0:T(8,128)S(1)}, f32[24,128]{1,0:T(8,128)S(1)}, u32[]{:S(2)}, u32[]{:S(2)}) collective-permute-start(f32[24,128]{1,0:T(8,128)S(1)} %add.114), channel_id=1, source_target_pairs={{0,8},{1,9},{2,10},{3,11},{4,12},{5,13},{6,14},{7,15},{8,0},{9,1},... | collective-permute-start | bytes 36872 | tf_op jit(solution)/shard_map/ppermute | solution.py:37
  111.0 4.6 %collective-permute-start.16 = (f32[24,128]{1,0:T(8,128)S(1)}, f32[24,128]{1,0:T(8,128)S(1)}, u32[]{:S(2)}, u32[]{:S(2)}) collective-permute-start(f32[24,128]{1,0:T(8,128)S(1)} %add.115), channel_id=1, source_target_pairs={{0,16},{1,17},{2,18},{3,19},{4,20},{5,21},{6,22},{7,23},{8,24},{9,... | collective-permute-start | bytes 36872 | tf_op jit(solution)/shard_map/ppermute | solution.py:37
  115.6 1.2 collective-permute-start.24
  124.4 2.0 %collective-permute-start.30 = (f32[576,128]{1,0:T(8,128)}, f32[576,128]{1,0:T(8,128)}, u32[]{:S(2)}, u32[]{:S(2)}) collective-permute-start(f32[576,128]{1,0:T(8,128)} %shard_map.90.mine_ref), channel_id=1, source_target_pairs={{0,1},{1,0},{2,3},{3,2},{4,5},{5,4},{6,7},{7,6},{8,9},{9,8},{10,11... | collective-permute-start | bytes 884744 | tf_op jit(solution)/shard_map/ppermute | solution.py:41

commit v4 on v3

--- a/solution.py
+++ b/solution.py
@@ -62,8 +62,12 @@
     return row_terms, jnp.concatenate([d_c, weight_f[None, :] * res_r], axis=0)
 
 
+def gain_slice(gain_ref, first, count):
+    return jnp.concatenate([gain_ref[pl.ds(first // 128 + c, 1)] for c in range(count // 128)], axis=1)
+
+
 def forward_kernel(
-    chunks, x_hbm, w_hbm, gain_ref, part_ref, sent_ref, sq_ref, x_ref, w_ref, sems
+    chunks, x_hbm, w_hbm, gain_hbm, part_ref, sent_ref, sq_ref, x_ref, w_ref, gain_ref, sems, gain_sem
 ):
     rows, feat = x_ref.shape
     width = w_ref.shape[0]
@@ -75,15 +79,18 @@
         copies.append(
             [pltpu.make_async_copy(a.at[:, span], b.at[:, span], sems.at[n, k]) for n, (a, b) in enumerate(pairs)]
         )
+    gains = pltpu.make_async_copy(gain_hbm, gain_ref, gain_sem)
+    gains.start()
     for pair in copies:
         for copy in pair:
             copy.start()
+    gains.wait()
     sq = None
     for k in range(chunks):
         span = slice(k * cols, (k + 1) * cols)
         for copy in copies[k]:
             copy.wait()
-        gained = (w_ref[:, span].astype(F32) * gain_ref[:, span]).astype(BF16)
+        gained = (w_ref[:, span].astype(F32) * gain_slice(gain_ref, k * cols, cols)).astype(BF16)
         x = x_ref[:, span]
         part = lax.dot_general(gained, x, (((1,), (1,)), ((), ())), preferred_element_type=F32)
         if k > 0:
@@ -134,12 +141,12 @@
     return pltpu.CompilerParams(vmem_limit_bytes=mib * 1024 * 1024)
 
 
-def forward(x, w_t, gain_row):
+def forward(x, w_t, gains):
     rows, feat = x.shape
     width = w_t.shape[0]
     return pl.pallas_call(
         functools.partial(forward_kernel, 2),
-        in_specs=[far(), far(), whole()],
+        in_specs=[far(), far(), far()],
         out_specs=[whole()] * 3,
         out_shape=[
             jax.ShapeDtypeStruct((width, rows), F32),
@@ -149,11 +156,13 @@
         scratch_shapes=[
             pltpu.VMEM(x.shape, BF16),
             pltpu.VMEM(w_t.shape, BF16),
+            pltpu.VMEM(gains.shape, F32),
             pltpu.SemaphoreType.DMA((2, 2)),
+            pltpu.SemaphoreType.DMA,
         ],
         compiler_params=vmem_limit(24),
         cost_estimate=pl.CostEstimate(flops=2 * rows * feat * width, bytes_accessed=10_000_000, transcendentals=0),
-    )(in_hbm(x), in_hbm(w_t), gain_row)
+    )(in_hbm(x), in_hbm(w_t), in_hbm(gains))
 
 
 def head_kernel(
@@ -168,14 +177,19 @@
     dest_ref,
     gain_ref,
     x_hbm,
+    d_hbm,
+    loss_ref,
+    a_hbm,
+    b_hbm,
+    c_hbm,
+    target_ref,
+    x_ref,
     d_ref,
-    loss_ref,
     a_ref,
     b_ref,
     c_ref,
-    target_ref,
-    x_ref,
     sems,
+    out_sems,
 ):
     t_copy = pltpu.make_async_copy(t_hbm, target_ref, sems.at[0])
     x_copy = pltpu.make_async_copy(x_hbm, x_ref, sems.at[1])
@@ -229,11 +243,23 @@
         for c in range(0, lanes, 128):
             sums = named[:, c : c + 128] if sums is None else sums + named[:, c : c + 128]
     loss_ref[...] = jnp.broadcast_to(jnp.sum(sums, axis=1, keepdims=True), loss_ref.shape)
+    d_copy = pltpu.make_async_copy(d_ref, d_hbm, sems.at[2])
+    d_copy.start()
     x_copy.wait()
-    grad_halves(where_ref, d_ref, x_ref, (a_ref, b_ref, c_ref))
-
-
-def grad_halves(where_ref, d_ref, x_ref, out_refs):
+    copies = []
+
+    def send(chain, half, slot):
+        near, away = (a_ref, b_ref, c_ref)[chain], (a_hbm, b_hbm, c_hbm)[chain]
+        copies.append(pltpu.make_async_copy(near.at[half], away.at[slot], out_sems.at[chain, half]))
+        copies[-1].start()
+
+    grad_halves(where_ref, d_ref, x_ref, (a_ref, b_ref, c_ref), send)
+    for copy in copies:
+        copy.wait()
+    d_copy.wait()
+
+
+def grad_halves(where_ref, d_ref, x_ref, out_refs, send=None):
     blocks, blk, rows = d_ref.shape
     cols = out_refs[0].shape[-1]
     for first, count in ((2, 1), (0, 2)):
@@ -243,7 +269,10 @@
             out = jnp.dot(lhs, x_ref[:, pl.ds(col, cols)], preferred_element_type=F32).astype(BF16)
             for c in range(count):
                 part = out[c * 4 * blk : (c + 1) * 4 * blk]
-                out_refs[first + c][i ^ where_ref[2 * (first + c) + 1]] = part.reshape(4, blk, cols)
+                slot = i ^ where_ref[2 * (first + c) + 1]
+                out_refs[first + c][i if send else slot] = part.reshape(4, blk, cols)
+                if send:
+                    send(first + c, i, slot)
 
 
 def head_call(part, got, sq, targets_t, dest_row, lengths, gain_col, x, where, row_masks, model_width, trainers):
@@ -252,26 +281,34 @@
     return pl.pallas_call(
         functools.partial(head_kernel, model_width),
         in_specs=[scalars()] * 3 + [whole()] * 3 + [far()] + [whole()] * 2 + [far()],
-        out_specs=[whole()] * 5,
+        out_specs=[far(), whole(), far(), far(), far()],
         out_shape=[
-            jax.ShapeDtypeStruct((12, blk, rows), BF16),
+            pltpu.HBM((12, blk, rows), BF16),
             jax.ShapeDtypeStruct((trainers, 128), F32),
         ]
-        + [jax.ShapeDtypeStruct((2, 4, blk, cols), BF16)] * 3,
+        + [pltpu.HBM((2, 4, blk, cols), BF16)] * 3,
         scratch_shapes=[
             pltpu.VMEM(targets_t.shape, BF16),
             pltpu.VMEM(x.shape, BF16),
-            pltpu.SemaphoreType.DMA((2,)),
+            pltpu.VMEM((12, blk, rows), BF16),
+        ]
+        + [pltpu.VMEM((2, 4, blk, cols), BF16)] * 3
+        + [
+            pltpu.SemaphoreType.DMA((3,)),
+            pltpu.SemaphoreType.DMA((3, 2)),
         ],
         compiler_params=vmem_limit(24),
         cost_estimate=pl.CostEstimate(flops=width * rows * cols * 4, bytes_accessed=12_000_000, transcendentals=0),
     )(where, row_masks, lengths, part, got, sq, in_hbm(targets_t), dest_row, gain_col, in_hbm(x))
 
 
-def keep_kernel(where_ref, d_ref, x_hbm, a_ref, b_ref, c_ref, x_ref, sem):
-    copy = pltpu.make_async_copy(x_hbm, x_ref, sem)
-    copy.start()
-    copy.wait()
+def keep_kernel(where_ref, d_hbm, x_hbm, a_ref, b_ref, c_ref, d_ref, x_ref, sems):
+    d_copy = pltpu.make_async_copy(d_hbm, d_ref, sems.at[0])
+    x_copy = pltpu.make_async_copy(x_hbm, x_ref, sems.at[1])
+    d_copy.start()
+    x_copy.start()
+    d_copy.wait()
+    x_copy.wait()
     grad_halves(where_ref, d_ref, x_ref, (a_ref, b_ref, c_ref))
 
 
@@ -279,13 +316,13 @@
     blk, cols = d.shape[1], x.shape[1] // 4
     return pl.pallas_call(
         keep_kernel,
-        in_specs=[scalars(), whole(), far()],
+        in_specs=[scalars(), far(), far()],
         out_specs=[whole()] * 3,
         out_shape=[jax.ShapeDtypeStruct((2, 4, blk, cols), BF16)] * 3,
-        scratch_shapes=[pltpu.VMEM(x.shape, BF16), pltpu.SemaphoreType.DMA],
+        scratch_shapes=[pltpu.VMEM(d.shape, BF16), pltpu.VMEM(x.shape, BF16), pltpu.SemaphoreType.DMA((2,))],
         compiler_params=vmem_limit(24),
         cost_estimate=pl.CostEstimate(flops=12 * blk * d.shape[2] * cols * 4, bytes_accessed=10_000_000, transcendentals=0),
-    )(where, d, in_hbm(x))
+    )(where, in_hbm(d), in_hbm(x))
 
 
 def w_copies(where_ref, w_hbm, w_buf, sem, count):
@@ -300,60 +337,71 @@
     return copies
 
 
-def updated_block(where_ref, coef_ref, gain_ref, w_buf, g_ref, s, j, mask):
+def step_size(entries, mine_ref, other_ref):
+    return RATE * lax.rsqrt((mine_ref[16:17] + other_ref[16:17]) / entries + EPS)
+
+
+def factors(where_ref, coef, gain_ref, s, cols):
+    return jnp.concatenate([coef] * (cols // 128), axis=1) * gain_slice(gain_ref, where_ref[s] * cols, cols)
+
+
+def updated_block(factor, w_buf, g_ref, s, j, mask):
     blk, cols = g_ref.shape[2:]
-    col = pl.multiple_of(where_ref[s] * cols, 128)
-    factor = coef_ref[0] * gain_ref[:, pl.ds(col, cols)]
     g = g_ref[s % 2, j ^ mask].astype(F32)
     return w_buf[s, j * blk : (j + 1) * blk].astype(F32) - factor * g
 
 
-def top_kernel(where_ref, coef_ref, gain_ref, w_hbm, start_ref, a_ref, b_ref, c_ref, out_ref, w_buf, sem):
-    copies = w_copies(where_ref, w_hbm, w_buf, sem, 6)
-    blk, cols = a_ref.shape[2:]
-    for s in range(6):
-        chain = s // 2
+def top_kernel(entries, where_ref, sum_ref, sum2_ref, gain_ref, w_hbm, *rest):
+    g_refs, (out_ref, w_buf, sem) = rest[:6], rest[6:]
+    copies = w_copies(where_ref, w_hbm, w_buf, sem, 12)
+    blk, cols = g_refs[0].shape[2:]
+    coef = step_size(entries, sum_ref, sum2_ref)
+    for s in range(12):
+        chain = (s % 6) // 2
+        factor = factors(where_ref, coef, gain_ref, s, cols)
         copies[s].wait()
         for j in range(4):
-            g_ref = (a_ref, b_ref, c_ref)[chain]
-            size = jnp.abs(
-                updated_block(where_ref, coef_ref, gain_ref, w_buf, g_ref, s, j, where_ref[6 + chain])
-            )
+            g_ref = g_refs[3 * (s // 6) + chain]
+            size = jnp.abs(updated_block(factor, w_buf, g_ref, s, j, where_ref[12 + chain]))
             here = slice((chain * 4 + j) * blk, (chain * 4 + j + 1) * blk)
-            top = start_ref[here] if s % 2 == 0 else out_ref[here]
-            for k in range(cols // 128):
+            top = size[:, :128]
+            for k in range(1, cols // 128):
                 top = jnp.maximum(top, size[:, k * 128 : (k + 1) * 128])
+            if s > 5 or s % 2 > 0:
+                top = jnp.maximum(top, out_ref[here])
             out_ref[here] = top
 
 
-def top_part(pieces, w_t, gain_row, coef, start, columns, row_masks):
+def top_all(entries, pieces, w_t, gains, sums, columns, row_masks):
     blk, cols = pieces[0].shape[-2:]
     where = jnp.stack([*columns, *row_masks]).astype(jnp.int32)
     return pl.pallas_call(
-        top_kernel,
-        in_specs=[scalars(), scalars(), whole(), far()] + [whole()] * 4,
+        functools.partial(top_kernel, entries),
+        in_specs=[scalars(), whole(), whole(), whole(), far()] + [whole()] * 6,
         out_specs=whole(),
         out_shape=jax.ShapeDtypeStruct((w_t.shape[0], 128), F32),
-        scratch_shapes=[pltpu.VMEM((6, 4 * blk, cols), BF16), pltpu.SemaphoreType.DMA((6,))],
-        compiler_params=vmem_limit(24),
-        cost_estimate=pl.CostEstimate(flops=4 * w_t.size, bytes_accessed=2 * w_t.size, transcendentals=0),
-    )(where, coef, gain_row, in_hbm(w_t), start, *pieces)
-
-
-def code_kernel(where_ref, coef_ref, gain_ref, w_hbm, mine_ref, other_ref, *rest):
+        scratch_shapes=[pltpu.VMEM((12, 4 * blk, cols), BF16), pltpu.SemaphoreType.DMA((12,))],
+        compiler_params=vmem_limit(20),
+        cost_estimate=pl.CostEstimate(flops=4 * w_t.size, bytes_accessed=4 * w_t.size, transcendentals=0),
+    )(where, *sums, gains, in_hbm(w_t), *pieces)
+
+
+def code_kernel(entries, where_ref, sum_ref, sum2_ref, gain_ref, w_hbm, mine_ref, other_ref, *rest):
     g_refs, (out_ref, buf, w_buf, inv_ref, sem, w_sem) = rest[:6], rest[6:]
     loads = w_copies(where_ref, w_hbm, w_buf, w_sem, 12)
     blk, cols = g_refs[0].shape[2:]
     rows = 4 * blk
     top = jnp.max(jnp.maximum(mine_ref[...], other_ref[...]), axis=1, keepdims=True)
     inv_ref[...] = jnp.broadcast_to(1.0 / (top + EPS), inv_ref.shape)
+    coef = step_size(entries, sum_ref, sum2_ref)
     copies = []
     for s in range(12):
         chain = (s % 6) // 2
         g_ref = g_refs[3 * (s // 6) + chain]
+        factor = factors(where_ref, coef, gain_ref, s, cols)
         loads[s].wait()
         for j in range(4):
-            new = updated_block(where_ref, coef_ref, gain_ref, w_buf, g_ref, s, j, where_ref[12 + chain])
+            new = updated_block(factor, w_buf, g_ref, s, j, where_ref[12 + chain])
             first = chain * rows + j * blk
             inv = jnp.concatenate([inv_ref[first : first + blk]] * (cols // 128), axis=1)
             buf[s, j * blk : (j + 1) * blk] = (new * inv).astype(BF16)
@@ -365,12 +413,12 @@
         copy.wait()
 
 
-def code_all(pieces, w_t, gain_row, coef, mine, other, columns, row_masks):
+def code_all(entries, pieces, w_t, gains, sums, mine, other, columns, row_masks):
     blk, cols = pieces[0].shape[-2:]
     where = jnp.stack([*columns, *row_masks]).astype(jnp.int32)
     return pl.pallas_call(
-        code_kernel,
-        in_specs=[scalars(), scalars(), whole(), far()] + [whole()] * 8,
+        functools.partial(code_kernel, entries),
+        in_specs=[scalars(), whole(), whole(), whole(), far()] + [whole()] * 8,
         out_specs=far(),
         out_shape=jax.ShapeDtypeStruct(w_t.shape, BF16),
         scratch_shapes=[
@@ -382,7 +430,7 @@
         ],
         compiler_params=vmem_limit(24),
         cost_estimate=pl.CostEstimate(flops=8 * w_t.size, bytes_accessed=6 * w_t.size, transcendentals=0),
-    )(where, coef, gain_row, in_hbm(w_t), mine, other, *pieces)
+    )(where, *sums, gains, in_hbm(w_t), mine, other, *pieces)
 
 
 def paired_shards(hidden, targets, group_lengths, dest_ids, input_gain, latent_gain, kv_weight):
@@ -403,8 +451,8 @@
     row_masks = [b[2] * 2 + b[3] for b in bits]
 
     w_t = kv_weight.T
-    gain_row = input_gain[None, :]
-    part, sent, squares = forward(hidden, w_t, gain_row)
+    gains = input_gain.reshape(feat // 128, 128)
+    part, sent, squares = forward(hidden, w_t, gains)
     got = swap_cores(sent)
     give = jnp.stack([v for b in bits for v in (1 - b[0], b[1])]).astype(jnp.int32)
     take = jnp.stack([v for b in bits for v in (b[0], b[1])]).astype(jnp.int32)
@@ -424,7 +472,7 @@
     )
     held = keep_call(d, hidden, take)
     own_cols = [b[0] * 2 + b[1] for b in bits]
-    own_gain = [lax.dynamic_slice(gain_row, (0, c * cols), (1, cols)) for c in own_cols]
+    own_gain = [lax.dynamic_slice(input_gain, (c * cols,), (cols,)) for c in own_cols]
     shape = (1, 2, 2, 2, blk, cols)
     away = [v.reshape(shape) for v in away]
     held = [v.reshape(shape) for v in held]
@@ -458,8 +506,11 @@
             continue
         got, flight[lane] = flight[lane], None
         if lane == 3:
-            small = small + got
-            settled.append(small)
+            if step == 4:
+                both = (small, got)
+            else:
+                small = small + got
+                settled.append(small)
         elif step < 4:
             keep = held[lane] if step == 0 else lax.index_in_dim(held[lane], 0, step, keepdims=True)
             held[lane] = sums[lane] = add(keep, got)
@@ -470,8 +521,7 @@
         else:
             held[lane] = (held[lane], got)
 
-    coef = RATE * lax.rsqrt(small[16, :1] / (model_width * width) + EPS)
-    top = jnp.zeros((width, 128), F32)
+    entries = model_width * width
     pieces, columns = [], []
     for n in range(2):
         part = [held[chain][n].reshape(2, 4, blk, cols) for chain in range(3)]
@@ -479,11 +529,11 @@
         for chain in range(3):
             inner = GATHER[chain][3] == 1
             spots += [(2 * i + n if inner else 2 * n + i) ^ own_cols[chain] for i in range(2)]
-        top = top_part(part, w_t, gain_row, coef, top, spots, row_masks)
         pieces += part
         columns += spots
-    codes = code_all(pieces, w_t, gain_row, coef, top, swap_cores(top), columns, row_masks)
-    loss = lax.dynamic_slice(small, (roll, 0), (1, 1))
+    top = top_all(entries, pieces, w_t, gains, both, columns, row_masks)
+    codes = code_all(entries, pieces, w_t, gains, both, top, swap_cores(top), columns, row_masks)
+    loss = sum(lax.dynamic_slice(v, (roll, 0), (1, 1)) for v in both)
     return loss.reshape(1), codes.T
 
 

time: 132 us -> 126 us (0.955)
  local copies, waits for them, and re-layouts: 5.89 us -> 1.19 us
  waiting for transfers between devices: 49.2 us -> 47.8 us
    unnamed x16 -> x8, local copies, waits for them, and re-layouts: 3.8 us -> 0.02 us
    ppermute x3, waiting for transfers between devices: 4.65 us -> 3.14 us  [swap_cores(): return lax.ppermute(value, 'tp', [(0, 1), (1, 0)])]
    pallas_call x4 -> x3, Pallas kernels: 16.3 us -> 14.9 us  [the longest x1 5.44 us: keep_call(): pl.pallas_call(keep_kernel, in_specs=[scalars(), far(), far()], out_specs...]
  transfers between devices with their start and end apart: 31 -> 31, of which waited for: 18 -> 18; matrix products, arithmetic and copies ran while one was open for 4% -> 5% of each run, Pallas kernels for 6% -> 4%
where the time goes in v4:
time: 126 us
  waiting for transfers between devices  47.8 us (38%)
  starting transfers between devices  39.6 us (31%)
  Pallas kernels  29.4 us (23%)
  other arithmetic  4.67 us (4%)
  between operations  3.01 us (2%)
    ppermute x28, waiting for transfers between devices, exchange(): return lax.ppermute(value, ('roll', 'tp'), pairs)  44.7 us
    ppermute x28, starting transfers between devices, exchange(): return lax.ppermute(value, ('roll', 'tp'), pairs)  38.9 us
    pallas_call x1, Pallas kernels, forward(): pl.pallas_call(functools.partial(forward_kernel, 2), in_specs=[far(), far...  8.1 us
    pallas_call x1, Pallas kernels, head_call(): pl.pallas_call(functools.partial(head_kernel, model_width), in_specs=[sca...  6.31 us
    pallas_call x1, Pallas kernels, keep_call(): pl.pallas_call(keep_kernel, in_specs=[scalars(), far(), far()], out_specs...  5.44 us
    pallas_call x1, Pallas kernels, code_all(): pl.pallas_call(functools.partial(code_kernel, entries), in_specs=[scalars...  4.93 us
    pallas_call x1, Pallas kernels, top_all(): pl.pallas_call(functools.partial(top_kernel, entries), in_specs=[scalars(...  4.58 us
    ppermute x3, waiting for transfers between devices, swap_cores(): return lax.ppermute(value, 'tp', [(0, 1), (1, 0)])  3.14 us
  transfers between devices with their start and end apart: 31, of which 18 were waited for; matrix products, arithmetic and copies ran while one was open for 5% of the time, Pallas kernels for 4%

profile of v4, /device:TPU:0, one launch (start us, length us, event | category | flops | bytes accessed | tf_op | source)
XLA Modules:
  0.0 125.7 jit_solution(10504551439878807729)
XLA Ops:
  0.7 8.1 %shard_map.86 = (f32[576,768]{1,0:T(8,128)S(1)}, bf16[592,768]{1,0:T(8,128)(2,1)}, f32[8,768]{1,0:T(8,128)S(1)}) custom-call(bf16[768,3584]{1,0:T(8,128)(2,1)} %x_hbm.5, bf16[576,3584]{1,0:T(8,128)(2,1)} %bitcast.70, f32[28,128]{1,0:T(8,128)} %bitcast.65), custom_call_target="tpu_custom_call" | custom-call | flops 3170893824 | bytes 10000000 | tf_op jit(solution)/shard_map/pallas_call | solution.py:147
  8.8 0.5 collective-permute-start
  9.3 0.1 copy.13.gain_ref
  9.4 0.1 stack.101.where_ref
  9.6 2.0 %collective-permute-done.got_ref = bf16[592,768]{1,0:T(8,128)(2,1)S(1)} collective-permute-done((bf16[592,768]{1,0:T(8,128)(2,1)}, bf16[592,768]{1,0:T(8,128)(2,1)S(1)}, u32[]{:S(2)}, u32[]{:S(2)}) %collective-permute-start) | collective-permute-done | bytes 909344 | tf_op jit(solution)/shard_map/ppermute | solution.py:41
  11.6 6.3 %shard_map.87 = (bf16[12,48,768]{2,1,0:T(8,128)(2,1)}, f32[16,128]{1,0:T(8,128)S(1)}, bf16[2,4,48,896]{3,2,1,0:T(8,128)(2,1)}, bf16[2,4,48,896]{3,2,1,0:T(8,128)(2,1)}, bf16[2,4,48,896]{3,2,1,0:T(8,128)(2,1)}) custom-call(s32[6]{0:T(128)S(1)} %stack.101.where_ref, s32[3]{0:T(128)S(1)} %pad_add_fusion.1.masks_ref, s32[8]{0:T(128)S(1)} %bitcast.69, ...), custom_call_target="tpu_custom_call" | custom-call | flops 1585446912 | bytes 12000000 | tf_op jit(solution)/shard_map/pallas_call | solution.py:281
  17.9 3.0 %collective-permute-start.5 = (bf16[1,2,2,2,48,896]{5,4,3,2,0,1:T(8,128)(2,1)}, bf16[1,2,2,2,48,896]{5,4,3,2,0,1:T(8,128)(2,1)S(1)}, u32[]{:S(2)}, u32[]{:S(2)}) collective-permute-start(bf16[1,2,2,2,48,896]{5,4,3,2,0,1:T(8,128)(2,1)} %bitcast.78), channel_id=1, source_target_pairs={{0,8},{1,9},{2,10},{3,11},{4,12},{5,13},{6,14},{7,15},{8,0},{9,1},... | collective-permute-start | bytes 2064392 | tf_op jit(solution)/shard_map/ppermute | solution.py:37
  20.9 1.5 %collective-permute-start.1 = (bf16[1,2,2,2,48,896]{5,4,3,2,1,0:T(8,128)(2,1)}, bf16[1,2,2,2,48,896]{5,4,3,2,1,0:T(8,128)(2,1)S(1)}, u32[]{:S(2)}, u32[]{:S(2)}) collective-permute-start(bf16[1,2,2,2,48,896]{5,4,3,2,1,0:T(8,128)(2,1)} %bitcast.77), channel_id=1, source_target_pairs={{0,2},{1,5},{2,0},{3,7},{4,6},{5,1},{6,4},{7,3},{8,10},{9,13},{10,... | collective-permute-start | bytes 2064392 | tf_op jit(solution)/shard_map/ppermute | solution.py:37
  22.4 0.1 fusion.3
  22.6 0.5 collective-permute-start.4
  23.1 5.4 %shard_map.88 = (bf16[2,4,48,896]{3,2,1,0:T(8,128)(2,1)S(1)}, bf16[2,4,48,896]{3,2,1,0:T(8,128)(2,1)S(1)}, bf16[2,4,48,896]{3,2,1,0:T(8,128)(2,1)S(1)}) custom-call(s32[6]{0:T(128)S(1)} %stack.105.where_ref, bf16[12,48,768]{2,1,0:T(8,128)(2,1)} %get-tuple-element.36.d_hbm, bf16[768,3584]{1,0:T(8,128)(2,1)} %x_hbm.5), custom_call_target="tpu_custom_call" | custom-call | flops 1585446912 | bytes 10000000 | tf_op jit(solution)/shard_map/pallas_call | solution.py:317
  28.6 8.3 %collective-permute-done.5 = bf16[1,2,2,2,48,896]{5,4,3,2,0,1:T(8,128)(2,1)S(1)} collective-permute-done((bf16[1,2,2,2,48,896]{5,4,3,2,0,1:T(8,128)(2,1)}, bf16[1,2,2,2,48,896]{5,4,3,2,0,1:T(8,128)(2,1)S(1)}, u32[]{:S(2)}, u32[]{:S(2)}) %collective-permute-start.5) | collective-permute-done | bytes 688160 | tf_op jit(solution)/shard_map/ppermute | solution.py:37
  36.9 0.2 fusion
  37.1 1.7 %collective-permute-start.10 = (bf16[1,1,2,2,48,896]{5,4,3,2,0,1:T(8,128)(2,1)S(1)}, bf16[1,1,2,2,48,896]{5,4,3,2,0,1:T(8,128)(2,1)S(1)}, u32[]{:S(2)}, u32[]{:S(2)}) collective-permute-start(bf16[1,1,2,2,48,896]{5,4,3,2,0,1:T(8,128)(2,1)S(1)} %slice.85), channel_id=1, source_target_pairs={{0,2},{1,5},{2,0},{3,7},{4,6},{5,1},{6,4},{7,3},{8,10},{9,13},{10,... | collective-permute-start | bytes 1032200 | tf_op jit(solution)/shard_map/ppermute | solution.py:37
  38.8 0.2 fusion.2
  39.0 1.6 %collective-permute-start.2 = (bf16[1,1,2,2,48,896]{5,4,3,2,1,0:T(8,128)(2,1)S(1)}, bf16[1,1,2,2,48,896]{5,4,3,2,1,0:T(8,128)(2,1)S(1)}, u32[]{:S(2)}, u32[]{:S(2)}) collective-permute-start(bf16[1,1,2,2,48,896]{5,4,3,2,1,0:T(8,128)(2,1)S(1)} %slice.73), channel_id=1, source_target_pairs={{0,4},{1,3},{2,6},{3,1},{4,0},{5,7},{6,2},{7,5},{8,12},{9,11},{10,... | collective-permute-start | bytes 1032200 | tf_op jit(solution)/shard_map/ppermute | solution.py:37
  40.6 0.2 fusion.1
  40.8 1.7 %collective-permute-start.6 = (bf16[1,1,2,2,48,896]{5,4,3,2,0,1:T(8,128)(2,1)S(1)}, bf16[1,1,2,2,48,896]{5,4,3,2,0,1:T(8,128)(2,1)S(1)}, u32[]{:S(2)}, u32[]{:S(2)}) collective-permute-start(bf16[1,1,2,2,48,896]{5,4,3,2,0,1:T(8,128)(2,1)S(1)} %slice.79), channel_id=1, source_target_pairs={{0,8},{1,9},{2,10},{3,11},{4,12},{5,13},{6,14},{7,15},{8,0},{9,1},... | collective-permute-start | bytes 1032200 | tf_op jit(solution)/shard_map/ppermute | solution.py:37
  42.5 5.6 %collective-permute-done.10 = bf16[1,1,2,2,48,896]{5,4,3,2,0,1:T(8,128)(2,1)S(1)} collective-permute-done((bf16[1,1,2,2,48,896]{5,4,3,2,0,1:T(8,128)(2,1)S(1)}, bf16[1,1,2,2,48,896]{5,4,3,2,0,1:T(8,128)(2,1)S(1)}, u32[]{:S(2)}, u32[]{:S(2)}) %collective-permute-start.10) | collective-permute-done | bytes 344096 | tf_op jit(solution)/shard_map/ppermute | solution.py:37
  48.2 1.4 %collective-permute-start.11 = (bf16[1,1,1,2,48,896]{5,4,3,2,0,1:T(8,128)(2,1)S(1)}, bf16[1,1,1,2,48,896]{5,4,3,2,0,1:T(8,128)(2,1)S(1)}, u32[]{:S(2)}, u32[]{:S(2)}) collective-permute-start(bf16[1,1,1,2,48,896]{5,4,3,2,0,1:T(8,128)(2,1)S(1)} %slice.87), channel_id=1, source_target_pairs={{0,4},{1,3},{2,6},{3,1},{4,0},{5,7},{6,2},{7,5},{8,12},{9,11},{10,... | collective-permute-start | bytes 516104 | tf_op jit(solution)/shard_map/ppermute | solution.py:37
  49.6 0.1 add_convert_fusion.2
  49.7 2.2 %collective-permute-start.3 = (bf16[1,1,1,2,48,896]{5,4,3,2,1,0:T(8,128)(2,1)S(1)}, bf16[1,1,1,2,48,896]{5,4,3,2,1,0:T(8,128)(2,1)S(1)}, u32[]{:S(2)}, u32[]{:S(2)}) collective-permute-start(bf16[1,1,1,2,48,896]{5,4,3,2,1,0:T(8,128)(2,1)S(1)} %slice.75), channel_id=1, source_target_pairs={{0,16},{1,17},{2,18},{3,19},{4,20},{5,21},{6,22},{7,23},{8,24},{9,... | collective-permute-start | bytes 516104 | tf_op jit(solution)/shard_map/ppermute | solution.py:37
  51.9 0.1 add_convert_fusion.1
  52.1 1.3 %collective-permute-start.7 = (bf16[1,1,1,2,48,896]{5,4,3,2,0,1:T(8,128)(2,1)S(1)}, bf16[1,1,1,2,48,896]{5,4,3,2,0,1:T(8,128)(2,1)S(1)}, u32[]{:S(2)}, u32[]{:S(2)}) collective-permute-start(bf16[1,1,1,2,48,896]{5,4,3,2,0,1:T(8,128)(2,1)S(1)} %slice.81), channel_id=1, source_target_pairs={{0,4},{1,3},{2,6},{3,1},{4,0},{5,7},{6,2},{7,5},{8,12},{9,11},{10,... | collective-permute-start | bytes 516104 | tf_op jit(solution)/shard_map/ppermute | solution.py:37
  53.4 0.3 collective-permute-done.11
  53.8 2.8 %collective-permute-start.12 = (bf16[1,1,1,1,48,896]{5,4,3,2,0,1:T(8,128)(2,1)S(1)}, bf16[1,1,1,1,48,896]{5,4,3,2,0,1:T(8,128)(2,1)S(1)}, u32[]{:S(2)}, u32[]{:S(2)}) collective-permute-start(bf16[1,1,1,1,48,896]{5,4,3,2,0,1:T(8,128)(2,1)S(1)} %slice.89), channel_id=1, source_target_pairs={{0,16},{1,17},{2,18},{3,19},{4,20},{5,21},{6,22},{7,23},{8,24},{9,... | collective-permute-start | bytes 258056 | tf_op jit(solution)/shard_map/ppermute | solution.py:37
  56.6 5.5 %collective-permute-done.3 = bf16[1,1,1,2,48,896]{5,4,3,2,1,0:T(8,128)(2,1)S(1)} collective-permute-done((bf16[1,1,1,2,48,896]{5,4,3,2,1,0:T(8,128)(2,1)S(1)}, bf16[1,1,1,2,48,896]{5,4,3,2,1,0:T(8,128)(2,1)S(1)}, u32[]{:S(2)}, u32[]{:S(2)}) %collective-permute-start.3) | collective-permute-done | bytes 172064 | tf_op jit(solution)/shard_map/ppermute | solution.py:37
  62.3 4.0 %collective-permute-start.8 = (bf16[1,1,1,1,48,896]{5,4,3,2,1,0:T(8,128)(2,1)S(1)}, bf16[1,1,1,1,48,896]{5,4,3,2,1,0:T(8,128)(2,1)S(1)}, u32[]{:S(2)}, u32[]{:S(2)}) collective-permute-start(bf16[1,1,1,1,48,896]{5,4,3,2,1,0:T(8,128)(2,1)S(1)} %slice.77), channel_id=1, source_target_pairs={{0,8},{1,9},{2,10},{3,11},{4,12},{5,13},{6,14},{7,15},{8,0},{9,1},... | collective-permute-start | bytes 258056 | tf_op jit(solution)/shard_map/ppermute | solution.py:37
  66.3 0.7 multiply_reduce_fusion
  67.1 2.3 %collective-permute-done.9 = bf16[1,1,1,1,48,896]{5,4,3,2,0,1:T(8,128)(2,1)S(1)} collective-permute-done((bf16[1,1,1,1,48,896]{5,4,3,2,0,1:T(8,128)(2,1)S(1)}, bf16[1,1,1,1,48,896]{5,4,3,2,0,1:T(8,128)(2,1)S(1)}, u32[]{:S(2)}, u32[]{:S(2)}) %collective-permute-start.9) | collective-permute-done | bytes 86048 | tf_op jit(solution)/shard_map/ppermute | solution.py:37
  69.4 0.6 multiply_reduce_fusion.1
  70.0 0.6 collective-permute-start.20
  70.6 0.6 multiply_reduce_fusion.2
  73.2 1.6 %collective-permute-start.13 = (f32[24,128]{1,0:T(8,128)S(1)}, f32[24,128]{1,0:T(8,128)S(1)}, u32[]{:S(2)}, u32[]{:S(2)}) collective-permute-start(f32[24,128]{1,0:T(8,128)S(1)} %concatenate.30), channel_id=1, source_target_pairs={{0,2},{1,5},{2,0},{3,7},{4,6},{5,1},{6,4},{7,3},{8,10},{9,13},{10,... | collective-permute-start | bytes 36872 | tf_op jit(solution)/shard_map/ppermute | solution.py:37
  74.7 1.8 %collective-permute-start.17 = (bf16[1,1,1,1,48,896]{5,4,3,2,1,0:T(8,128)(2,1)S(1)}, bf16[1,1,1,1,48,896]{5,4,3,2,1,0:T(8,128)(2,1)S(1)}, u32[]{:S(2)}, u32[]{:S(2)}) collective-permute-start(bf16[1,1,1,1,48,896]{5,4,3,2,1,0:T(8,128)(2,1)S(1)} %get-tuple-element.52), channel_id=1, source_target_pairs={{0,8},{1,9},{2,10},{3,11},{4,12},{5,13},{6,14},{7,15},{8,0},{9,1},... | collective-permute-start | bytes 258056 | tf_op jit(solution)/shard_map/ppermute | solution.py:37
  76.5 0.7 collective-permute-done.20
  77.3 0.7 collective-permute-start.21
  78.0 1.2 collective-permute-done.17
  79.2 2.8 %collective-permute-start.19 = (bf16[1,1,1,2,48,896]{5,4,3,2,1,0:T(8,128)(2,1)S(1)}, bf16[1,1,1,2,48,896]{5,4,3,2,1,0:T(8,128)(2,1)S(1)}, u32[]{:S(2)}, u32[]{:S(2)}) collective-permute-start(bf16[1,1,1,2,48,896]{5,4,3,2,1,0:T(8,128)(2,1)S(1)} %pad_maximum_fusion.6), channel_id=1, source_target_pairs={{0,16},{1,17},{2,18},{3,19},{4,20},{5,21},{6,22},{7,23},{8,24},{9,... | collective-permute-start | bytes 516104 | tf_op jit(solution)/shard_map/ppermute | solution.py:37
  82.1 0.6 collective-permute-done.21
  82.8 1.6 %collective-permute-start.22 = (bf16[1,1,2,2,48,896]{5,4,3,2,0,1:T(8,128)(2,1)S(1)}, bf16[1,1,2,2,48,896]{5,4,3,2,0,1:T(8,128)(2,1)S(1)}, u32[]{:S(2)}, u32[]{:S(2)}) collective-permute-start(bf16[1,1,2,2,48,896]{5,4,3,2,0,1:T(8,128)(2,1)S(1)} %pad_maximum_fusion.4), channel_id=1, source_target_pairs={{0,2},{1,5},{2,0},{3,7},{4,6},{5,1},{6,4},{7,3},{8,10},{9,13},{10,... | collective-permute-start | bytes 1032200 | tf_op jit(solution)/shard_map/ppermute | solution.py:37
  84.3 3.7 %collective-permute-done.14 = f32[24,128]{1,0:T(8,128)S(1)} collective-permute-done((f32[24,128]{1,0:T(8,128)S(1)}, f32[24,128]{1,0:T(8,128)S(1)}, u32[]{:S(2)}, u32[]{:S(2)}) %collective-permute-start.14) | collective-permute-done | bytes 12320 | tf_op jit(solution)/shard_map/ppermute | solution.py:37
  88.1 0.2 collective-permute-start.26
  88.3 1.0 collective-permute-done.19
  89.3 1.8 %collective-permute-done.22 = bf16[1,1,2,2,48,896]{5,4,3,2,0,1:T(8,128)(2,1)S(1)} collective-permute-done((bf16[1,1,2,2,48,896]{5,4,3,2,0,1:T(8,128)(2,1)S(1)}, bf16[1,1,2,2,48,896]{5,4,3,2,0,1:T(8,128)(2,1)S(1)}, u32[]{:S(2)}, u32[]{:S(2)}) %collective-permute-start.22) | collective-permute-done | bytes 344096 | tf_op jit(solution)/shard_map/ppermute | solution.py:37
  91.2 0.1 pad_maximum_fusion
  91.3 1.9 %collective-permute-start.23 = (bf16[1,1,2,2,48,896]{5,4,3,2,1,0:T(8,128)(2,1)S(1)}, bf16[1,1,2,2,48,896]{5,4,3,2,1,0:T(8,128)(2,1)S(1)}, u32[]{:S(2)}, u32[]{:S(2)}) collective-permute-start(bf16[1,1,2,2,48,896]{5,4,3,2,1,0:T(8,128)(2,1)S(1)} %pad_maximum_fusion.3), channel_id=1, source_target_pairs={{0,4},{1,3},{2,6},{3,1},{4,0},{5,7},{6,2},{7,5},{8,12},{9,11},{10,... | collective-permute-start | bytes 1032200 | tf_op jit(solution)/shard_map/ppermute | solution.py:37
  93.2 1.0 collective-permute-start.28
  94.2 1.2 collective-permute-done.26
  95.4 0.1 pad_maximum_fusion.2
  95.5 0.8 collective-permute-start.29
  96.3 5.2 %collective-permute-done.23 = bf16[1,1,2,2,48,896]{5,4,3,2,1,0:T(8,128)(2,1)S(1)} collective-permute-done((bf16[1,1,2,2,48,896]{5,4,3,2,1,0:T(8,128)(2,1)S(1)}, bf16[1,1,2,2,48,896]{5,4,3,2,1,0:T(8,128)(2,1)S(1)}, u32[]{:S(2)}, u32[]{:S(2)}) %collective-permute-start.23) | collective-permute-done | bytes 344096 | tf_op jit(solution)/shard_map/ppermute | solution.py:37
  101.5 0.1 pad_maximum_fusion.1
  101.6 3.0 %collective-permute-start.27 = (bf16[1,2,2,2,48,896]{5,4,3,2,1,0:T(8,128)(2,1)S(1)}, bf16[1,2,2,2,48,896]{5,4,3,2,1,0:T(8,128)(2,1)}, u32[]{:S(2)}, u32[]{:S(2)}) collective-permute-start(bf16[1,2,2,2,48,896]{5,4,3,2,1,0:T(8,128)(2,1)S(1)} %pad_maximum_fusion.1), channel_id=1, source_target_pairs={{0,2},{1,5},{2,0},{3,7},{4,6},{5,1},{6,4},{7,3},{8,10},{9,13},{10,... | collective-permute-start | bytes 2064392 | tf_op jit(solution)/shard_map/ppermute | solution.py:37
  104.6 3.7 %collective-permute-done.15 = f32[24,128]{1,0:T(8,128)S(1)} collective-permute-done((f32[24,128]{1,0:T(8,128)S(1)}, f32[24,128]{1,0:T(8,128)S(1)}, u32[]{:S(2)}, u32[]{:S(2)}) %collective-permute-start.15) | collective-permute-done | bytes 12320 | tf_op jit(solution)/shard_map/ppermute | solution.py:37
  108.3 1.0 collective-permute-start.16
  109.3 3.5 %collective-permute-done.16 = f32[24,128]{1,0:T(8,128)S(1)} collective-permute-done((f32[24,128]{1,0:T(8,128)S(1)}, f32[24,128]{1,0:T(8,128)S(1)}, u32[]{:S(2)}, u32[]{:S(2)}) %collective-permute-start.16) | collective-permute-done | bytes 12320 | tf_op jit(solution)/shard_map/ppermute | solution.py:37
  112.9 0.1 stack.118.where_ref
  112.9 1.1 collective-permute-done.24.sum2_ref
  114.0 4.6 %shard_map.89.mine_ref = f32[576,128]{1,0:T(8,128)} custom-call(s32[15]{0:T(128)S(1)} %stack.118.where_ref, f32[24,128]{1,0:T(8,128)S(1)} %add.113.sum_ref, f32[24,128]{1,0:T(8,128)S(1)} %collective-permute-done.24.sum2_ref, f32[28,128]{1,0:T(8,128)S(1)} %bitcast.66, bf16[576,3584]{1,0:T(8,128)(2,1)} %bitcast.71, bf16[2,4,48,896]{3,2,1,0:T(8,128)(2,1)S(1)} %bitcast.56, ...), custom_call_target="tpu_custom_call" | custom-call | flops 8257536 | bytes 8257536 | tf_op jit(solution)/shard_map/pallas_call | solution.py:378
  118.6 0.2 collective-permute-start.30
  118.9 0.5 constant_dynamic-slice_fusion
  119.4 1.2 fusion.4
  120.6 4.9 %shard_map.90 = bf16[576,3584]{1,0:T(8,128)(2,1)} custom-call(s32[15]{0:T(128)S(1)} %stack.118.where_ref, f32[24,128]{1,0:T(8,128)S(1)} %add.113.sum_ref, f32[24,128]{1,0:T(8,128)S(1)} %collective-permute-done.24.sum2_ref, f32[28,128]{1,0:T(8,128)S(1)} %bitcast.67, bf16[576,3584]{1,0:T(8,128)(2,1)} %bitcast.72, f32[576,128]{1,0:T(8,128)} %shard_map.89.mine_ref, ...), custom_call_target="tpu_custom_call" | custom-call | flops 16515072 | bytes 12386304 | tf_op jit(solution)/shard_map/pallas_call | solution.py:419
  (55 shorter events, 1.1 us)
Async XLA Ops:
  0.6 8.7 %copy-start.3 = (f32[512]{0:T(512)S(1)}, f32[512]{0:T(512)}, u32[]{:S(2)}) copy-start(f32[512]{0:T(512)} %param.12) | copy-start | bytes 6148
  0.6 10.9 %copy-start.1 = (s32[768,1]{0,1:T(1,128)S(1)}, s32[768,1]{0,1:T(1,128)}, u32[]{:S(2)}) copy-start(s32[768,1]{0,1:T(1,128)} %param.10) | copy-start | bytes 9220
  0.7 10.9 %copy-start.2 = (s32[1,8]{1,0:T(1,128)S(1)}, s32[1,8]{1,0:T(1,128)}, u32[]{:S(2)}) copy-start(s32[1,8]{1,0:T(1,128)} %param.9) | copy-start | bytes 100
  8.8 2.8 %collective-permute-start = (bf16[592,768]{1,0:T(8,128)(2,1)}, bf16[592,768]{1,0:T(8,128)(2,1)S(1)}, u32[]{:S(2)}, u32[]{:S(2)}) collective-permute-start(bf16[592,768]{1,0:T(8,128)(2,1)} %get-tuple-element.33), channel_id=1, source_target_pairs={{0,1},{1,0},{2,3},{3,2},{4,5},{5,4},{6,7},{7,6},{8,9},{9,8},{10,11... | collective-permute-start | bytes 2727944 | tf_op jit(solution)/shard_map/ppermute | solution.py:41
  11.6 10.8 %copy-start = (f32[3584]{0:T(1024)S(1)}, f32[3584]{0:T(1024)}, u32[]{:S(2)}) copy-start(f32[3584]{0:T(1024)} %param.11) | copy-start | bytes 43012
  17.9 19.0 %collective-permute-start.5 = (bf16[1,2,2,2,48,896]{5,4,3,2,0,1:T(8,128)(2,1)}, bf16[1,2,2,2,48,896]{5,4,3,2,0,1:T(8,128)(2,1)S(1)}, u32[]{:S(2)}, u32[]{:S(2)}) collective-permute-start(bf16[1,2,2,2,48,896]{5,4,3,2,0,1:T(8,128)(2,1)} %bitcast.78), channel_id=1, source_target_pairs={{0,8},{1,9},{2,10},{3,11},{4,12},{5,13},{6,14},{7,15},{8,0},{9,1},... | collective-permute-start | bytes 2064392 | tf_op jit(solution)/shard_map/ppermute | solution.py:37
  20.9 17.9 %collective-permute-start.1 = (bf16[1,2,2,2,48,896]{5,4,3,2,1,0:T(8,128)(2,1)}, bf16[1,2,2,2,48,896]{5,4,3,2,1,0:T(8,128)(2,1)S(1)}, u32[]{:S(2)}, u32[]{:S(2)}) collective-permute-start(bf16[1,2,2,2,48,896]{5,4,3,2,1,0:T(8,128)(2,1)} %bitcast.77), channel_id=1, source_target_pairs={{0,2},{1,5},{2,0},{3,7},{4,6},{5,1},{6,4},{7,3},{8,10},{9,13},{10,... | collective-permute-start | bytes 2064392 | tf_op jit(solution)/shard_map/ppermute | solution.py:37
  22.6 18.0 %collective-permute-start.4 = (bf16[1,2,2,2,48,896]{5,4,3,2,0,1:T(8,128)(2,1)}, bf16[1,2,2,2,48,896]{5,4,3,2,0,1:T(8,128)(2,1)S(1)}, u32[]{:S(2)}, u32[]{:S(2)}) collective-permute-start(bf16[1,2,2,2,48,896]{5,4,3,2,0,1:T(8,128)(2,1)} %bitcast.76), channel_id=1, source_target_pairs={{0,2},{1,5},{2,0},{3,7},{4,6},{5,1},{6,4},{7,3},{8,10},{9,13},{10,... | collective-permute-start | bytes 2064392 | tf_op jit(solution)/shard_map/ppermute | solution.py:37
  37.1 11.0 %collective-permute-start.10 = (bf16[1,1,2,2,48,896]{5,4,3,2,0,1:T(8,128)(2,1)S(1)}, bf16[1,1,2,2,48,896]{5,4,3,2,0,1:T(8,128)(2,1)S(1)}, u32[]{:S(2)}, u32[]{:S(2)}) collective-permute-start(bf16[1,1,2,2,48,896]{5,4,3,2,0,1:T(8,128)(2,1)S(1)} %slice.85), channel_id=1, source_target_pairs={{0,2},{1,5},{2,0},{3,7},{4,6},{5,1},{6,4},{7,3},{8,10},{9,13},{10,... | collective-permute-start | bytes 1032200 | tf_op jit(solution)/shard_map/ppermute | solution.py:37
  39.0 10.6 %collective-permute-start.2 = (bf16[1,1,2,2,48,896]{5,4,3,2,1,0:T(8,128)(2,1)S(1)}, bf16[1,1,2,2,48,896]{5,4,3,2,1,0:T(8,128)(2,1)S(1)}, u32[]{:S(2)}, u32[]{:S(2)}) collective-permute-start(bf16[1,1,2,2,48,896]{5,4,3,2,1,0:T(8,128)(2,1)S(1)} %slice.73), channel_id=1, source_target_pairs={{0,4},{1,3},{2,6},{3,1},{4,0},{5,7},{6,2},{7,5},{8,12},{9,11},{10,... | collective-permute-start | bytes 1032200 | tf_op jit(solution)/shard_map/ppermute | solution.py:37
  40.8 11.1 %collective-permute-start.6 = (bf16[1,1,2,2,48,896]{5,4,3,2,0,1:T(8,128)(2,1)S(1)}, bf16[1,1,2,2,48,896]{5,4,3,2,0,1:T(8,128)(2,1)S(1)}, u32[]{:S(2)}, u32[]{:S(2)}) collective-permute-start(bf16[1,1,2,2,48,896]{5,4,3,2,0,1:T(8,128)(2,1)S(1)} %slice.79), channel_id=1, source_target_pairs={{0,8},{1,9},{2,10},{3,11},{4,12},{5,13},{6,14},{7,15},{8,0},{9,1},... | collective-permute-start | bytes 1032200 | tf_op jit(solution)/shard_map/ppermute | solution.py:37
  48.2 5.5 %collective-permute-start.11 = (bf16[1,1,1,2,48,896]{5,4,3,2,0,1:T(8,128)(2,1)S(1)}, bf16[1,1,1,2,48,896]{5,4,3,2,0,1:T(8,128)(2,1)S(1)}, u32[]{:S(2)}, u32[]{:S(2)}) collective-permute-start(bf16[1,1,1,2,48,896]{5,4,3,2,0,1:T(8,128)(2,1)S(1)} %slice.87), channel_id=1, source_target_pairs={{0,4},{1,3},{2,6},{3,1},{4,0},{5,7},{6,2},{7,5},{8,12},{9,11},{10,... | collective-permute-start | bytes 516104 | tf_op jit(solution)/shard_map/ppermute | solution.py:37
  49.7 12.3 %collective-permute-start.3 = (bf16[1,1,1,2,48,896]{5,4,3,2,1,0:T(8,128)(2,1)S(1)}, bf16[1,1,1,2,48,896]{5,4,3,2,1,0:T(8,128)(2,1)S(1)}, u32[]{:S(2)}, u32[]{:S(2)}) collective-permute-start(bf16[1,1,1,2,48,896]{5,4,3,2,1,0:T(8,128)(2,1)S(1)} %slice.75), channel_id=1, source_target_pairs={{0,16},{1,17},{2,18},{3,19},{4,20},{5,21},{6,22},{7,23},{8,24},{9,... | collective-permute-start | bytes 516104 | tf_op jit(solution)/shard_map/ppermute | solution.py:37
  52.1 10.0 %collective-permute-start.7 = (bf16[1,1,1,2,48,896]{5,4,3,2,0,1:T(8,128)(2,1)S(1)}, bf16[1,1,1,2,48,896]{5,4,3,2,0,1:T(8,128)(2,1)S(1)}, u32[]{:S(2)}, u32[]{:S(2)}) collective-permute-start(bf16[1,1,1,2,48,896]{5,4,3,2,0,1:T(8,128)(2,1)S(1)} %slice.81), channel_id=1, source_target_pairs={{0,4},{1,3},{2,6},{3,1},{4,0},{5,7},{6,2},{7,5},{8,12},{9,11},{10,... | collective-permute-start | bytes 516104 | tf_op jit(solution)/shard_map/ppermute | solution.py:37
  53.8 12.5 %collective-permute-start.12 = (bf16[1,1,1,1,48,896]{5,4,3,2,0,1:T(8,128)(2,1)S(1)}, bf16[1,1,1,1,48,896]{5,4,3,2,0,1:T(8,128)(2,1)S(1)}, u32[]{:S(2)}, u32[]{:S(2)}) collective-permute-start(bf16[1,1,1,1,48,896]{5,4,3,2,0,1:T(8,128)(2,1)S(1)} %slice.89), channel_id=1, source_target_pairs={{0,16},{1,17},{2,18},{3,19},{4,20},{5,21},{6,22},{7,23},{8,24},{9,... | collective-permute-start | bytes 258056 | tf_op jit(solution)/shard_map/ppermute | solution.py:37
  62.2 7.2 %collective-permute-start.9 = (bf16[1,1,1,1,48,896]{5,4,3,2,0,1:T(8,128)(2,1)S(1)}, bf16[1,1,1,1,48,896]{5,4,3,2,0,1:T(8,128)(2,1)S(1)}, u32[]{:S(2)}, u32[]{:S(2)}) collective-permute-start(bf16[1,1,1,1,48,896]{5,4,3,2,0,1:T(8,128)(2,1)S(1)} %slice.83), channel_id=1, source_target_pairs={{0,16},{1,17},{2,18},{3,19},{4,20},{5,21},{6,22},{7,23},{8,24},{9,... | collective-permute-start | bytes 258056 | tf_op jit(solution)/shard_map/ppermute | solution.py:37
  62.3 8.3 %collective-permute-start.8 = (bf16[1,1,1,1,48,896]{5,4,3,2,1,0:T(8,128)(2,1)S(1)}, bf16[1,1,1,1,48,896]{5,4,3,2,1,0:T(8,128)(2,1)S(1)}, u32[]{:S(2)}, u32[]{:S(2)}) collective-permute-start(bf16[1,1,1,1,48,896]{5,4,3,2,1,0:T(8,128)(2,1)S(1)} %slice.77), channel_id=1, source_target_pairs={{0,8},{1,9},{2,10},{3,11},{4,12},{5,13},{6,14},{7,15},{8,0},{9,1},... | collective-permute-start | bytes 258056 | tf_op jit(solution)/shard_map/ppermute | solution.py:37
  67.0 10.9 %collective-permute-start.18 = (bf16[1,1,1,1,48,896]{5,4,3,2,0,1:T(8,128)(2,1)S(1)}, bf16[1,1,1,1,48,896]{5,4,3,2,0,1:T(8,128)(2,1)S(1)}, u32[]{:S(2)}, u32[]{:S(2)}) collective-permute-start(bf16[1,1,1,1,48,896]{5,4,3,2,0,1:T(8,128)(2,1)S(1)} %get-tuple-element.53), channel_id=1, source_target_pairs={{0,16},{1,17},{2,18},{3,19},{4,20},{5,21},{6,22},{7,23},{8,24},{9,... | collective-permute-start | bytes 258056 | tf_op jit(solution)/shard_map/ppermute | solution.py:37
  70.0 7.2 %collective-permute-start.20 = (bf16[1,1,1,1,48,896]{5,4,3,2,0,1:T(8,128)(2,1)S(1)}, bf16[1,1,1,1,48,896]{5,4,3,2,0,1:T(8,128)(2,1)S(1)}, u32[]{:S(2)}, u32[]{:S(2)}) collective-permute-start(bf16[1,1,1,1,48,896]{5,4,3,2,0,1:T(8,128)(2,1)S(1)} %get-tuple-element.55), channel_id=1, source_target_pairs={{0,16},{1,17},{2,18},{3,19},{4,20},{5,21},{6,22},{7,23},{8,24},{9,... | collective-permute-start | bytes 258056 | tf_op jit(solution)/shard_map/ppermute | solution.py:37
  73.2 11.2 %collective-permute-start.13 = (f32[24,128]{1,0:T(8,128)S(1)}, f32[24,128]{1,0:T(8,128)S(1)}, u32[]{:S(2)}, u32[]{:S(2)}) collective-permute-start(f32[24,128]{1,0:T(8,128)S(1)} %concatenate.30), channel_id=1, source_target_pairs={{0,2},{1,5},{2,0},{3,7},{4,6},{5,1},{6,4},{7,3},{8,10},{9,13},{10,... | collective-permute-start | bytes 36872 | tf_op jit(solution)/shard_map/ppermute | solution.py:37
  74.7 4.5 %collective-permute-start.17 = (bf16[1,1,1,1,48,896]{5,4,3,2,1,0:T(8,128)(2,1)S(1)}, bf16[1,1,1,1,48,896]{5,4,3,2,1,0:T(8,128)(2,1)S(1)}, u32[]{:S(2)}, u32[]{:S(2)}) collective-permute-start(bf16[1,1,1,1,48,896]{5,4,3,2,1,0:T(8,128)(2,1)S(1)} %get-tuple-element.52), channel_id=1, source_target_pairs={{0,8},{1,9},{2,10},{3,11},{4,12},{5,13},{6,14},{7,15},{8,0},{9,1},... | collective-permute-start | bytes 258056 | tf_op jit(solution)/shard_map/ppermute | solution.py:37
  77.3 5.5 %collective-permute-start.21 = (bf16[1,1,1,2,48,896]{5,4,3,2,0,1:T(8,128)(2,1)S(1)}, bf16[1,1,1,2,48,896]{5,4,3,2,0,1:T(8,128)(2,1)S(1)}, u32[]{:S(2)}, u32[]{:S(2)}) collective-permute-start(bf16[1,1,1,2,48,896]{5,4,3,2,0,1:T(8,128)(2,1)S(1)} %pad_maximum_fusion.8), channel_id=1, source_target_pairs={{0,4},{1,3},{2,6},{3,1},{4,0},{5,7},{6,2},{7,5},{8,12},{9,11},{10,... | collective-permute-start | bytes 516104 | tf_op jit(solution)/shard_map/ppermute | solution.py:37
  78.0 10.1 %collective-permute-start.25 = (bf16[1,1,1,2,48,896]{5,4,3,2,0,1:T(8,128)(2,1)S(1)}, bf16[1,1,1,2,48,896]{5,4,3,2,0,1:T(8,128)(2,1)S(1)}, u32[]{:S(2)}, u32[]{:S(2)}) collective-permute-start(bf16[1,1,1,2,48,896]{5,4,3,2,0,1:T(8,128)(2,1)S(1)} %pad_maximum_fusion.7), channel_id=1, source_target_pairs={{0,8},{1,9},{2,10},{3,11},{4,12},{5,13},{6,14},{7,15},{8,0},{9,1},... | collective-permute-start | bytes 516104 | tf_op jit(solution)/shard_map/ppermute | solution.py:37
  79.2 10.1 %collective-permute-start.19 = (bf16[1,1,1,2,48,896]{5,4,3,2,1,0:T(8,128)(2,1)S(1)}, bf16[1,1,1,2,48,896]{5,4,3,2,1,0:T(8,128)(2,1)S(1)}, u32[]{:S(2)}, u32[]{:S(2)}) collective-permute-start(bf16[1,1,1,2,48,896]{5,4,3,2,1,0:T(8,128)(2,1)S(1)} %pad_maximum_fusion.6), channel_id=1, source_target_pairs={{0,16},{1,17},{2,18},{3,19},{4,20},{5,21},{6,22},{7,23},{8,24},{9,... | collective-permute-start | bytes 516104 | tf_op jit(solution)/shard_map/ppermute | solution.py:37
  82.8 8.4 %collective-permute-start.22 = (bf16[1,1,2,2,48,896]{5,4,3,2,0,1:T(8,128)(2,1)S(1)}, bf16[1,1,2,2,48,896]{5,4,3,2,0,1:T(8,128)(2,1)S(1)}, u32[]{:S(2)}, u32[]{:S(2)}) collective-permute-start(bf16[1,1,2,2,48,896]{5,4,3,2,0,1:T(8,128)(2,1)S(1)} %pad_maximum_fusion.4), channel_id=1, source_target_pairs={{0,2},{1,5},{2,0},{3,7},{4,6},{5,1},{6,4},{7,3},{8,10},{9,13},{10,... | collective-permute-start | bytes 1032200 | tf_op jit(solution)/shard_map/ppermute | solution.py:37
  84.3 3.7 %collective-permute-start.14 = (f32[24,128]{1,0:T(8,128)S(1)}, f32[24,128]{1,0:T(8,128)S(1)}, u32[]{:S(2)}, u32[]{:S(2)}) collective-permute-start(f32[24,128]{1,0:T(8,128)S(1)} %pad_add_fusion), channel_id=1, source_target_pairs={{0,4},{1,3},{2,6},{3,1},{4,0},{5,7},{6,2},{7,5},{8,12},{9,11},{10,... | collective-permute-start | bytes 36872 | tf_op jit(solution)/shard_map/ppermute | solution.py:37
  88.1 7.3 %collective-permute-start.26 = (bf16[2,1,1,2,48,896]{5,4,3,2,0,1:T(8,128)(2,1)S(1)}, bf16[2,1,1,2,48,896]{5,4,3,2,0,1:T(8,128)(2,1)S(1)}, u32[]{:S(2)}, u32[]{:S(2)}) collective-permute-start(bf16[2,1,1,2,48,896]{5,4,3,2,0,1:T(8,128)(2,1)S(1)} %pad_maximum_fusion.5), channel_id=1, source_target_pairs={{0,4},{1,3},{2,6},{3,1},{4,0},{5,7},{6,2},{7,5},{8,12},{9,11},{10,... | collective-permute-start | bytes 1032200 | tf_op jit(solution)/shard_map/ppermute | solution.py:37
  91.3 10.2 %collective-permute-start.23 = (bf16[1,1,2,2,48,896]{5,4,3,2,1,0:T(8,128)(2,1)S(1)}, bf16[1,1,2,2,48,896]{5,4,3,2,1,0:T(8,128)(2,1)S(1)}, u32[]{:S(2)}, u32[]{:S(2)}) collective-permute-start(bf16[1,1,2,2,48,896]{5,4,3,2,1,0:T(8,128)(2,1)S(1)} %pad_maximum_fusion.3), channel_id=1, source_target_pairs={{0,4},{1,3},{2,6},{3,1},{4,0},{5,7},{6,2},{7,5},{8,12},{9,11},{10,... | collective-permute-start | bytes 1032200 | tf_op jit(solution)/shard_map/ppermute | solution.py:37
  93.2 20.9 %collective-permute-start.28 = (bf16[2,1,2,2,48,896]{5,4,3,2,0,1:T(8,128)(2,1)S(1)}, bf16[2,1,2,2,48,896]{5,4,3,2,0,1:T(8,128)(2,1)S(1)}, u32[]{:S(2)}, u32[]{:S(2)}) collective-permute-start(bf16[2,1,2,2,48,896]{5,4,3,2,0,1:T(8,128)(2,1)S(1)} %pad_maximum_fusion), channel_id=1, source_target_pairs={{0,8},{1,9},{2,10},{3,11},{4,12},{5,13},{6,14},{7,15},{8,0},{9,1},... | collective-permute-start | bytes 2064392 | tf_op jit(solution)/shard_map/ppermute | solution.py:37
  95.5 18.5 %collective-permute-start.29 = (bf16[2,1,2,2,48,896]{5,4,3,2,0,1:T(8,128)(2,1)S(1)}, bf16[2,1,2,2,48,896]{5,4,3,2,0,1:T(8,128)(2,1)S(1)}, u32[]{:S(2)}, u32[]{:S(2)}) collective-permute-start(bf16[2,1,2,2,48,896]{5,4,3,2,0,1:T(8,128)(2,1)S(1)} %pad_maximum_fusion.2), channel_id=1, source_target_pairs={{0,2},{1,5},{2,0},{3,7},{4,6},{5,1},{6,4},{7,3},{8,10},{9,13},{10,... | collective-permute-start | bytes 2064392 | tf_op jit(solution)/shard_map/ppermute | solution.py:37
  101.6 12.5 %collective-permute-start.27 = (bf16[1,2,2,2,48,896]{5,4,3,2,1,0:T(8,128)(2,1)S(1)}, bf16[1,2,2,2,48,896]{5,4,3,2,1,0:T(8,128)(2,1)}, u32[]{:S(2)}, u32[]{:S(2)}) collective-permute-start(bf16[1,2,2,2,48,896]{5,4,3,2,1,0:T(8,128)(2,1)S(1)} %pad_maximum_fusion.1), channel_id=1, source_target_pairs={{0,2},{1,5},{2,0},{3,7},{4,6},{5,1},{6,4},{7,3},{8,10},{9,13},{10,... | collective-permute-start | bytes 2064392 | tf_op jit(solution)/shard_map/ppermute | solution.py:37
  104.6 3.7 %collective-permute-start.15 = (f32[24,128]{1,0:T(8,128)S(1)}, f32[24,128]{1,0:T(8,128)S(1)}, u32[]{:S(2)}, u32[]{:S(2)}) collective-permute-start(f32[24,128]{1,0:T(8,128)S(1)} %add.111), channel_id=1, source_target_pairs={{0,8},{1,9},{2,10},{3,11},{4,12},{5,13},{6,14},{7,15},{8,0},{9,1},... | collective-permute-start | bytes 36872 | tf_op jit(solution)/shard_map/ppermute | solution.py:37
  108.3 4.6 %collective-permute-start.16 = (f32[24,128]{1,0:T(8,128)S(1)}, f32[24,128]{1,0:T(8,128)S(1)}, u32[]{:S(2)}, u32[]{:S(2)}) collective-permute-start(f32[24,128]{1,0:T(8,128)S(1)} %add.112), channel_id=1, source_target_pairs={{0,16},{1,17},{2,18},{3,19},{4,20},{5,21},{6,22},{7,23},{8,24},{9,... | collective-permute-start | bytes 36872 | tf_op jit(solution)/shard_map/ppermute | solution.py:37
  112.9 1.2 collective-permute-start.24
  118.6 2.0 %collective-permute-start.30 = (f32[576,128]{1,0:T(8,128)}, f32[576,128]{1,0:T(8,128)}, u32[]{:S(2)}, u32[]{:S(2)}) collective-permute-start(f32[576,128]{1,0:T(8,128)} %shard_map.89.mine_ref), channel_id=1, source_target_pairs={{0,1},{1,0},{2,3},{3,2},{4,5},{5,4},{6,7},{7,6},{8,9},{9,8},{10,11... | collective-permute-start | bytes 884744 | tf_op jit(solution)/shard_map/ppermute | solution.py:41
